TPU v7x, 32 devices: a whole 2x2x4 slice. The times are simulated.
32 devices in a mesh: grp: 4 (over y, x), blk: 8 (over z, core).
Axes of the slice: x: 2, y: 2, z: 4, core: 2. Of those that a mesh axis runs over, the one named last changes fastest.
Arguments:
- adjoint_init: float32 [5, 128, 8192], P(None, 'grp', 'blk'), may hold values from -6 to 6
- adjoint_rhs: float32 [5, 128, 8192], P(None, 'grp', 'blk'), may hold values from -24 to 24
- flow_state: float32 [5, 128, 8192], P(None, 'grp', 'blk'), may hold values from -2 to 8, as said below
- face_weights: bfloat16 [6, 128, 8192], P(None, 'grp', 'blk'), may hold values from 0.29882812 to 1.1953125
- pseudo_time: float32 [128, 8192], P('grp', 'blk'), may hold values from 1 to 4
- tet_coords: float32 [4, 3, 65536], P(None, None, ('grp', 'blk')), may hold values from -6 to 6
- tet_weights: float32 [4, 65536], P(None, ('grp', 'blk')), may hold values from 0.25 to 1
- tet_cell: int32 [65536], P(('grp', 'blk')), may hold values from 0 to 32767
- tet_vertex: int32 [4, 65536], P(None, ('grp', 'blk')), may hold values from 0 to 1535
- tet_count: int32 [32, 8], P(('grp', 'blk')), may hold values from 1 to 256, as said below
Outputs:
- adjoint_field: float32 [5, 128, 8192], P(None, 'grp', 'blk')
- sensitivity: float32 [3, 49152], P(None, ('grp', 'blk'))
Inputs may be any that keep to these rules, and one draw needn't show every extreme that they name: `flow_state`: the density is 0.5 to 2, pressure 0.4 (energy - momentum squared / (2 density)) is about 0.5 to 2, each velocity component is below 1 in magnitude. A block's slots are grouped by owner: slots o * 256 to (o + 1) * 256 - 1 of a block are for owner o of its group, and the first tet_count[block, o] of them are live. In every group one owner, drawn from the seed, gets exactly 256 live tetrahedra from every block of the group. `tet_vertex`: A corner's vertex belongs to the owner of its slot's range. `tet_cell`: cell index x 32 * 32 + y * 32 + z within the block.
All inputs are finite; a program needn't handle non-finite values.
Results may differ from a plain program's by a relative error of at most 0.0003.
Values sent between devices are 32-bit elements; how exact they have to be, the bound alone decides.
No kernel may reach another device: no remote copies, remote signals or barrier semaphores. Data moves between devices by JAX's collectives and lax.ppermute only.
A program may use at most 128 MiB of HBM per device.

v0:
```python
import jax
import jax.numpy as jnp
from jax import lax
from jax.sharding import PartitionSpec as P

SWEEPS = 2
VERT_DEV = 1536


GAMMA = 1.4


def padded(block, sides, width):
    for axis, dim in sides:
        count = lax.axis_size(axis)
        forward = [(i, i + 1) for i in range(count - 1)]
        backward = [(target, source) for source, target in forward]
        low = lax.ppermute(
            lax.slice_in_dim(block, block.shape[dim] - width, None, axis=dim), axis, forward
        )
        high = lax.ppermute(lax.slice_in_dim(block, 0, width, axis=dim), axis, backward)
        block = jnp.concatenate([low, block, high], axis=dim)
    return block


def flow_split(state):
    density = state[0]
    velocity = state[1:4] / density
    speed_sq = jnp.sum(velocity * velocity, axis=0)
    pressure = (GAMMA - 1.0) * (state[4] - 0.5 * density * speed_sq)
    return (velocity, speed_sq, pressure)


def jacobians(state):
    density = state[0]
    velocity, speed_sq, pressure = flow_split(state)
    enthalpy = (state[4] + pressure) / density
    reach = jnp.sqrt(speed_sq) + jnp.sqrt(GAMMA * pressure / density)
    half_sq = 0.5 * (GAMMA - 1.0) * speed_sq
    tables = []
    for axis_id in range(3):
        normal_vel = velocity[axis_id]
        matrix = [[1.0 if column == axis_id + 1 else 0.0 for column in range(5)]]
        for first in range(3):
            n_first = 1.0 if first == axis_id else 0.0
            line = [half_sq * n_first - velocity[first] * normal_vel]
            for second in range(3):
                n_second = 1.0 if second == axis_id else 0.0
                entry = velocity[first] * n_second - (GAMMA - 1.0) * n_first * velocity[second]
                if first == second:
                    entry = entry + normal_vel
                line.append(entry)
            line.append((GAMMA - 1.0) * n_first)
            matrix.append(line)
        energy_line = [normal_vel * (half_sq - enthalpy)]
        for second in range(3):
            n_second = 1.0 if second == axis_id else 0.0
            energy_line.append(enthalpy * n_second - (GAMMA - 1.0) * normal_vel * velocity[second])
        energy_line.append(GAMMA * normal_vel)
        matrix.append(energy_line)
        tables.append(matrix)
    return (reach, tables)


def apply_transpose(matrix, adjoint):
    result = []
    for column in range(5):
        total = matrix[0][column] * adjoint[0]
        for line in range(1, 5):
            total = total + matrix[line][column] * adjoint[line]
        result.append(total)
    return jnp.stack(result)


def relax_cells(reach, tables, faces, pseudo, rhs, neighbours):
    total = rhs
    weight = pseudo
    for direction in range(6):
        axis_id = direction // 2
        sign_value = 1.0 if direction % 2 == 0 else -1.0
        nearby = neighbours[direction]
        face = faces[direction].astype(jnp.float32)
        total = total + 0.5 * face * (
            sign_value * apply_transpose(tables[axis_id], nearby) + reach * nearby
        )
        weight = weight + 0.5 * reach * face
    return total / weight


def cross_product(left, right):
    return jnp.stack(
        [
            left[1] * right[2] - left[2] * right[1],
            left[2] * right[0] - left[0] * right[2],
            left[0] * right[1] - left[1] * right[0],
        ]
    )


def tet_terms(adj_tet, state_tet, coords, weights, live):
    velocity, speed_sq, pressure = flow_split(state_tet)
    volume_weight = pressure * adj_tet[4]
    face_weight = pressure * adj_tet[1:4]
    corner = [coords[k] for k in range(4)]
    edge_one = corner[1] - corner[0]
    edge_two = corner[2] - corner[0]
    edge_three = corner[3] - corner[0]
    grad_one = cross_product(edge_two, edge_three) / 6.0
    grad_two = cross_product(edge_three, edge_one) / 6.0
    grad_three = cross_product(edge_one, edge_two) / 6.0
    grad_zero = -(grad_one + grad_two + grad_three)
    side_one = corner[2] - corner[1]
    side_two = corner[3] - corner[1]
    face_two = 0.5 * cross_product(side_two, face_weight)
    face_three = 0.5 * cross_product(face_weight, side_one)
    face_one = -(face_two + face_three)
    terms = jnp.stack(
        [
            volume_weight * grad_zero,
            volume_weight * grad_one + face_one,
            volume_weight * grad_two + face_two,
            volume_weight * grad_three + face_three,
        ]
    )
    return terms * (weights * live)[:, None, :]


def local(
    adjoint_init,
    adjoint_rhs,
    flow_state,
    face_weights,
    pseudo_time,
    tet_coords,
    tet_weights,
    tet_cell,
    tet_vertex,
    tet_count,
):
    edge = adjoint_init.shape[1]
    span = adjoint_init.shape[2]
    owners = lax.axis_size("blk")
    tet_total = tet_cell.shape[0]
    capacity = tet_total // owners
    vertices = VERT_DEV
    column_pos = jnp.arange(span, dtype=jnp.int32) % edge
    keep_upper = (column_pos != edge - 1).astype(jnp.float32)
    keep_lower = (column_pos != 0).astype(jnp.float32)
    zero_single = jnp.zeros((5, edge, 1), jnp.float32)
    reach, tables = jacobians(flow_state)
    adjoint = adjoint_init
    for sweep_index in range(SWEEPS):
        along_x = padded(adjoint, (("grp", 1),), 1)
        along_y = padded(adjoint, (("blk", 2),), edge)
        neighbours = [
            along_x[:, 2:],
            along_x[:, :-2],
            along_y[:, :, 2 * edge :],
            along_y[:, :, : -2 * edge],
            jnp.concatenate([adjoint[:, :, 1:], zero_single], 2) * keep_upper,
            jnp.concatenate([zero_single, adjoint[:, :, :-1]], 2) * keep_lower,
        ]
        adjoint = relax_cells(reach, tables, face_weights, pseudo_time, adjoint_rhs, neighbours)
    slot = jnp.arange(tet_total, dtype=jnp.int32)
    owner_slot = slot // capacity
    slot_counts = jnp.broadcast_to(tet_count[0][:, None], (owners, capacity)).reshape(-1)
    live = (slot % capacity < slot_counts).astype(jnp.float32)
    adj_tet = jnp.take(adjoint.reshape(5, -1), tet_cell, axis=1)
    state_tet = jnp.take(flow_state.reshape(5, -1), tet_cell, axis=1)
    terms = tet_terms(adj_tet, state_tet, tet_coords, tet_weights, live)
    target = (owner_slot[None, :] * vertices + tet_vertex).reshape(-1)
    data = jnp.transpose(terms, (1, 0, 2)).reshape(3, -1)
    inside = (target >= 0) & (target < 1 * lax.axis_size("blk") * vertices)
    clipped = jnp.where(inside, target, 0)
    masked = jnp.where(inside[None, :], data, 0.0)
    summed = jax.vmap(
        lambda values: jax.ops.segment_sum(
            values, clipped, num_segments=1 * lax.axis_size("blk") * vertices
        )
    )(masked)
    sums = lax.psum_scatter(
        jnp.transpose(summed.reshape(3, 1 * lax.axis_size("blk"), vertices), (1, 0, 2)),
        "blk",
        scatter_dimension=0,
        tiled=True,
    )[0]
    return (adjoint, sums)


def solution(mesh):
    return jax.shard_map(
        local,
        mesh=mesh,
        in_specs=(
            P(None, "grp", "blk"),
            P(None, "grp", "blk"),
            P(None, "grp", "blk"),
            P(None, "grp", "blk"),
            P("grp", "blk"),
            P(None, None, ("grp", "blk")),
            P(None, ("grp", "blk")),
            P(("grp", "blk")),
            P(None, ("grp", "blk")),
            P(("grp", "blk"), None),
        ),
        out_specs=(P(None, "grp", "blk"), P(None, ("grp", "blk"))),
        check_vma=False,
    )
```

profile of v0, /device:TPU:5, one launch (start us, length us, event | category | flops | bytes accessed | tf_op | source)
XLA Modules:
  0.0 243.0 jit_solution(11431342531331995407)
XLA Ops:
  7.3 1.7 fusion.163
  9.0 3.1 %collective-permute-start.1 = (f32[5,1,1024]{2,1,0:T(1,128)S(1)}, f32[5,1,1024]{2,1,0:T(1,128)S(1)}, u32[]{:S(2)}, u32[]{:S(2)}) collective-permute-start(f32[5,1,1024]{2,1,0:T(1,128)S(1)} %get-tuple-element.94), channel_id=1, source_target_pairs={{0,8},{8,16},{16,24},{1,9},{9,17},{17,25},{2,10},{10,18},{18,26},{... | collective-permute-start | bytes 61448 | tf_op jit(solution)/shard_map/ppermute | solution.py:18
  12.1 1.7 fusion.164
  13.8 4.0 %collective-permute-start.3 = (f32[5,32,32]{2,1,0:T(8,128)}, f32[5,32,32]{2,1,0:T(8,128)}, u32[]{:S(2)}, u32[]{:S(2)}) collective-permute-start(f32[5,32,32]{2,1,0:T(8,128)} %get-tuple-element.98), channel_id=1, source_target_pairs={{0,1},{1,2},{2,3},{3,4},{4,5},{5,6},{6,7},{8,9},{9,10},{10,11},{11... | collective-permute-start | bytes 61448 | tf_op jit(solution)/shard_map/ppermute | solution.py:18
  17.8 1.9 collective-permute-start.2
  19.7 3.1 %collective-permute-start = (f32[5,1,1024]{2,1,0:T(1,128)}, f32[5,1,1024]{2,1,0:T(1,128)}, u32[]{:S(2)}, u32[]{:S(2)}) collective-permute-start(f32[5,1,1024]{2,1,0:T(1,128)} %get-tuple-element.93), channel_id=1, source_target_pairs={{8,0},{16,8},{24,16},{9,1},{17,9},{25,17},{10,2},{18,10},{26,18},{... | collective-permute-start | bytes 61448 | tf_op jit(solution)/shard_map/ppermute | solution.py:21
  22.8 1.5 fusion.162
  25.1 1.3 compare_and_fusion
  26.4 1.2 fusion.165
  33.8 2.0 fusion.41
  37.7 1.8 fusion.48
  40.3 9.9 %copy.78 = f32[5,32,1024]{0,2,1:T(8,128)} copy(f32[5,32,1024]{2,1,0:T(8,128)} %param.14) | data formatting | bytes 1310720 | tf_op args[2]
  50.2 13.4 %gather_fusion = f32[2048,5]{1,0:T(8,128)} fusion(f32[5,32768]{0,1:T(8,128)} %bitcast.207, s32[2048]{0:T(1024)S(1)} %fusion.117), kind=kCustom, calls=%fused_computation.clone | custom fusion | bytes 90112 | tf_op jit(solution)/shard_map/jit(_take)/gather | solution.py:169
  63.6 2.2 copy.79
  66.4 2.1 add_dynamic-update-slice_fusion.54
  69.5 2.1 add_dynamic-update-slice_fusion.44
  71.6 2.4 add_dynamic-update-slice_fusion.39
  74.9 1.6 add_dynamic-update-slice_fusion.34
  76.6 2.4 %add_dynamic-update-slice_fusion.38 = (f32[5,32,1024]{2,1,0:T(8,128)}, f32[1,32,1024]{2,1,0:T(8,128)S(1)}, f32[1,32,1024]{2,1,0:T(8,128)S(1)}, f32[1,32,1024]{2,...) fusion(f32[5,32,1024]{2,1,0:T(8,128)} %get-tuple-element.79, ...), kind=kLoop, calls=%fused_computation.228 | loop fusion | flops 1179648 | bytes 3145728
  79.0 2.1 add_dynamic-update-slice_fusion.37
  86.4 2.2 fusion.27
  89.1 1.9 collective-permute-start.6
  91.0 3.9 %collective-permute-start.7 = (f32[5,32,32]{2,1,0:T(8,128)S(1)}, f32[5,32,32]{2,1,0:T(8,128)S(1)}, u32[]{:S(2)}, u32[]{:S(2)}) collective-permute-start(f32[5,32,32]{2,1,0:T(8,128)S(1)} %get-tuple-element.90), channel_id=1, source_target_pairs={{0,1},{1,2},{2,3},{3,4},{4,5},{5,6},{6,7},{8,9},{9,10},{10,11},{11... | collective-permute-start | bytes 61448 | tf_op jit(solution)/shard_map/ppermute | solution.py:18
  94.9 2.2 collective-permute-start.4
  97.1 3.3 %collective-permute-start.5 = (f32[5,1,1024]{2,1,0:T(1,128)S(1)}, f32[5,1,1024]{2,1,0:T(1,128)S(1)}, u32[]{:S(2)}, u32[]{:S(2)}) collective-permute-start(f32[5,1,1024]{2,1,0:T(1,128)S(1)} %get-tuple-element.88), channel_id=1, source_target_pairs={{0,8},{8,16},{16,24},{1,9},{9,17},{17,25},{2,10},{10,18},{18,26},{... | collective-permute-start | bytes 61448 | tf_op jit(solution)/shard_map/ppermute | solution.py:18
  104.8 8.8 %copy.80 = f32[5,32,1024]{0,2,1:T(8,128)} copy(f32[5,32,1024]{2,1,0:T(8,128)S(1)} %fusion.8) | data formatting | bytes 1310720 | tf_op jit(solution)/shard_map/div | solution.py:87
  113.6 11.2 %gather_fusion.1 = f32[2048,5]{1,0:T(8,128)S(1)} fusion(f32[5,32768]{0,1:T(8,128)} %bitcast.206, s32[2048]{0:T(1024)S(1)} %fusion.117), kind=kCustom, calls=%fused_computation.1.clone | custom fusion | bytes 90112 | tf_op jit(solution)/shard_map/jit(_take)/gather | solution.py:168
  125.9 2.7 %copy.86 = f32[8192,3]{1,0:T(8,128)} copy(f32[8192,3]{0,1:T(4,128)S(1)} %select_bitcast_fusion) | data formatting | bytes 196608 | tf_op jit(solution)/shard_map/jit(_where)/select_n | solution.py:175
  128.6 47.2 %scatter_custom_fusion = f32[3,12288]{0,1:T(8,128)} fusion(s32[8192]{0:T(1024)} %bitcast.214, f32[8192,3]{1,0:T(8,128)} %copy.86, f32[]{:T(128)} %constant.73.clone.1), kind=kCustom, calls=%fused_computation.3 | custom fusion | flops 24576 | bytes 147968 | tf_op jit(solution)/shard_map/vmap()/scatter-add | solution.py:177
  175.8 5.1 %copy.87 = f32[3,8,1536]{2,0,1:T(4,128)} copy(f32[3,8,1536]{0,2,1:T(8,128)} %bitcast.205) | data formatting | bytes 294912 | tf_op jit(solution)/shard_map/reshape | solution.py:182
  181.5 52.7 %all-reduce.7.cloned.1.call-done = f32[8,3,1536]{2,1,0:T(4,128)} async-done(((f32[8,3,1536]{2,1,0:T(4,128)}), f32[8,3,1536]{2,1,0:T(4,128)}) %all-reduce.7.cloned.1.call-update) | async-done | bytes 147472
  234.2 1.9 dynamic-slice_bitcast_fusion
  (219 shorter events, 23.0 us)
Async XLA Ops:
  7.2 28.6 %copy-start = (s32[1,8]{1,0:T(1,128)S(1)}, s32[1,8]{1,0:T(1,128)}, u32[]{:S(2)}) copy-start(s32[1,8]{1,0:T(1,128)} %param.21) | copy-start | bytes 100
  7.2 33.0 %copy-start.2 = (f32[5,32,1024]{2,1,0:T(8,128)S(1)}, f32[5,32,1024]{2,1,0:T(8,128)}, u32[]{:S(2)}) copy-start(f32[5,32,1024]{2,1,0:T(8,128)} %param.12) | copy-start | bytes 1966084
  7.2 30.5 %copy-start.31 = (bf16[6,32,1024]{2,1,0:T(8,128)(2,1)S(1)}, bf16[6,32,1024]{2,1,0:T(8,128)(2,1)}, u32[]{:S(2)}) copy-start(bf16[6,32,1024]{2,1,0:T(8,128)(2,1)} %param.15) | copy-start | bytes 1179652
  7.2 30.5 %copy-start.48 = (f32[32,1024]{1,0:T(8,128)S(1)}, f32[32,1024]{1,0:T(8,128)}, u32[]{:S(2)}) copy-start(f32[32,1024]{1,0:T(8,128)} %param.16) | copy-start | bytes 393220
  7.2 32.4 %copy-start.65 = (f32[4,2048]{1,0:T(4,128)S(1)}, f32[4,2048]{1,0:T(4,128)}, u32[]{:S(2)}) copy-start(f32[4,2048]{1,0:T(4,128)} %param.18) | copy-start | bytes 98308
  7.2 227.0 %all-reduce.7.cloned.1.call-start = ((), (), s32[]{:S(2)}) async-start(), calls=%async_computation | async-start | bytes 393216
  9.0 57.4 %collective-permute-start.1 = (f32[5,1,1024]{2,1,0:T(1,128)S(1)}, f32[5,1,1024]{2,1,0:T(1,128)S(1)}, u32[]{:S(2)}, u32[]{:S(2)}) collective-permute-start(f32[5,1,1024]{2,1,0:T(1,128)S(1)} %get-tuple-element.94), channel_id=1, source_target_pairs={{0,8},{8,16},{16,24},{1,9},{9,17},{17,25},{2,10},{10,18},{18,26},{... | collective-permute-start | bytes 61448 | tf_op jit(solution)/shard_map/ppermute | solution.py:18
  13.8 55.7 %collective-permute-start.3 = (f32[5,32,32]{2,1,0:T(8,128)}, f32[5,32,32]{2,1,0:T(8,128)}, u32[]{:S(2)}, u32[]{:S(2)}) collective-permute-start(f32[5,32,32]{2,1,0:T(8,128)} %get-tuple-element.98), channel_id=1, source_target_pairs={{0,1},{1,2},{2,3},{3,4},{4,5},{5,6},{6,7},{8,9},{9,10},{10,11},{11... | collective-permute-start | bytes 61448 | tf_op jit(solution)/shard_map/ppermute | solution.py:18
  17.8 50.7 %collective-permute-start.2 = (f32[5,32,32]{2,1,0:T(8,128)}, f32[5,32,32]{2,1,0:T(8,128)}, u32[]{:S(2)}, u32[]{:S(2)}) collective-permute-start(f32[5,32,32]{2,1,0:T(8,128)} %get-tuple-element.97), channel_id=1, source_target_pairs={{1,0},{2,1},{3,2},{4,3},{5,4},{6,5},{7,6},{9,8},{10,9},{11,10},{12... | collective-permute-start | bytes 61448 | tf_op jit(solution)/shard_map/ppermute | solution.py:21
  19.7 54.2 %collective-permute-start = (f32[5,1,1024]{2,1,0:T(1,128)}, f32[5,1,1024]{2,1,0:T(1,128)}, u32[]{:S(2)}, u32[]{:S(2)}) collective-permute-start(f32[5,1,1024]{2,1,0:T(1,128)} %get-tuple-element.93), channel_id=1, source_target_pairs={{8,0},{16,8},{24,16},{9,1},{17,9},{25,17},{10,2},{18,10},{26,18},{... | collective-permute-start | bytes 61448 | tf_op jit(solution)/shard_map/ppermute | solution.py:21
  24.4 25.8 %copy-start.59 = (f32[1024]{0:T(1024)}, f32[1024]{0:T(1024)S(1)}, u32[]{:S(2)}) copy-start(f32[1024]{0:T(1024)S(1)} %fusion.123) | copy-start | bytes 12292
  89.1 12.3 %collective-permute-start.6 = (f32[5,32,32]{2,1,0:T(8,128)S(1)}, f32[5,32,32]{2,1,0:T(8,128)S(1)}, u32[]{:S(2)}, u32[]{:S(2)}) collective-permute-start(f32[5,32,32]{2,1,0:T(8,128)S(1)} %get-tuple-element.89), channel_id=1, source_target_pairs={{1,0},{2,1},{3,2},{4,3},{5,4},{6,5},{7,6},{9,8},{10,9},{11,10},{12... | collective-permute-start | bytes 61448 | tf_op jit(solution)/shard_map/ppermute | solution.py:21
  91.0 10.7 %collective-permute-start.7 = (f32[5,32,32]{2,1,0:T(8,128)S(1)}, f32[5,32,32]{2,1,0:T(8,128)S(1)}, u32[]{:S(2)}, u32[]{:S(2)}) collective-permute-start(f32[5,32,32]{2,1,0:T(8,128)S(1)} %get-tuple-element.90), channel_id=1, source_target_pairs={{0,1},{1,2},{2,3},{3,4},{4,5},{5,6},{6,7},{8,9},{9,10},{10,11},{11... | collective-permute-start | bytes 61448 | tf_op jit(solution)/shard_map/ppermute | solution.py:18
  94.9 7.5 %collective-permute-start.4 = (f32[5,1,1024]{2,1,0:T(1,128)S(1)}, f32[5,1,1024]{2,1,0:T(1,128)S(1)}, u32[]{:S(2)}, u32[]{:S(2)}) collective-permute-start(f32[5,1,1024]{2,1,0:T(1,128)S(1)} %get-tuple-element.87), channel_id=1, source_target_pairs={{8,0},{16,8},{24,16},{9,1},{17,9},{25,17},{10,2},{18,10},{26,18},{... | collective-permute-start | bytes 61448 | tf_op jit(solution)/shard_map/ppermute | solution.py:21
  97.1 5.6 %collective-permute-start.5 = (f32[5,1,1024]{2,1,0:T(1,128)S(1)}, f32[5,1,1024]{2,1,0:T(1,128)S(1)}, u32[]{:S(2)}, u32[]{:S(2)}) collective-permute-start(f32[5,1,1024]{2,1,0:T(1,128)S(1)} %get-tuple-element.88), channel_id=1, source_target_pairs={{0,8},{8,16},{16,24},{1,9},{9,17},{17,25},{2,10},{10,18},{18,26},{... | collective-permute-start | bytes 61448 | tf_op jit(solution)/shard_map/ppermute | solution.py:18
  104.7 20.5 %copy-start.46 = (f32[2048,5]{0,1:T(8,128)S(1)}, f32[2048,5]{0,1:T(8,128)}, u32[]{:S(2)}) copy-start(f32[2048,5]{0,1:T(8,128)} %copy.79) | copy-start | bytes 122884
  104.7 20.5 %copy-start.66 = (pred[2048]{0:T(1024)(128)(4,1)S(1)}, pred[2048]{0:T(1024)(128)(4,1)}, u32[]{:S(2)}) copy-start(pred[2048]{0:T(1024)(128)(4,1)} %compare_and_fusion) | copy-start | bytes 6148
  104.7 20.6 %copy-start.50 = (f32[1,3,2048]{2,1,0:T(4,128)S(1)}, f32[1,3,2048]{2,1,0:T(4,128)}, u32[]{:S(2)}) copy-start(f32[1,3,2048]{2,1,0:T(4,128)} %get-tuple-element.179) | copy-start | bytes 73732
  104.7 20.7 %copy-start.49 = (f32[1,3,2048]{2,1,0:T(4,128)S(1)}, f32[1,3,2048]{2,1,0:T(4,128)}, u32[]{:S(2)}) copy-start(f32[1,3,2048]{2,1,0:T(4,128)} %get-tuple-element.183) | copy-start | bytes 73732
  104.7 20.7 %copy-start.51 = (f32[1,1,2048]{2,1,0:T(1,128)S(1)}, f32[1,1,2048]{2,1,0:T(1,128)}, u32[]{:S(2)}) copy-start(f32[1,1,2048]{2,1,0:T(1,128)} %get-tuple-element.160) | copy-start | bytes 24580
  104.7 20.7 %copy-start.52 = (f32[1,1,2048]{2,1,0:T(1,128)S(1)}, f32[1,1,2048]{2,1,0:T(1,128)}, u32[]{:S(2)}) copy-start(f32[1,1,2048]{2,1,0:T(1,128)} %get-tuple-element.161) | copy-start | bytes 24580
  104.7 20.7 %copy-start.53 = (f32[1,1,2048]{2,1,0:T(1,128)S(1)}, f32[1,1,2048]{2,1,0:T(1,128)}, u32[]{:S(2)}) copy-start(f32[1,1,2048]{2,1,0:T(1,128)} %get-tuple-element.162) | copy-start | bytes 24580
  104.8 20.7 %copy-start.54 = (f32[1,1,2048]{2,1,0:T(1,128)S(1)}, f32[1,1,2048]{2,1,0:T(1,128)}, u32[]{:S(2)}) copy-start(f32[1,1,2048]{2,1,0:T(1,128)} %get-tuple-element.166) | copy-start | bytes 24580
  104.8 20.7 %copy-start.55 = (f32[1,1,2048]{2,1,0:T(1,128)S(1)}, f32[1,1,2048]{2,1,0:T(1,128)}, u32[]{:S(2)}) copy-start(f32[1,1,2048]{2,1,0:T(1,128)} %get-tuple-element.167) | copy-start | bytes 24580
  104.8 20.7 %copy-start.56 = (f32[1,1,2048]{2,1,0:T(1,128)S(1)}, f32[1,1,2048]{2,1,0:T(1,128)}, u32[]{:S(2)}) copy-start(f32[1,1,2048]{2,1,0:T(1,128)} %get-tuple-element.168) | copy-start | bytes 24580
  104.8 20.8 %copy-start.61 = (f32[1,1,2048]{2,1,0:T(1,128)S(1)}, f32[1,1,2048]{2,1,0:T(1,128)}, u32[]{:S(2)}) copy-start(f32[1,1,2048]{2,1,0:T(1,128)} %get-tuple-element.172) | copy-start | bytes 24580
  104.8 20.8 %copy-start.62 = (f32[1,1,2048]{2,1,0:T(1,128)S(1)}, f32[1,1,2048]{2,1,0:T(1,128)}, u32[]{:S(2)}) copy-start(f32[1,1,2048]{2,1,0:T(1,128)} %get-tuple-element.173) | copy-start | bytes 24580
  104.8 20.8 %copy-start.63 = (f32[1,1,2048]{2,1,0:T(1,128)S(1)}, f32[1,1,2048]{2,1,0:T(1,128)}, u32[]{:S(2)}) copy-start(f32[1,1,2048]{2,1,0:T(1,128)} %get-tuple-element.174) | copy-start | bytes 24580
  104.8 21.0 %copy-start.47 = (f32[4,2048]{1,0:T(4,128)S(1)}, f32[4,2048]{1,0:T(4,128)}, u32[]{:S(2)}) copy-start(f32[4,2048]{1,0:T(4,128)} %broadcast_multiply_fusion.3) | copy-start | bytes 98308
  104.8 21.0 %copy-start.64 = (pred[1,16,4,128]{3,1,2,0:T(8,128)(4,1)S(1)}, pred[1,16,4,128]{3,1,2,0:T(8,128)(4,1)}, u32[]{:S(2)}) copy-start(pred[1,16,4,128]{3,1,2,0:T(8,128)(4,1)} %copy.93) | copy-start | bytes 24580
  128.6 107.6 %copy-start.1 = (s32[1,8]{1,0:T(1,128)S(1)}, s32[1,8]{1,0:T(1,128)}, u32[]{:S(2)}) copy-start(s32[1,8]{1,0:T(1,128)} %param.21) | copy-start | bytes 100
  128.6 52.4 %copy-start.67 = (u32[32]{0:T(128)S(1)}, u32[32]{0:T(128)}, u32[]{:S(2)}) copy-start(u32[32]{0:T(128)} %constant.101) | copy-start | bytes 388
  (45 other events, 285.7 us)
Sparse Core Ops, SparseCore 0:
  181.1 53.1 all-reduce.6
where the time goes:
time: 248 us; the launch traced here: 243 us
  other arithmetic  85 us (34%)
  local copies, waits for them, and re-layouts  66.5 us (27%)
  waiting for transfers between devices  52.7 us (21%)
  starting transfers between devices  23.5 us (9%)
  between operations  15.4 us (6%)
    unnamed x2, waiting for transfers between devices  52.7 us
    scatter-add x1, other arithmetic, local(): jax.ops.segment_sum(values, clipped, num_segments=1 * lax.axis_size('blk'...  47.2 us
    unnamed x32, other arithmetic  20.1 us
    gather x2, local copies, waits for them, and re-layouts, local(): state_tet = jnp.take(flow_state.reshape(5, -1), tet_cell, axis=1)  15.6 us
    ppermute x4, starting transfers between devices, padded(): lax.ppermute(lax.slice_in_dim(block, block.shape[dim] - width, None, axis...  14.4 us
    unnamed x143, local copies, waits for them, and re-layouts  11.7 us
    gather x2, local copies, waits for them, and re-layouts, local(): adj_tet = jnp.take(adjoint.reshape(5, -1), tet_cell, axis=1)  11.6 us
    ppermute x4, starting transfers between devices, padded(): lax.ppermute(lax.slice_in_dim(block, 0, width, axis=dim), axis, backward)  9.07 us
  transfers between devices with their start and end apart: 9, of which 1 were waited for; matrix products, arithmetic and copies ran while one was open for 23% of the time, Pallas kernels for 0%

commit v1 on v0

v1 whole, which is shorter than its diff:
```python
import functools
import jax
import jax.numpy as jnp
from jax import lax
from jax.experimental import pallas as pl
from jax.experimental.pallas import tpu as pltpu
from jax.sharding import PartitionSpec as P

VERT_DEV = 1536
GAMMA = 1.4
LANES = 128
ROWS = 8
PARTS = VERT_DEV // LANES
F32 = jnp.float32
BF16 = jnp.bfloat16
VMEM = pl.BlockSpec(memory_space=pltpu.VMEM)
SMEM = pl.BlockSpec(memory_space=pltpu.SMEM)
HBM = pl.BlockSpec(memory_space=pl.ANY)
LIMIT = 40 * 1024 * 1024


def call(kernel, outs, in_specs, out_specs, scratch, name, cost=None):
    return pl.pallas_call(
        kernel,
        out_shape=outs,
        in_specs=in_specs,
        out_specs=out_specs,
        scratch_shapes=scratch,
        compiler_params=pltpu.CompilerParams(vmem_limit_bytes=LIMIT),
        cost_estimate=cost,
        name=name,
    )


def is_even(axis):
    return lax.rem(lax.axis_index(axis), 2) == 0


def reach_of(speed_sq, enthalpy):
    sound_sq = (GAMMA - 1.0) * (enthalpy - 0.5 * speed_sq)
    return jnp.sqrt(speed_sq) + jnp.sqrt(sound_sq)


def transposed(vel, enthalpy, half_sq, axis_id, field):
    normal = vel[axis_id]
    energy = normal * field[4]
    common = vel[0] * field[1] + vel[1] * field[2] + vel[2] * field[3] + enthalpy * field[4]
    along = field[1 + axis_id] + energy
    scaled = (GAMMA - 1.0) * along
    out = [half_sq * along - normal * common]
    for j in range(3):
        entry = normal * field[1 + j] - vel[j] * scaled
        if j == axis_id:
            entry = entry + (field[0] + common)
        out.append(entry)
    out.append(scaled + energy)
    return out


def one_sided(vel, enthalpy, axis_id, sign, field):
    speed_sq = vel[0] * vel[0] + vel[1] * vel[1] + vel[2] * vel[2]
    reach = reach_of(speed_sq, enthalpy)
    turned = transposed(vel, enthalpy, 0.5 * (GAMMA - 1.0) * speed_sq, axis_id, field)
    return [sign * turned[k] + reach * field[k] for k in range(5)]


def cell_state(state):
    density, m1, m2, m3, energy = state
    inverse = 1.0 / density
    vel = [m1 * inverse, m2 * inverse, m3 * inverse]
    speed_sq = vel[0] * vel[0] + vel[1] * vel[1] + vel[2] * vel[2]
    pressure = (GAMMA - 1.0) * (energy - 0.5 * density * speed_sq)
    enthalpy = (energy + pressure) * inverse
    reach = jnp.sqrt(speed_sq) + jnp.sqrt(GAMMA * pressure * inverse)
    return vel, speed_sq, pressure, enthalpy, reach


def sweep_tile(grid, row, lane, edge, vel, speed_sq, enthalpy, reach, faces, rhs):
    def at(k, drow, dlane):
        return grid[k, pl.ds(row + drow, ROWS), pl.ds(lane + dlane, LANES)]

    place = lax.broadcasted_iota(jnp.int32, (ROWS, LANES), 1)
    depth = lax.rem(place, edge)
    first = place < edge
    last = place >= LANES - edge
    zero = jnp.zeros((ROWS, LANES), F32)
    faces = list(faces)
    faces[4] = jnp.where(depth == edge - 1, zero, faces[4])
    faces[5] = jnp.where(depth == 0, zero, faces[5])
    here = [at(k, 0, 0) for k in range(5)]
    spread = None
    total = None
    for axis_id in range(3):
        if axis_id == 0:
            upper = [at(k, 1, 0) for k in range(5)]
            lower = [at(k, -1, 0) for k in range(5)]
        elif axis_id == 1:
            upper = [
                pltpu.roll(jnp.where(first, at(k, 0, LANES), here[k]), LANES - edge, 1) for k in range(5)
            ]
            lower = [pltpu.roll(jnp.where(last, at(k, 0, -LANES), here[k]), edge, 1) for k in range(5)]
        else:
            upper = [pltpu.roll(here[k], LANES - 1, 1) for k in range(5)]
            lower = [pltpu.roll(here[k], 1, 1) for k in range(5)]
        upper = [faces[2 * axis_id] * v for v in upper]
        lower = [faces[2 * axis_id + 1] * v for v in lower]
        both = [u + v for u, v in zip(upper, lower)]
        difference = [u - v for u, v in zip(upper, lower)]
        spread = both if spread is None else [u + v for u, v in zip(spread, both)]
        turned = transposed(vel, enthalpy, 0.5 * (GAMMA - 1.0) * speed_sq, axis_id, difference)
        total = turned if total is None else [u + v for u, v in zip(total, turned)]
    return [rhs[k] + total[k] + reach * spread[k] for k in range(5)]


def tile_coefficients(i_half, rows, lanes, state_ref, face_tiles, pseudo_ref, rhs_ref):
    state = [state_ref[k, rows, lanes] for k in range(5)]
    vel, speed_sq, pressure, enthalpy, reach = cell_state(state)
    faces = [f[i_half * ROWS : (i_half + 1) * ROWS] for f in face_tiles]
    area = faces[0]
    for f in faces[1:]:
        area = area + f
    inverse = 1.0 / (pseudo_ref[rows, lanes] + 0.5 * reach * area)
    half = 0.5 * inverse
    faces = [half * f for f in faces]
    rhs = [rhs_ref[k, rows, lanes] * inverse for k in range(5)]
    return vel, speed_sq, pressure, enthalpy, reach, faces, rhs


def clear_pads(grid, edge, span):
    high = grid.shape[1]
    wide = grid.shape[2]
    for k in range(5):
        grid[k, 0:ROWS, :] = jnp.zeros((ROWS, wide), F32)
        grid[k, ROWS + edge : high, :] = jnp.zeros((high - ROWS - edge, wide), F32)
        grid[k, ROWS : ROWS + edge, 0:LANES] = jnp.zeros((edge, LANES), F32)
        grid[k, ROWS : ROWS + edge, LANES + span : wide] = jnp.zeros((edge, LANES), F32)


def for_each_tile(edge, span, body):
    for top in range(0, edge, 2 * ROWS):

        def step(j, carry, top=top):
            body(top, pl.multiple_of(j * LANES, LANES))
            return carry

        lax.fori_loop(0, span // LANES, step, 0)


def first_kernel(
    adjoint_ref, rhs_ref, state_ref, face_ref, pseudo_ref,
    part_ref, xa_ref, xb_ref, ylo_ref, yhi_ref,
    grid, coef, xsides, sem,
):
    edge, span = pseudo_ref.shape
    copy = pltpu.make_async_copy(
        adjoint_ref, grid.at[:, pl.ds(ROWS, edge), pl.ds(LANES, span)], sem
    )
    copy.start()
    clear_pads(grid, edge, span)
    copy.wait()

    def body(top, offset):
        lanes = pl.ds(offset, LANES)
        face_tiles = [face_ref[d, pl.ds(top, 2 * ROWS), lanes].astype(F32) for d in range(6)]
        for i_half in range(2):
            rows = pl.ds(top + i_half * ROWS, ROWS)
            vel, speed_sq, pressure, enthalpy, reach, faces, rhs = tile_coefficients(
                i_half, rows, lanes, state_ref, face_tiles, pseudo_ref, rhs_ref
            )
            out = sweep_tile(
                grid, ROWS + top + i_half * ROWS, pl.multiple_of(LANES + offset, LANES), edge,
                vel, speed_sq, enthalpy, reach, faces, rhs,
            )
            for k in range(5):
                part_ref[k, rows, lanes] = out[k]
            for k, value in enumerate(vel + [enthalpy] + faces[:4]):
                coef[k, rows, lanes] = value

    for_each_tile(edge, span, body)

    even = is_even("grp")
    place = lax.broadcasted_iota(jnp.int32, (1, span), 1)
    for side, row in ((0, 0), (1, edge - 1)):
        slot = jnp.where(even, 1 - side, side)
        at = slice(row, row + 1)
        message = [part_ref[k, at, :] for k in range(5)]
        message += [grid[k, ROWS + row : ROWS + row + 1, LANES : LANES + span] for k in range(5)]
        message += [coef[4 + 1 - side, at, :]]
        message += [coef[k, at, :] for k in range(4)]
        message += [jnp.where(place < edge, coef[7, at, :], coef[6, at, :])]
        for k, value in enumerate(message):
            xsides[slot, k : k + 1, :] = value
    xa_ref[...] = xsides[0]
    xb_ref[...] = xsides[1]

    lane = lax.broadcasted_iota(jnp.int32, (edge, LANES), 1)
    quarter = lane // edge
    for side, base, ref in ((0, 0, ylo_ref), (1, span - LANES, yhi_ref)):
        lanes = slice(base, base + LANES)
        fields = [part_ref[k, :, lanes] for k in range(5)]
        fields += [grid[k, ROWS : ROWS + edge, LANES + base : LANES + base + LANES] for k in range(5)]
        fields += [coef[6 + 1 - side, :, lanes]]
        fields += [coef[k, :, lanes] for k in range(4)]
        start = 0 if side == 0 else LANES - edge
        per = LANES // edge
        for g in range(4):
            packed = None
            for q in range(per):
                k = g * per + q
                if k >= len(fields):
                    value = jnp.zeros((edge, LANES), F32)
                else:
                    shift = (q * edge - start) % LANES
                    value = pltpu.roll(fields[k], shift, 1) if shift else fields[k]
                packed = value if packed is None else jnp.where(quarter == q, value, packed)
            ref[g] = packed


def meet(axis_id, side, own, other):
    sign = 1.0 if side == 1 else -1.0
    mine = one_sided(own[11:14], own[14], axis_id, sign, other[5:10])
    theirs = one_sided(other[11:14], other[14], axis_id, -sign, own[5:10])
    added = [own[10] * v for v in mine]
    finished = [other[k] + other[10] * theirs[k] for k in range(5)]
    return added, finished


def second_kernel(xa_ref, xb_ref, ra_ref, rb_ref, ylo_ref, yhi_ref, res_ref, ya_ref, yb_ref, ysides):
    span = xa_ref.shape[1]
    edge = ylo_ref.shape[1]
    per = LANES // edge
    even = is_even("grp")
    even_y = is_even("blk")
    ysides[0] = ylo_ref[...]
    ysides[1] = yhi_ref[...]
    lane = lax.broadcasted_iota(jnp.int32, (1, LANES), 1)
    quarter = lane // edge

    def pick(a_ref, b_ref, flag):
        return [jnp.where(flag, a_ref[k : k + 1, :], b_ref[k : k + 1, :]) for k in range(15)]

    for side in (0, 1):
        flag = even if side == 1 else jnp.logical_not(even)
        own = pick(xa_ref, xb_ref, flag)
        other = pick(ra_ref, rb_ref, flag)
        added, finished = meet(0, side, own, other)
        row = 0 if side == 0 else edge - 1
        for k in range(5):
            res_ref[side, k : k + 1, :] = added[k]
            res_ref[side, 5 + k : 6 + k, :] = finished[k]
        for ys, base, start in ((0, 0, 0), (1, span - LANES, LANES - edge)):
            for k in range(5):
                g, q = divmod(k, per)
                shift = (q * edge - start) % LANES
                piece = added[k][:, base : base + LANES]
                piece = pltpu.roll(piece, shift, 1) if shift else piece
                old = ysides[ys, g, row : row + 1, :]
                ysides[ys, g, row : row + 1, :] = old + jnp.where(quarter == q, piece, 0.0)
                g, q = divmod(15, per)
                shift = (q * edge - start) % LANES
                piece = other[5 + k][:, base : base + LANES]
                piece = pltpu.roll(piece, shift, 1) if shift else piece
                at = 2 * k + side
                old = ysides[ys, g, at : at + 1, :]
                ysides[ys, g, at : at + 1, :] = jnp.where(quarter == q, piece, old)
    ya_ref[...] = ysides[jnp.where(even_y, 1, 0)]
    yb_ref[...] = ysides[jnp.where(even_y, 0, 1)]


def cross(left, right):
    return [
        left[1] * right[2] - left[2] * right[1],
        left[2] * right[0] - left[0] * right[2],
        left[0] * right[1] - left[1] * right[0],
    ]


def minus(left, right):
    return [u - v for u, v in zip(left, right)]


def tet_terms(volume, face, corner, weights):
    edge_one = minus(corner[1], corner[0])
    edge_two = minus(corner[2], corner[0])
    edge_three = minus(corner[3], corner[0])
    sixth = volume * (1.0 / 6.0)
    g1 = [sixth * v for v in cross(edge_two, edge_three)]
    g2 = [sixth * v for v in cross(edge_three, edge_one)]
    g3 = [sixth * v for v in cross(edge_one, edge_two)]
    side_one = minus(corner[2], corner[1])
    side_two = minus(corner[3], corner[1])
    half = [0.5 * v for v in face]
    h2 = cross(side_two, half)
    h3 = cross(half, side_one)
    terms = [[], [], [], []]
    for k in range(3):
        terms[0].append(-weights[0] * (g1[k] + g2[k] + g3[k]))
        terms[1].append(weights[1] * (g1[k] - (h2[k] + h3[k])))
        terms[2].append(weights[2] * (g2[k] + h2[k]))
        terms[3].append(weights[3] * (g3[k] + h3[k]))
    return terms


def split(value):
    high = value.astype(BF16)
    return high, (value - high.astype(F32)).astype(BF16)


def hot(shape, index):
    rows = lax.broadcasted_iota(jnp.int32, shape, 0)
    return jnp.where(rows == index, 1.0, 0.0).astype(BF16)


def third_kernel(
    part_ref, rhs_ref, state_ref, face_ref, pseudo_ref, res_ref, ra_ref, rb_ref, ya_ref, yb_ref, sa_ref, sb_ref,
    coord_ref, weight_ref, cell_ref, vertex_ref, count_ref,
    out_ref, keep_ref, send_ref,
    grid, field, high, low, sums, sem,
):
    edge, span = pseudo_ref.shape
    per = LANES // edge
    owners = count_ref.shape[1]
    slots = weight_ref.shape[1]
    capacity = slots // owners
    copy = pltpu.make_async_copy(
        part_ref, grid.at[:, pl.ds(ROWS, edge), pl.ds(LANES, span)], sem.at[0]
    )
    copy.start()
    even = is_even("grp")
    even_y = is_even("blk")
    for k in range(5):
        for side, row in ((0, ROWS - 1), (1, ROWS + edge)):
            grid[k, row : row + 1, LANES : LANES + span] = res_ref[side, 5 + k : 6 + k, :]
    copy.wait()
    for k in range(5):
        for side, row in ((0, ROWS), (1, ROWS + edge - 1)):
            at = (k, slice(row, row + 1), slice(LANES, LANES + span))
            grid[at] = grid[at] + res_ref[side, k : k + 1, :]

    lane = lax.broadcasted_iota(jnp.int32, (edge, LANES), 1)
    lane_row = lax.broadcasted_iota(jnp.int32, (1, LANES), 1)

    def pick(a_ref, b_ref, flag, k):
        g, q = divmod(k, per)
        value = jnp.where(flag, a_ref[g], b_ref[g])
        return pltpu.roll(value, LANES - q * edge, 1) if q else value

    for side in (0, 1):
        flag = even_y if side == 1 else jnp.logical_not(even_y)
        own = [pick(ya_ref, yb_ref, flag, k) for k in range(15)]
        other = [pick(sa_ref, sb_ref, flag, k) for k in range(16)]
        added, finished = meet(1, side, own, other[:15])
        base = LANES if side == 0 else span
        beyond = 0 if side == 0 else LANES + span
        rows = slice(ROWS, ROWS + edge)
        for k in range(5):
            if side == 0:
                extra = jnp.where(lane < edge, added[k], 0.0)
                halo = pltpu.roll(finished[k], LANES - edge, 1)
            else:
                extra = jnp.where(lane >= LANES - edge, pltpu.roll(added[k], LANES - edge, 1), 0.0)
                halo = finished[k]
            at = (k, rows, slice(base, base + LANES))
            grid[at] = grid[at] + extra
            grid[k, rows, beyond : beyond + LANES] = halo
        start = 0 if side == 0 else span - LANES
        for xs, row in ((0, ROWS - 1), (1, ROWS + edge)):
            flag_x = even if xs == 1 else jnp.logical_not(even)
            lanes = slice(start, start + LANES)
            state = [jnp.where(flag_x, ra_ref[k : k + 1, lanes], rb_ref[k : k + 1, lanes]) for k in range(11, 16)]
            corner = [other[15][2 * k + xs : 2 * k + xs + 1, :] for k in range(5)]
            if side == 1:
                corner = [pltpu.roll(v, LANES - edge, 1) for v in corner]
            extra = one_sided(state[:3], state[3], 1, 1.0 if side == 1 else -1.0, corner)
            inside = lane_row < edge if side == 0 else lane_row >= LANES - edge
            for k in range(5):
                at = (k, slice(row, row + 1), slice(base, base + LANES))
                grid[at] = grid[at] + jnp.where(inside, state[4] * extra[k], 0.0)

    def body(top, offset):
        lanes = pl.ds(offset, LANES)
        face_tiles = [face_ref[d, pl.ds(top, 2 * ROWS), lanes].astype(F32) for d in range(6)]
        tables = [[], [], [], []]
        for i_half in range(2):
            rows = pl.ds(top + i_half * ROWS, ROWS)
            vel, speed_sq, pressure, enthalpy, reach, faces, rhs = tile_coefficients(
                i_half, rows, lanes, state_ref, face_tiles, pseudo_ref, rhs_ref
            )
            out = sweep_tile(
                grid, ROWS + top + i_half * ROWS, pl.multiple_of(LANES + offset, LANES), edge,
                vel, speed_sq, enthalpy, reach, faces, rhs,
            )
            for k in range(5):
                field[k, rows, lanes] = out[k]
            for k in range(4):
                tables[k].append(pressure * out[1 + k])
        column = offset // (2 * LANES)
        wide = pl.ds(pl.multiple_of(lax.rem(offset, 2 * LANES), LANES), LANES)
        for k in range(4):
            big, small = split(jnp.concatenate(tables[k], axis=0))
            at = pl.ds(pl.multiple_of(k * (high.shape[0] // 4) + column * edge + top, 2 * ROWS), 2 * ROWS)
            high[at, wide] = big
            low[at, wide] = small

    for_each_tile(edge, span, body)
    store = pltpu.make_async_copy(field, out_ref, sem.at[1])
    store.start()

    table_rows = high.shape[0] // 4
    width = 2 * LANES
    step = min(slots, 512)
    gathered = [[], [], [], []]
    for s in range(0, slots, step):
        cell = cell_ref[:, s : s + step]
        x = cell // span
        yz = lax.rem(cell, span)
        row = (yz // width) * edge + x
        column = hot((width, step), lax.rem(yz, width))
        product = jnp.dot(high[...], column, preferred_element_type=F32)
        product = product + jnp.dot(low[...], column, preferred_element_type=F32)
        here = lax.broadcasted_iota(jnp.int32, (table_rows, step), 0) == row
        for k in range(4):
            piece = product[k * table_rows : (k + 1) * table_rows]
            gathered[k].append(jnp.sum(jnp.where(here, piece, 0.0), axis=0, keepdims=True))
    gathered = [jnp.concatenate(v, axis=1) for v in gathered]

    group = max(capacity, LANES)
    together = group // capacity
    vertex_rows = -(-together * PARTS // 16) * 16
    lane_group = lax.broadcasted_iota(jnp.int32, (1, group), 1)
    chunk = lane_group // capacity
    within = lax.rem(lane_group, capacity)
    for s in range(0, slots // group):
        lanes = slice(s * group, (s + 1) * group)
        count = count_ref[0, s * together]
        for q in range(1, together):
            count = jnp.where(chunk == q, count_ref[0, s * together + q], count)
        live = jnp.where(within < count, 1.0, 0.0)
        corner = [[coord_ref[c, k : k + 1, lanes] for k in range(3)] for c in range(4)]
        weights = [weight_ref[c : c + 1, lanes] * live for c in range(4)]
        terms = tet_terms(gathered[3][:, lanes], [gathered[k][:, lanes] for k in range(3)], corner, weights)
        left, right = [], []
        for c in range(4):
            vertex = vertex_ref[c : c + 1, lanes]
            row = vertex // LANES + chunk * PARTS
            match = lax.broadcasted_iota(jnp.int32, (vertex_rows, group), 0) == row
            blocks = []
            for k in range(3):
                blocks += split(jnp.where(match, terms[c][k], 0.0))
            left.append(jnp.concatenate(blocks, axis=0))
            right.append(hot((LANES, group), lax.rem(vertex, LANES)))
        product = lax.dot_general(
            jnp.concatenate(left, axis=1), jnp.concatenate(right, axis=1),
            (((1,), (1,)), ((), ())), preferred_element_type=F32,
        )
        for k in range(3):
            big = product[2 * k * vertex_rows : (2 * k + 1) * vertex_rows]
            small = product[(2 * k + 1) * vertex_rows : (2 * k + 2) * vertex_rows]
            total = big + small
            for q in range(together):
                owner = s * together + q
                sums[owner % 2, owner // 2, k * PARTS : (k + 1) * PARTS, :] = total[q * PARTS : (q + 1) * PARTS]
    core = lax.rem(lax.axis_index("blk"), 2)
    keep_ref[...] = sums[core]
    send_ref[...] = sums[1 - core]
    store.wait()


def fourth_kernel(keep_ref, got_ref, mine_ref, *refs):
    count = keep_ref.shape[0]
    me = lax.rem(lax.axis_index("blk") // 2, count)
    mine_ref[...] = keep_ref[me] + got_ref[me]
    for k, ref in enumerate(refs):
        partner = lax.bitwise_xor(me, k + 1)
        ref[...] = keep_ref[partner] + got_ref[partner]


def last_kernel(*refs):
    total = refs[0][...]
    for ref in refs[1:-1]:
        total = total + ref[...]
    for k in range(3):
        for part in range(PARTS):
            at = k * PARTS + part
            refs[-1][k : k + 1, part * LANES : (part + 1) * LANES] = total[at : at + 1, :]


def swap(value, axis, pairs):
    return lax.ppermute(value, axis, pairs + [(b, a) for a, b in pairs])


def neighbours(value_a, value_b, axis):
    count = lax.axis_size(axis)
    first = [(i, i + 1) for i in range(0, count - 1, 2)]
    second = [(i, i + 1) for i in range(1, count - 1, 2)]
    return swap(value_a, axis, first), swap(value_b, axis, second)


def local(
    adjoint_init, adjoint_rhs, flow_state, face_weights, pseudo_time,
    tet_coords, tet_weights, tet_cell, tet_vertex, tet_count,
):
    edge, span = pseudo_time.shape
    owners = tet_count.shape[1]
    blocks = lax.axis_size("blk")
    padded = (5, edge + 2 * ROWS, span + 2 * LANES)
    struct = jax.ShapeDtypeStruct
    packed = (16 * edge // LANES, edge, LANES)
    part, xa, xb, ylo, yhi = call(
        first_kernel,
        [struct((5, edge, span), F32), struct((16, span), F32), struct((16, span), F32),
         struct(packed, F32), struct(packed, F32)],
        [HBM, VMEM, VMEM, VMEM, VMEM],
        [VMEM] * 5,
        [pltpu.VMEM(padded, F32), pltpu.VMEM((8, edge, span), F32), pltpu.VMEM((2, 16, span), F32),
         pltpu.SemaphoreType.DMA],
        "partial_sweep",
    )(adjoint_init, adjoint_rhs, flow_state, face_weights, pseudo_time)
    ra, rb = neighbours(xa, xb, "grp")
    res, ya, yb = call(
        second_kernel,
        [struct((2, 16, span), F32), struct(packed, F32), struct(packed, F32)],
        [VMEM] * 6,
        [VMEM] * 3,
        [pltpu.VMEM((2,) + packed, F32)],
        "streamwise_halo",
    )(xa, xb, ra, rb, ylo, yhi)
    sa, sb = neighbours(ya, yb, "blk")
    half = owners // 2
    sums_shape = (half, 3 * PARTS, LANES)
    table = (4 * edge * span // (2 * LANES), 2 * LANES)
    adjoint, keep, send = call(
        third_kernel,
        [struct((5, edge, span), F32), struct(sums_shape, F32), struct(sums_shape, F32)],
        [HBM] + [VMEM] * 15 + [SMEM],
        [HBM, VMEM, VMEM],
        [pltpu.VMEM(padded, F32), pltpu.VMEM((5, edge, span), F32), pltpu.VMEM(table, BF16),
         pltpu.VMEM(table, BF16), pltpu.VMEM((2,) + sums_shape, F32), pltpu.SemaphoreType.DMA((2,))],
        "last_sweep_and_tets",
    )(
        part, adjoint_rhs, flow_state, face_weights, pseudo_time, res, ra, rb, ya, yb, sa, sb,
        tet_coords, tet_weights, tet_cell.reshape(1, -1), tet_vertex, tet_count,
    )
    got = swap(send, "blk", [(i, i + 1) for i in range(0, blocks, 2)])
    place = lax.axis_index("blk") // 2
    while half > 4:
        half //= 2
        both = (keep + got).reshape(2, half, 3 * PARTS, LANES)
        bit = lax.rem(place // half, 2)
        keep = lax.dynamic_index_in_dim(both, bit, 0, keepdims=False)
        send = lax.dynamic_index_in_dim(both, 1 - bit, 0, keepdims=False)
        got = lax.ppermute(send, "blk", [(i, i ^ (2 * half)) for i in range(blocks)])
    one = struct((3 * PARTS, LANES), F32)
    mine, *others = call(
        fourth_kernel, [one] * half, [VMEM] * 2, [VMEM] * half, [], "core_pair_sums"
    )(keep, got)
    others = [
        lax.ppermute(v, "blk", [(i, i ^ (2 * (k + 1))) for i in range(blocks)]) for k, v in enumerate(others)
    ]
    sensitivity = call(
        last_kernel, struct((3, VERT_DEV), F32), [VMEM] * half, VMEM, [], "own_sums"
    )(mine, *others)
    return adjoint, sensitivity


def solution(mesh):
    return jax.shard_map(
        local,
        mesh=mesh,
        in_specs=(
            P(None, "grp", "blk"),
            P(None, "grp", "blk"),
            P(None, "grp", "blk"),
            P(None, "grp", "blk"),
            P("grp", "blk"),
            P(None, None, ("grp", "blk")),
            P(None, ("grp", "blk")),
            P(("grp", "blk")),
            P(None, ("grp", "blk")),
            P(("grp", "blk"), None),
        ),
        out_specs=(P(None, "grp", "blk"), P(None, ("grp", "blk"))),
        check_vma=False,
    )
```

time: 248 us -> 41.1 us (0.17)
  the two profiles are of different devices: /device:TPU:5 before, /device:TPU:4 now
where the time goes in v1:
time: 41.1 us; the launch traced here: 40.6 us
  starting transfers between devices  13.8 us (34%)
  waiting for transfers between devices  11.5 us (28%)
  Pallas kernels  8.69 us (21%)
  local copies, waits for them, and re-layouts  5.87 us (14%)
  between operations  0.78 us (2%)
    ppermute x5, starting transfers between devices, swap(): return lax.ppermute(value, axis, pairs + [(b, a) for a, b in pairs])  9.32 us
    ppermute x5, waiting for transfers between devices, swap(): return lax.ppermute(value, axis, pairs + [(b, a) for a, b in pairs])  6.41 us
    unnamed x27, local copies, waits for them, and re-layouts  5.87 us
    pallas_call x1, Pallas kernels, local(): call(third_kernel, [struct((5, edge, span), F32), struct(sums_shape, F32)...  5.62 us
    ppermute x3, waiting for transfers between devices, local(): lax.ppermute(v, 'blk', [(i, i ^ 2 * (k + 1)) for i in range(blocks)])  5.1 us
    ppermute x3, starting transfers between devices, local(): lax.ppermute(v, 'blk', [(i, i ^ 2 * (k + 1)) for i in range(blocks)])  4.45 us
    pallas_call x1, Pallas kernels, local(): call(first_kernel, [struct((5, edge, span), F32), struct((16, span), F32)...  2.26 us
  transfers between devices with their start and end apart: 8, of which 6 were waited for; matrix products, arithmetic and copies ran while one was open for 0% of the time, Pallas kernels for 0%

profile of v1, /device:TPU:4, one launch (start us, length us, event | category | flops | bytes accessed | tf_op | source)
XLA Modules:
  0.0 40.6 jit_solution(5783233994468738549)
XLA Ops:
  0.6 1.1 %copy-done = f32[5,32,1024]{2,1,0:T(8,128)S(1)} copy-done((f32[5,32,1024]{2,1,0:T(8,128)S(1)}, f32[5,32,1024]{2,1,0:T(8,128)}, u32[]{:S(2)}) %copy-start) | copy-done | bytes 655384
  1.7 1.1 %copy-done.2 = f32[5,32,1024]{2,1,0:T(8,128)S(1)} copy-done((f32[5,32,1024]{2,1,0:T(8,128)S(1)}, f32[5,32,1024]{2,1,0:T(8,128)}, u32[]{:S(2)}) %copy-start.2) | copy-done | bytes 655384
  2.8 1.0 %copy-done.4 = bf16[6,32,1024]{2,1,0:T(8,128)(2,1)S(1)} copy-done((bf16[6,32,1024]{2,1,0:T(8,128)(2,1)S(1)}, bf16[6,32,1024]{2,1,0:T(8,128)(2,1)}, u32[]{:S(2)}) %copy-start.4) | copy-done | bytes 393240
  3.8 1.1 %copy-done.6 = f32[5,32,1024]{2,1,0:T(8,128)S(1)} copy-done((f32[5,32,1024]{2,1,0:T(8,128)S(1)}, f32[5,32,1024]{2,1,0:T(8,128)}, u32[]{:S(2)}) %copy-start.6) | copy-done | bytes 655384
  4.9 0.9 %copy-done.7 = f32[32,1024]{1,0:T(8,128)S(1)} copy-done((f32[32,1024]{1,0:T(8,128)S(1)}, f32[32,1024]{1,0:T(8,128)}, u32[]{:S(2)}) %copy-start.7) | copy-done | bytes 131096
  5.8 2.3 %partial_sweep.1 = (f32[5,32,1024]{2,1,0:T(8,128)S(1)}, f32[16,1024]{1,0:T(8,128)S(1)}, f32[16,1024]{1,0:T(8,128)S(1)}, f32[4,32,128]{2,1,0:T(8,128)S(1)}, f32[4,32,128]{2,1,0:T(8,128)S(1)}) custom-call(f32[5,32,1024]{2,1,0:T(8,128)S(1)} %copy-done.6, f32[5,32,1024]{2,1,0:T(8,128)S(1)} %copy-done, f32[5,32,1024]{2,1,0:T(8,128)S(1)} %copy-done.2, ...), custom_call_target="tpu_custom_call" | custom-call | tf_op jit(solution)/shard_map/partial_sweep/pallas_call | solution.py:509
  8.1 0.0 copy-start.5
  8.1 1.6 %collective-permute-start = (f32[16,1024]{1,0:T(8,128)S(1)}, f32[16,1024]{1,0:T(8,128)S(1)}, u32[]{:S(2)}, u32[]{:S(2)}) collective-permute-start(f32[16,1024]{1,0:T(8,128)S(1)} %get-tuple-element.18.xa_ref), channel_id=1, source_target_pairs={{0,8},{16,24},{8,0},{24,16},{1,9},{17,25},{9,1},{25,17},{2,10},{18... | collective-permute-start | bytes 196616 | tf_op jit(solution)/shard_map/ppermute | solution.py:489
  9.6 2.0 %collective-permute-start.1 = (f32[16,1024]{1,0:T(8,128)S(1)}, f32[16,1024]{1,0:T(8,128)S(1)}, u32[]{:S(2)}, u32[]{:S(2)}) collective-permute-start(f32[16,1024]{1,0:T(8,128)S(1)} %get-tuple-element.19.xb_ref), channel_id=1, source_target_pairs={{8,16},{16,8},{9,17},{17,9},{10,18},{18,10},{11,19},{19,11},{12,20... | collective-permute-start | bytes 196616 | tf_op jit(solution)/shard_map/ppermute | solution.py:489
  11.6 0.8 %collective-permute-done.ra_ref = f32[16,1024]{1,0:T(8,128)S(1)} collective-permute-done((f32[16,1024]{1,0:T(8,128)S(1)}, f32[16,1024]{1,0:T(8,128)S(1)}, u32[]{:S(2)}, u32[]{:S(2)}) %collective-permute-start) | collective-permute-done | bytes 65568 | tf_op jit(solution)/shard_map/ppermute | solution.py:489
  12.4 4.3 %collective-permute-done.1.rb_ref = f32[16,1024]{1,0:T(8,128)S(1)} collective-permute-done((f32[16,1024]{1,0:T(8,128)S(1)}, f32[16,1024]{1,0:T(8,128)S(1)}, u32[]{:S(2)}, u32[]{:S(2)}) %collective-permute-start.1) | collective-permute-done | bytes 65568 | tf_op jit(solution)/shard_map/ppermute | solution.py:489
  16.7 0.2 streamwise_halo.1
  16.9 0.1 collective-permute-start.2
  16.9 0.0 copy-start.8
  17.0 0.0 copy-start.9
  17.0 0.7 %collective-permute-start.3 = (f32[4,32,128]{2,1,0:T(8,128)S(1)}, f32[4,32,128]{2,1,0:T(8,128)S(1)}, u32[]{:S(2)}, u32[]{:S(2)}) collective-permute-start(f32[4,32,128]{2,1,0:T(8,128)S(1)} %get-tuple-element.24.yb_ref), channel_id=1, source_target_pairs={{1,2},{3,4},{5,6},{2,1},{4,3},{6,5},{9,10},{11,12},{13,14},{10,9},... | collective-permute-start | bytes 196616 | tf_op jit(solution)/shard_map/ppermute | solution.py:489
  17.7 0.0 copy-start.10
  17.7 0.1 copy.12.coord_ref
  17.7 0.4 %collective-permute-done.2.sa_ref = f32[4,32,128]{2,1,0:T(8,128)S(1)} collective-permute-done((f32[4,32,128]{2,1,0:T(8,128)S(1)}, f32[4,32,128]{2,1,0:T(8,128)S(1)}, u32[]{:S(2)}, u32[]{:S(2)}) %collective-permute-start.2) | collective-permute-done | bytes 65568 | tf_op jit(solution)/shard_map/ppermute | solution.py:489
  18.2 0.0 collective-permute-done.3.sb_ref
  18.2 0.1 copy-done.10
  18.4 0.5 %copy-done.11 = s32[1,8]{1,0:T(1,128)S(1)} copy-done((s32[1,8]{1,0:T(1,128)S(1)}, s32[1,8]{1,0:T(1,128)}, u32[]{:S(2)}) %copy-start.11) | copy-done | bytes 56
  18.8 5.6 %last_sweep_and_tets.1 = (f32[5,32,1024]{2,1,0:T(8,128)}, f32[4,36,128]{2,1,0:T(8,128)S(1)}, f32[4,36,128]{2,1,0:T(8,128)S(1)}) custom-call(f32[5,32,1024]{2,1,0:T(8,128)S(1)} %get-tuple-element.17.part_ref, f32[5,32,1024]{2,1,0:T(8,128)S(1)} %copy-done.1, f32[5,32,1024]{2,1,0:T(8,128)S(1)} %copy-done.3, bf16[6,32,1024]{2,1,0:T(8,128)(2,1)S(1)} %copy-done.5, ...), custom_call_target="tpu_custom_call" | custom-call | tf_op jit(solution)/shard_map/last_sweep_and_tets/pallas_call | solution.py:532
  24.5 5.0 %collective-permute-start.4 = (f32[4,36,128]{2,1,0:T(8,128)S(1)}, f32[4,36,128]{2,1,0:T(8,128)S(1)}, u32[]{:S(2)}, u32[]{:S(2)}) collective-permute-start(f32[4,36,128]{2,1,0:T(8,128)S(1)} %get-tuple-element.27), channel_id=1, source_target_pairs={{0,1},{2,3},{4,5},{6,7},{1,0},{3,2},{5,4},{7,6},{8,9},{10,11},{12,... | collective-permute-start | bytes 221192 | tf_op jit(solution)/shard_map/ppermute | solution.py:489
  29.5 0.9 %collective-permute-done.4.got_ref = f32[4,36,128]{2,1,0:T(8,128)S(1)} collective-permute-done((f32[4,36,128]{2,1,0:T(8,128)S(1)}, f32[4,36,128]{2,1,0:T(8,128)S(1)}, u32[]{:S(2)}, u32[]{:S(2)}) %collective-permute-start.4) | collective-permute-done | bytes 73760 | tf_op jit(solution)/shard_map/ppermute | solution.py:489
  30.4 1.6 %collective-permute-start.5 = (f32[36,128]{1,0:T(8,128)S(1)}, f32[36,128]{1,0:T(8,128)S(1)}, u32[]{:S(2)}, u32[]{:S(2)}) collective-permute-start(f32[36,128]{1,0:T(8,128)S(1)} %get-tuple-element.29), channel_id=1, source_target_pairs={{0,2},{1,3},{2,0},{3,1},{4,6},{5,7},{6,4},{7,5},{8,10},{9,11},{10,... | collective-permute-start | bytes 55304 | tf_op jit(solution)/shard_map/ppermute | solution.py:558
  32.1 2.3 %collective-permute-start.6 = (f32[36,128]{1,0:T(8,128)S(1)}, f32[36,128]{1,0:T(8,128)S(1)}, u32[]{:S(2)}, u32[]{:S(2)}) collective-permute-start(f32[36,128]{1,0:T(8,128)S(1)} %get-tuple-element.30), channel_id=1, source_target_pairs={{0,4},{1,5},{2,6},{3,7},{4,0},{5,1},{6,2},{7,3},{8,12},{9,13},{10,... | collective-permute-start | bytes 55304 | tf_op jit(solution)/shard_map/ppermute | solution.py:558
  34.4 0.5 %collective-permute-start.7 = (f32[36,128]{1,0:T(8,128)S(1)}, f32[36,128]{1,0:T(8,128)S(1)}, u32[]{:S(2)}, u32[]{:S(2)}) collective-permute-start(f32[36,128]{1,0:T(8,128)S(1)} %get-tuple-element.31), channel_id=1, source_target_pairs={{0,6},{1,7},{2,4},{3,5},{4,2},{5,3},{6,0},{7,1},{8,14},{9,15},{10,... | collective-permute-start | bytes 55304 | tf_op jit(solution)/shard_map/ppermute | solution.py:558
  34.9 0.0 collective-permute-done.5.refs_1_
  34.9 2.0 %collective-permute-done.6.refs_2_ = f32[36,128]{1,0:T(8,128)S(1)} collective-permute-done((f32[36,128]{1,0:T(8,128)S(1)}, f32[36,128]{1,0:T(8,128)S(1)}, u32[]{:S(2)}, u32[]{:S(2)}) %collective-permute-start.6) | collective-permute-done | bytes 18464 | tf_op jit(solution)/shard_map/ppermute | solution.py:558
  36.9 3.1 %collective-permute-done.7.refs_3_ = f32[36,128]{1,0:T(8,128)S(1)} collective-permute-done((f32[36,128]{1,0:T(8,128)S(1)}, f32[36,128]{1,0:T(8,128)S(1)}, u32[]{:S(2)}, u32[]{:S(2)}) %collective-permute-start.7) | collective-permute-done | bytes 18464 | tf_op jit(solution)/shard_map/ppermute | solution.py:558
  40.0 0.6 %own_sums.1 = f32[3,1536]{1,0:T(4,128)} custom-call(f32[36,128]{1,0:T(8,128)S(1)} %get-tuple-element.28.refs_0_, f32[36,128]{1,0:T(8,128)S(1)} %collective-permute-done.5.refs_1_, f32[36,128]{1,0:T(8,128)S(1)} %collective-permute-done.6.refs_2_, f32[36,128]{1,0:T(8,128)S(1)} %collective-permute-done.7.refs_3_), custom_call_target="tpu_custom_call" | custom-call | tf_op jit(solution)/shard_map/own_sums/pallas_call | solution.py:560
  (16 shorter events, 0.0 us)
Async XLA Ops:
  0.6 1.1 %copy-start = (f32[5,32,1024]{2,1,0:T(8,128)S(1)}, f32[5,32,1024]{2,1,0:T(8,128)}, u32[]{:S(2)}) copy-start(f32[5,32,1024]{2,1,0:T(8,128)} %rhs_ref.3) | copy-start | bytes 1966084
  1.7 1.1 %copy-start.2 = (f32[5,32,1024]{2,1,0:T(8,128)S(1)}, f32[5,32,1024]{2,1,0:T(8,128)}, u32[]{:S(2)}) copy-start(f32[5,32,1024]{2,1,0:T(8,128)} %state_ref.3) | copy-start | bytes 1966084
  2.8 1.0 %copy-start.4 = (bf16[6,32,1024]{2,1,0:T(8,128)(2,1)S(1)}, bf16[6,32,1024]{2,1,0:T(8,128)(2,1)}, u32[]{:S(2)}) copy-start(bf16[6,32,1024]{2,1,0:T(8,128)(2,1)} %face_ref.3) | copy-start | bytes 1179652
  3.8 1.1 %copy-start.6 = (f32[5,32,1024]{2,1,0:T(8,128)S(1)}, f32[5,32,1024]{2,1,0:T(8,128)}, u32[]{:S(2)}) copy-start(f32[5,32,1024]{2,1,0:T(8,128)} %adjoint_ref.1) | copy-start | bytes 1966084
  4.9 0.9 %copy-start.7 = (f32[32,1024]{1,0:T(8,128)S(1)}, f32[32,1024]{1,0:T(8,128)}, u32[]{:S(2)}) copy-start(f32[32,1024]{1,0:T(8,128)} %pseudo_ref.3) | copy-start | bytes 393220
  5.8 11.8 %copy-start.12 = (f32[4,3,2048]{2,0,1:T(4,128)S(1)}, f32[4,3,2048]{2,0,1:T(4,128)}, u32[]{:S(2)}) copy-start(f32[4,3,2048]{2,0,1:T(4,128)} %param.15) | copy-start | bytes 294916
  5.8 12.4 %copy-start.1 = (f32[5,32,1024]{2,1,0:T(8,128)S(1)}, f32[5,32,1024]{2,1,0:T(8,128)}, u32[]{:S(2)}) copy-start(f32[5,32,1024]{2,1,0:T(8,128)} %rhs_ref.3) | copy-start | bytes 1966084
  5.8 12.4 %copy-start.3 = (f32[5,32,1024]{2,1,0:T(8,128)S(1)}, f32[5,32,1024]{2,1,0:T(8,128)}, u32[]{:S(2)}) copy-start(f32[5,32,1024]{2,1,0:T(8,128)} %state_ref.3) | copy-start | bytes 1966084
  8.1 10.1 %copy-start.5 = (bf16[6,32,1024]{2,1,0:T(8,128)(2,1)S(1)}, bf16[6,32,1024]{2,1,0:T(8,128)(2,1)}, u32[]{:S(2)}) copy-start(bf16[6,32,1024]{2,1,0:T(8,128)(2,1)} %face_ref.3) | copy-start | bytes 1179652
  8.1 4.3 %collective-permute-start = (f32[16,1024]{1,0:T(8,128)S(1)}, f32[16,1024]{1,0:T(8,128)S(1)}, u32[]{:S(2)}, u32[]{:S(2)}) collective-permute-start(f32[16,1024]{1,0:T(8,128)S(1)} %get-tuple-element.18.xa_ref), channel_id=1, source_target_pairs={{0,8},{16,24},{8,0},{24,16},{1,9},{17,25},{9,1},{25,17},{2,10},{18... | collective-permute-start | bytes 196616 | tf_op jit(solution)/shard_map/ppermute | solution.py:489
  9.6 7.0 %collective-permute-start.1 = (f32[16,1024]{1,0:T(8,128)S(1)}, f32[16,1024]{1,0:T(8,128)S(1)}, u32[]{:S(2)}, u32[]{:S(2)}) collective-permute-start(f32[16,1024]{1,0:T(8,128)S(1)} %get-tuple-element.19.xb_ref), channel_id=1, source_target_pairs={{8,16},{16,8},{9,17},{17,9},{10,18},{18,10},{11,19},{19,11},{12,20... | collective-permute-start | bytes 196616 | tf_op jit(solution)/shard_map/ppermute | solution.py:489
  16.9 1.3 %collective-permute-start.2 = (f32[4,32,128]{2,1,0:T(8,128)S(1)}, f32[4,32,128]{2,1,0:T(8,128)S(1)}, u32[]{:S(2)}, u32[]{:S(2)}) collective-permute-start(f32[4,32,128]{2,1,0:T(8,128)S(1)} %get-tuple-element.23.ya_ref), channel_id=1, source_target_pairs={{0,1},{2,3},{4,5},{6,7},{1,0},{3,2},{5,4},{7,6},{8,9},{10,11},{12,... | collective-permute-start | bytes 196616 | tf_op jit(solution)/shard_map/ppermute | solution.py:489
  16.9 1.3 %copy-start.8 = (f32[4,2048]{1,0:T(4,128)S(1)}, f32[4,2048]{1,0:T(4,128)}, u32[]{:S(2)}) copy-start(f32[4,2048]{1,0:T(4,128)} %weight_ref.1) | copy-start | bytes 98308
  17.0 1.3 %copy-start.9 = (s32[4,2048]{1,0:T(4,128)S(1)}, s32[4,2048]{1,0:T(4,128)}, u32[]{:S(2)}) copy-start(s32[4,2048]{1,0:T(4,128)} %vertex_ref.1) | copy-start | bytes 98308
  17.0 1.2 %collective-permute-start.3 = (f32[4,32,128]{2,1,0:T(8,128)S(1)}, f32[4,32,128]{2,1,0:T(8,128)S(1)}, u32[]{:S(2)}, u32[]{:S(2)}) collective-permute-start(f32[4,32,128]{2,1,0:T(8,128)S(1)} %get-tuple-element.24.yb_ref), channel_id=1, source_target_pairs={{1,2},{3,4},{5,6},{2,1},{4,3},{6,5},{9,10},{11,12},{13,14},{10,9},... | collective-permute-start | bytes 196616 | tf_op jit(solution)/shard_map/ppermute | solution.py:489
  17.7 0.7 %copy-start.10 = (s32[2048]{0:T(1024)S(1)}, s32[2048]{0:T(1024)}, u32[]{:S(2)}) copy-start(s32[2048]{0:T(1024)} %param.17) | copy-start | bytes 24580
  18.2 0.7 %copy-start.11 = (s32[1,8]{1,0:T(1,128)S(1)}, s32[1,8]{1,0:T(1,128)}, u32[]{:S(2)}) copy-start(s32[1,8]{1,0:T(1,128)} %count_ref.1) | copy-start | bytes 100
  24.5 6.0 %collective-permute-start.4 = (f32[4,36,128]{2,1,0:T(8,128)S(1)}, f32[4,36,128]{2,1,0:T(8,128)S(1)}, u32[]{:S(2)}, u32[]{:S(2)}) collective-permute-start(f32[4,36,128]{2,1,0:T(8,128)S(1)} %get-tuple-element.27), channel_id=1, source_target_pairs={{0,1},{2,3},{4,5},{6,7},{1,0},{3,2},{5,4},{7,6},{8,9},{10,11},{12,... | collective-permute-start | bytes 221192 | tf_op jit(solution)/shard_map/ppermute | solution.py:489
  30.4 4.5 %collective-permute-start.5 = (f32[36,128]{1,0:T(8,128)S(1)}, f32[36,128]{1,0:T(8,128)S(1)}, u32[]{:S(2)}, u32[]{:S(2)}) collective-permute-start(f32[36,128]{1,0:T(8,128)S(1)} %get-tuple-element.29), channel_id=1, source_target_pairs={{0,2},{1,3},{2,0},{3,1},{4,6},{5,7},{6,4},{7,5},{8,10},{9,11},{10,... | collective-permute-start | bytes 55304 | tf_op jit(solution)/shard_map/ppermute | solution.py:558
  32.1 4.8 %collective-permute-start.6 = (f32[36,128]{1,0:T(8,128)S(1)}, f32[36,128]{1,0:T(8,128)S(1)}, u32[]{:S(2)}, u32[]{:S(2)}) collective-permute-start(f32[36,128]{1,0:T(8,128)S(1)} %get-tuple-element.30), channel_id=1, source_target_pairs={{0,4},{1,5},{2,6},{3,7},{4,0},{5,1},{6,2},{7,3},{8,12},{9,13},{10,... | collective-permute-start | bytes 55304 | tf_op jit(solution)/shard_map/ppermute | solution.py:558
  34.4 5.6 %collective-permute-start.7 = (f32[36,128]{1,0:T(8,128)S(1)}, f32[36,128]{1,0:T(8,128)S(1)}, u32[]{:S(2)}, u32[]{:S(2)}) collective-permute-start(f32[36,128]{1,0:T(8,128)S(1)} %get-tuple-element.31), channel_id=1, source_target_pairs={{0,6},{1,7},{2,4},{3,5},{4,2},{5,3},{6,0},{7,1},{8,14},{9,15},{10,... | collective-permute-start | bytes 55304 | tf_op jit(solution)/shard_map/ppermute | solution.py:558

commit v2 on v1

v2 whole, which is shorter than its diff:
```python
import functools
import jax
import jax.numpy as jnp
from jax import lax
from jax.experimental import pallas as pl
from jax.experimental.pallas import tpu as pltpu
from jax.sharding import PartitionSpec as P

VERT_DEV = 1536
GAMMA = 1.4
LANES = 128
ROWS = 8
PARTS = VERT_DEV // LANES
F32 = jnp.float32
BF16 = jnp.bfloat16
VMEM = pl.BlockSpec(memory_space=pltpu.VMEM)
SMEM = pl.BlockSpec(memory_space=pltpu.SMEM)
HBM = pl.BlockSpec(memory_space=pltpu.HBM)
LIMIT = 40 * 1024 * 1024


def call(kernel, outs, in_specs, out_specs, scratch, name, flops=1000, aliases={}):
    return pl.pallas_call(
        kernel,
        out_shape=outs,
        in_specs=in_specs,
        out_specs=out_specs,
        scratch_shapes=scratch,
        compiler_params=pltpu.CompilerParams(vmem_limit_bytes=LIMIT),
        cost_estimate=pl.CostEstimate(flops=flops, bytes_accessed=flops // 4, transcendentals=0),
        input_output_aliases=aliases,
        name=name,
    )


def is_even(axis):
    return lax.rem(lax.axis_index(axis), 2) == 0


def reach_of(speed_sq, enthalpy):
    sound_sq = (GAMMA - 1.0) * (enthalpy - 0.5 * speed_sq)
    return jnp.sqrt(speed_sq) + jnp.sqrt(sound_sq)


def transposed(vel, enthalpy, half_sq, axis_id, field):
    normal = vel[axis_id]
    energy = normal * field[4]
    common = vel[0] * field[1] + vel[1] * field[2] + vel[2] * field[3] + enthalpy * field[4]
    along = field[1 + axis_id] + energy
    scaled = (GAMMA - 1.0) * along
    out = [half_sq * along - normal * common]
    for j in range(3):
        entry = normal * field[1 + j] - vel[j] * scaled
        if j == axis_id:
            entry = entry + (field[0] + common)
        out.append(entry)
    out.append(scaled + energy)
    return out


def one_sided(vel, enthalpy, axis_id, sign, field):
    speed_sq = vel[0] * vel[0] + vel[1] * vel[1] + vel[2] * vel[2]
    reach = reach_of(speed_sq, enthalpy)
    turned = transposed(vel, enthalpy, 0.5 * (GAMMA - 1.0) * speed_sq, axis_id, field)
    return [sign * turned[k] + reach * field[k] for k in range(5)]


def cell_state(state):
    density, m1, m2, m3, energy = state
    inverse = 1.0 / density
    vel = [m1 * inverse, m2 * inverse, m3 * inverse]
    speed_sq = vel[0] * vel[0] + vel[1] * vel[1] + vel[2] * vel[2]
    pressure = (GAMMA - 1.0) * (energy - 0.5 * density * speed_sq)
    enthalpy = (energy + pressure) * inverse
    reach = jnp.sqrt(speed_sq) + jnp.sqrt(GAMMA * pressure * inverse)
    return vel, speed_sq, pressure, enthalpy, reach


def combine(rhs, reach, vel, speed_sq, enthalpy, faces, pairs):
    spread = None
    total = None
    for axis_id, (upper, lower) in enumerate(pairs):
        upper = [faces[2 * axis_id] * v for v in upper]
        lower = [faces[2 * axis_id + 1] * v for v in lower]
        both = [u + v for u, v in zip(upper, lower)]
        difference = [u - v for u, v in zip(upper, lower)]
        spread = both if spread is None else [u + v for u, v in zip(spread, both)]
        turned = transposed(vel, enthalpy, 0.5 * (GAMMA - 1.0) * speed_sq, axis_id, difference)
        total = turned if total is None else [u + v for u, v in zip(total, turned)]
    return [rhs[k] + total[k] + reach * spread[k] for k in range(5)]


def inside_faces(faces, edge, shape):
    depth = lax.rem(lax.broadcasted_iota(jnp.int32, shape, 1), edge)
    faces = list(faces)
    faces[4] = jnp.where(depth == edge - 1, 0.0, faces[4])
    faces[5] = jnp.where(depth == 0, 0.0, faces[5])
    return faces


def lane_pairs(here, after, before, edge, shape):
    place = lax.broadcasted_iota(jnp.int32, shape, 1)
    first = place < edge
    last = place >= LANES - edge
    along_y = (
        [pltpu.roll(jnp.where(first, a, h), LANES - edge, 1) for h, a in zip(here, after)],
        [pltpu.roll(jnp.where(last, b, h), edge, 1) for h, b in zip(here, before)],
    )
    along_z = ([pltpu.roll(h, LANES - 1, 1) for h in here], [pltpu.roll(h, 1, 1) for h in here])
    return along_y, along_z


def sweep_tile(grid, row, lane, edge, vel, speed_sq, enthalpy, reach, faces, rhs):
    def at(drow, dlane):
        return [grid[k, pl.ds(row + drow, ROWS), pl.ds(lane + dlane, LANES)] for k in range(5)]

    shape = (ROWS, LANES)
    pairs = lane_pairs(at(0, 0), at(0, LANES), at(0, -LANES), edge, shape)
    return combine(
        rhs, reach, vel, speed_sq, enthalpy, inside_faces(faces, edge, shape), ((at(1, 0), at(-1, 0)),) + pairs
    )


def coefficients(state, faces, pseudo, rhs):
    vel, speed_sq, pressure, enthalpy, reach = cell_state(state)
    area = faces[0]
    for f in faces[1:]:
        area = area + f
    inverse = 1.0 / (pseudo + 0.5 * reach * area)
    half = 0.5 * inverse
    return vel, speed_sq, pressure, enthalpy, reach, [half * f for f in faces], [inverse * v for v in rhs]


def tile_coefficients(i_half, rows, lanes, state_ref, face_tiles, pseudo_ref, rhs_ref):
    return coefficients(
        [state_ref[k, rows, lanes] for k in range(5)],
        [f[i_half * ROWS : (i_half + 1) * ROWS] for f in face_tiles],
        pseudo_ref[rows, lanes],
        [rhs_ref[k, rows, lanes] for k in range(5)],
    )


def clear_pads(grid, edge, span):
    high = grid.shape[1]
    wide = grid.shape[2]
    for k in range(5):
        grid[k, 0:ROWS, :] = jnp.zeros((ROWS, wide), F32)
        grid[k, ROWS + edge : high, :] = jnp.zeros((high - ROWS - edge, wide), F32)
        grid[k, ROWS : ROWS + edge, 0:LANES] = jnp.zeros((edge, LANES), F32)
        grid[k, ROWS : ROWS + edge, LANES + span : wide] = jnp.zeros((edge, LANES), F32)


def for_each_tile(edge, first, last, body):
    for top in range(0, edge, 2 * ROWS):

        def step(j, carry, top=top):
            body(top, pl.multiple_of(j * LANES, LANES))
            return carry

        lax.fori_loop(first, last, step, 0)


def plane_kernel(
    adjoint_hbm, rhs_hbm, state_hbm, face_hbm, pseudo_hbm,
    xa_ref, xb_ref,
    adjoint_ref, rhs_ref, state_ref, face_ref, pseudo_ref, xsides, sem,
):
    edge, span = pseudo_hbm.shape
    copies = [pltpu.make_async_copy(face_hbm, face_ref, sem.at[0])]
    for source, target in (
        (state_hbm, state_ref), (adjoint_hbm, adjoint_ref), (rhs_hbm, rhs_ref), (pseudo_hbm, pseudo_ref)
    ):
        for side in (0, 1):
            there = pl.ds(side * (edge - ROWS), ROWS)
            here = pl.ds(side * ROWS, ROWS)
            whole = (slice(None),) * (len(source.shape) - 2)
            copies.append(
                pltpu.make_async_copy(
                    source.at[whole + (there,)], target.at[whole + (here,)], sem.at[len(copies)]
                )
            )
    for copy in copies:
        copy.start()
    for copy in copies:
        copy.wait()
    even = is_even("grp")
    shape = (2, LANES)
    upper_row = lax.broadcasted_iota(jnp.int32, shape, 0) == 1
    sub = lax.broadcasted_iota(jnp.int32, (ROWS, LANES), 0)
    place = lax.broadcasted_iota(jnp.int32, shape, 1)
    tiles = span // LANES
    zero = jnp.zeros(shape, F32)

    def planes(ref, k, j, inner=0):
        at = (k,) if k is not None else ()
        lanes = slice(j * LANES, (j + 1) * LANES)
        last = 2 * ROWS - 2 - inner
        return jnp.where(upper_row, ref[at + (slice(last, last + 2), lanes)], ref[at + (slice(inner, inner + 2), lanes)])

    for j in range(tiles):
        lanes = pl.ds(j * LANES, LANES)
        faces = []
        for d in range(6):
            low = face_ref[d, pl.ds(0, 2 * ROWS), lanes].astype(F32)[:ROWS]
            high = face_ref[d, pl.ds(edge - 2 * ROWS, 2 * ROWS), lanes].astype(F32)[ROWS:]
            faces.append(jnp.where(sub == 0, low, pltpu.roll(high, 2, 0))[:2])
        vel, speed_sq, pressure, enthalpy, reach, faces, rhs = coefficients(
            [planes(state_ref, k, j) for k in range(5)],
            faces,
            planes(pseudo_ref, None, j),
            [planes(rhs_ref, k, j) for k in range(5)],
        )
        here = [planes(adjoint_ref, k, j) for k in range(5)]
        after = [planes(adjoint_ref, k, j + 1) if j + 1 < tiles else zero for k in range(5)]
        before = [planes(adjoint_ref, k, j - 1) if j > 0 else zero for k in range(5)]
        inner = [planes(adjoint_ref, k, j, 1) for k in range(5)]
        along_x = ([jnp.where(upper_row, 0.0, v) for v in inner], [jnp.where(upper_row, v, 0.0) for v in inner])
        pairs = lane_pairs(here, after, before, edge, shape)
        out = combine(
            rhs, reach, vel, speed_sq, enthalpy, inside_faces(faces, edge, shape), (along_x,) + pairs
        )
        message = out + here + [jnp.where(upper_row, faces[0], faces[1])] + vel + [enthalpy]
        message.append(jnp.where(place < edge, faces[3], faces[2]) if j == 0 else faces[2])
        for side in (0, 1):
            slot = jnp.where(even, 1 - side, side)
            for k, value in enumerate(message):
                xsides[slot, k : k + 1, lanes] = value[side : side + 1]
    xa_ref[...] = xsides[0]
    xb_ref[...] = xsides[1]


def first_kernel(
    adjoint_ref, rhs_ref, state_ref, face_ref, pseudo_ref, coord_ref, weight_ref, cell_ref, vertex_ref, count_ref,
    part_ref, ylo_ref, yhi_ref, column_ref, vertex_hot_ref, shape_ref,
    grid, coef,
):
    edge, span = pseudo_ref.shape
    clear_pads(grid, edge, span)
    for k in range(5):
        grid[k, ROWS : ROWS + edge, LANES : LANES + span] = adjoint_ref[k]

    def body(top, offset):
        lanes = pl.ds(offset, LANES)
        face_tiles = [face_ref[d, pl.ds(top, 2 * ROWS), lanes].astype(F32) for d in range(6)]
        for i_half in range(2):
            rows = pl.ds(top + i_half * ROWS, ROWS)
            vel, speed_sq, pressure, enthalpy, reach, faces, rhs = tile_coefficients(
                i_half, rows, lanes, state_ref, face_tiles, pseudo_ref, rhs_ref
            )
            out = sweep_tile(
                grid, ROWS + top + i_half * ROWS, pl.multiple_of(LANES + offset, LANES), edge,
                vel, speed_sq, enthalpy, reach, faces, rhs,
            )
            for k in range(5):
                part_ref[k, rows, lanes] = out[k]
            for k, value in enumerate(vel + [enthalpy] + faces[2:4]):
                coef[k, rows, lanes] = value

    for_each_tile(edge, 0, span // LANES, body)

    lane = lax.broadcasted_iota(jnp.int32, (edge, LANES), 1)
    quarter = lane // edge
    for side, base, ref in ((0, 0, ylo_ref), (1, span - LANES, yhi_ref)):
        lanes = slice(base, base + LANES)
        fields = [part_ref[k, :, lanes] for k in range(5)]
        fields += [grid[k, ROWS : ROWS + edge, LANES + base : LANES + base + LANES] for k in range(5)]
        fields += [coef[4 + 1 - side, :, lanes]]
        fields += [coef[k, :, lanes] for k in range(4)]
        start = 0 if side == 0 else LANES - edge
        per = LANES // edge
        for g in range(4):
            packed = None
            for q in range(per):
                k = g * per + q
                if k >= len(fields):
                    value = jnp.zeros((edge, LANES), F32)
                else:
                    shift = (q * edge - start) % LANES
                    value = pltpu.roll(fields[k], shift, 1) if shift else fields[k]
                packed = value if packed is None else jnp.where(quarter == q, value, packed)
            ref[g] = packed

    owners = count_ref.shape[1]
    slots = weight_ref.shape[1]
    capacity = slots // owners
    width = 2 * LANES
    step = min(slots, 512)
    for s in range(0, slots, step):
        part = slice(s, s + step)
        column = lax.rem(cell_ref[:, part] + LANES, width)
        column_ref[:, part] = hot((width, step), column)
        for c in range(4):
            vertex_hot_ref[c, :, part] = hot((LANES, step), lax.rem(vertex_ref[c : c + 1, part], LANES))

    group = max(capacity, LANES)
    together = group // capacity
    lane_group = lax.broadcasted_iota(jnp.int32, (1, group), 1)
    chunk = lane_group // capacity
    within = lax.rem(lane_group, capacity)
    for s in range(0, slots // group):
        lanes = slice(s * group, (s + 1) * group)
        count = count_ref[0, s * together]
        for q in range(1, together):
            count = jnp.where(chunk == q, count_ref[0, s * together + q], count)
        live = jnp.where(within < count, 1.0, 0.0)
        weights = [weight_ref[c : c + 1, lanes] * live for c in range(4)]
        corner = [[coord_ref[k, c : c + 1, lanes] for k in range(3)] for c in range(4)]
        for k, value in enumerate(tet_shapes(corner, weights)):
            shape_ref[k : k + 1, lanes] = value


def meet(axis_id, side, own, other):
    sign = 1.0 if side == 1 else -1.0
    mine = one_sided(own[11:14], own[14], axis_id, sign, other[5:10])
    theirs = one_sided(other[11:14], other[14], axis_id, -sign, own[5:10])
    added = [own[10] * v for v in mine]
    finished = [other[k] + other[10] * theirs[k] for k in range(5)]
    return added, finished


def second_kernel(xa_ref, xb_ref, ra_ref, rb_ref, ylo_ref, yhi_ref, res_ref, ya_ref, yb_ref, ysides):
    span = xa_ref.shape[1]
    edge = ylo_ref.shape[1]
    per = LANES // edge
    even = is_even("grp")
    even_y = is_even("blk")
    ysides[0] = ylo_ref[...]
    ysides[1] = yhi_ref[...]
    lane = lax.broadcasted_iota(jnp.int32, (1, LANES), 1)
    quarter = lane // edge

    def pick(a_ref, b_ref, flag):
        return [jnp.where(flag, a_ref[k : k + 1, :], b_ref[k : k + 1, :]) for k in range(15)]

    for side in (0, 1):
        flag = even if side == 1 else jnp.logical_not(even)
        own = pick(xa_ref, xb_ref, flag)
        other = pick(ra_ref, rb_ref, flag)
        added, finished = meet(0, side, own, other)
        row = 0 if side == 0 else edge - 1
        for k in range(5):
            res_ref[side, k : k + 1, :] = added[k]
            res_ref[side, 5 + k : 6 + k, :] = finished[k]
        for ys, base, start in ((0, 0, 0), (1, span - LANES, LANES - edge)):
            for k in range(5):
                g, q = divmod(k, per)
                shift = (q * edge - start) % LANES
                piece = added[k][:, base : base + LANES]
                piece = pltpu.roll(piece, shift, 1) if shift else piece
                old = ysides[ys, g, row : row + 1, :]
                ysides[ys, g, row : row + 1, :] = old + jnp.where(quarter == q, piece, 0.0)
                g, q = divmod(15, per)
                shift = (q * edge - start) % LANES
                piece = other[5 + k][:, base : base + LANES]
                piece = pltpu.roll(piece, shift, 1) if shift else piece
                at = 2 * k + side
                old = ysides[ys, g, at : at + 1, :]
                ysides[ys, g, at : at + 1, :] = jnp.where(quarter == q, piece, old)
    ya_ref[...] = ysides[jnp.where(even_y, 1, 0)]
    yb_ref[...] = ysides[jnp.where(even_y, 0, 1)]


def cross(left, right):
    return [
        left[1] * right[2] - left[2] * right[1],
        left[2] * right[0] - left[0] * right[2],
        left[0] * right[1] - left[1] * right[0],
    ]


def minus(left, right):
    return [u - v for u, v in zip(left, right)]


def tet_shapes(corner, weights):
    edge_one = minus(corner[1], corner[0])
    edge_two = minus(corner[2], corner[0])
    edge_three = minus(corner[3], corner[0])
    g1 = cross(edge_two, edge_three)
    g2 = cross(edge_three, edge_one)
    g3 = cross(edge_one, edge_two)
    g0 = [-(u + v + w) for u, v, w in zip(g1, g2, g3)]
    sixth = [w * (1.0 / 6.0) for w in weights]
    half = [w * 0.5 for w in weights]
    out = []
    for c, g in enumerate((g0, g1, g2, g3)):
        out += [sixth[c] * v for v in g]
    out += [half[1] * v for v in minus(corner[2], corner[3])]
    out += [half[2] * v for v in minus(corner[3], corner[1])]
    out += [half[3] * v for v in minus(corner[1], corner[2])]
    return out


def tet_terms(volume, face, shape):
    terms = []
    for c in range(4):
        term = [volume * shape[3 * c + k] for k in range(3)]
        if c:
            turned = cross(shape[9 + 3 * c : 12 + 3 * c], face)
            term = [u + v for u, v in zip(term, turned)]
        terms.append(term)
    return terms


def split(value):
    high = value.astype(BF16)
    return high, (value - high.astype(F32)).astype(BF16)


def hot(shape, index):
    rows = lax.broadcasted_iota(jnp.int32, shape, 0)
    return jnp.where(rows == index, 1.0, 0.0).astype(BF16)


def gather(high, low, column_ref, row):
    table_rows = high.shape[0] // 4
    slots = column_ref.shape[1]
    step = min(slots, 512)
    gathered = [[], [], [], []]
    for s in range(0, slots, step):
        column = column_ref[:, s : s + step]
        product = jnp.dot(high[...], column, preferred_element_type=F32)
        product = product + jnp.dot(low[...], column, preferred_element_type=F32)
        here = lax.broadcasted_iota(jnp.int32, (table_rows, step), 0) == row[:, s : s + step]
        for k in range(4):
            piece = product[k * table_rows : (k + 1) * table_rows]
            gathered[k].append(jnp.sum(jnp.where(here, piece, 0.0), axis=0, keepdims=True))
    return [jnp.concatenate(v, axis=1) for v in gathered]


def chunk_of(cell, span):
    yz = lax.rem(cell, span) + LANES
    return cell // span, lax.rem(yz // (2 * LANES), span // (2 * LANES))


def middle_kernel(
    part_ref, rhs_ref, state_ref, face_ref, pseudo_ref, res_ref, column_ref, cell_ref,
    out_ref, gathered_ref,
    grid, field, high, low, sem,
):
    edge, span = pseudo_ref.shape
    tiles = span // LANES
    for k in range(5):
        grid[k, ROWS : ROWS + edge, LANES : LANES + span] = part_ref[k]
    for k in range(5):
        for side, row, beyond in ((0, ROWS, ROWS - 1), (1, ROWS + edge - 1, ROWS + edge)):
            at = (k, slice(row, row + 1), slice(LANES, LANES + span))
            grid[at] = grid[at] + res_ref[side, k : k + 1, :]
            grid[k, beyond : beyond + 1, LANES : LANES + span] = res_ref[side, 5 + k : 6 + k, :]

    def body(top, offset):
        lanes = pl.ds(offset, LANES)
        face_tiles = [face_ref[d, pl.ds(top, 2 * ROWS), lanes].astype(F32) for d in range(6)]
        tables = [[], [], [], []]
        for i_half in range(2):
            rows = pl.ds(top + i_half * ROWS, ROWS)
            vel, speed_sq, pressure, enthalpy, reach, faces, rhs = tile_coefficients(
                i_half, rows, lanes, state_ref, face_tiles, pseudo_ref, rhs_ref
            )
            out = sweep_tile(
                grid, ROWS + top + i_half * ROWS, pl.multiple_of(LANES + offset, LANES), edge,
                vel, speed_sq, enthalpy, reach, faces, rhs,
            )
            for k in range(5):
                field[k, rows, pl.ds(pl.multiple_of(offset - LANES, LANES), LANES)] = out[k]
            for k in range(4):
                tables[k].append(pressure * out[1 + k])
        chunk = (offset - LANES) // (2 * LANES)
        wide = pl.ds(pl.multiple_of(lax.rem(offset - LANES, 2 * LANES), LANES), LANES)
        for k in range(4):
            big, small = split(jnp.concatenate(tables[k], axis=0))
            at = pl.ds(pl.multiple_of(k * (high.shape[0] // 4) + chunk * edge + top, 2 * ROWS), 2 * ROWS)
            high[at, wide] = big
            low[at, wide] = small

    for_each_tile(edge, 1, tiles - 1, body)
    store = pltpu.make_async_copy(field, out_ref.at[:, :, pl.ds(LANES, span - 2 * LANES)], sem)
    store.start()
    x, chunk = chunk_of(cell_ref[...], span)
    row = jnp.where(chunk > 0, (chunk - 1) * edge + x, -1)
    for k, value in enumerate(gather(high, low, column_ref, row)):
        gathered_ref[k : k + 1, :] = value
    store.wait()


def third_kernel(
    adjoint_ref, part_ref, rhs_ref, state_ref, face_ref, pseudo_ref, res_ref, ra_ref, rb_ref,
    ya_ref, yb_ref, sa_ref, sb_ref, gathered_ref, column_ref, cell_ref, vertex_ref, vertex_hot_ref, shape_ref,
    out_ref, keep_ref, send_ref,
    grids, field, high, low, sums, sem,
):
    edge, span = pseudo_ref.shape
    per = LANES // edge
    owners = 2 * keep_ref.shape[0]
    slots = cell_ref.shape[1]
    capacity = slots // owners
    even = is_even("grp")
    even_y = is_even("blk")
    lane = lax.broadcasted_iota(jnp.int32, (edge, LANES), 1)
    lane_row = lax.broadcasted_iota(jnp.int32, (1, LANES), 1)
    rows = slice(ROWS, ROWS + edge)
    stores = []

    def pick(a_ref, b_ref, flag, k):
        g, q = divmod(k, per)
        value = jnp.where(flag, a_ref[g], b_ref[g])
        return pltpu.roll(value, LANES - q * edge, 1) if q else value

    for side in (0, 1):
        grid = grids.at[side]
        start = 0 if side == 0 else span - 2 * LANES
        lanes = slice(start, start + 2 * LANES)
        base = LANES if side == 0 else 0
        into = slice(base, base + 2 * LANES)
        for k in range(5):
            grid[k, rows, into] = part_ref[k, :, lanes]
            for xs, row, beyond in ((0, ROWS, ROWS - 1), (1, ROWS + edge - 1, ROWS + edge)):
                at = (k, slice(row, row + 1), into)
                grid[at] = grid[at] + res_ref[xs, k : k + 1, lanes]
                grid[k, beyond : beyond + 1, into] = res_ref[xs, 5 + k : 6 + k, lanes]
        flag = even_y if side == 1 else jnp.logical_not(even_y)
        own = [pick(ya_ref, yb_ref, flag, k) for k in range(15)]
        other = [pick(sa_ref, sb_ref, flag, k) for k in range(16)]
        added, finished = meet(1, side, own, other[:15])
        beyond = 0 if side == 0 else 2 * LANES
        for k in range(5):
            if side == 0:
                extra = jnp.where(lane < edge, added[k], 0.0)
                halo = pltpu.roll(finished[k], LANES - edge, 1)
            else:
                extra = jnp.where(lane >= LANES - edge, pltpu.roll(added[k], LANES - edge, 1), 0.0)
                halo = finished[k]
            at = (k, rows, slice(LANES, 2 * LANES))
            grid[at] = grid[at] + extra
            grid[k, rows, beyond : beyond + LANES] = halo
        start = 0 if side == 0 else span - LANES
        for xs, row in ((0, ROWS - 1), (1, ROWS + edge)):
            flag_x = even if xs == 1 else jnp.logical_not(even)
            lanes = slice(start, start + LANES)
            state = [jnp.where(flag_x, ra_ref[k : k + 1, lanes], rb_ref[k : k + 1, lanes]) for k in range(11, 16)]
            corner = [other[15][2 * k + xs : 2 * k + xs + 1, :] for k in range(5)]
            if side == 1:
                corner = [pltpu.roll(v, LANES - edge, 1) for v in corner]
            extra = one_sided(state[:3], state[3], 1, 1.0 if side == 1 else -1.0, corner)
            inside = lane_row < edge if side == 0 else lane_row >= LANES - edge
            for k in range(5):
                at = (k, slice(row, row + 1), slice(LANES, 2 * LANES))
                grid[at] = grid[at] + jnp.where(inside, state[4] * extra[k], 0.0)

        lanes = pl.ds(start, LANES)
        wide = slice(LANES, 2 * LANES) if side == 0 else slice(0, LANES)
        for top in range(0, edge, 2 * ROWS):
            face_tiles = [face_ref[d, pl.ds(top, 2 * ROWS), lanes].astype(F32) for d in range(6)]
            tables = [[], [], [], []]
            for i_half in range(2):
                here = pl.ds(top + i_half * ROWS, ROWS)
                vel, speed_sq, pressure, enthalpy, reach, faces, rhs = tile_coefficients(
                    i_half, here, lanes, state_ref, face_tiles, pseudo_ref, rhs_ref
                )
                out = sweep_tile(
                    grid, ROWS + top + i_half * ROWS, LANES, edge, vel, speed_sq, enthalpy, reach, faces, rhs
                )
                for k in range(5):
                    field[side, k, here, :] = out[k]
                for k in range(4):
                    tables[k].append(pressure * out[1 + k])
            for k in range(4):
                big, small = split(jnp.concatenate(tables[k], axis=0))
                at = slice(k * edge + top, k * edge + top + 2 * ROWS)
                high[at, wide] = big
                low[at, wide] = small
        store = pltpu.make_async_copy(field.at[side], out_ref.at[:, :, lanes], sem.at[side])
        store.start()
        stores.append(store)

    x, number = chunk_of(cell_ref[...], span)
    gathered = gather(high, low, column_ref, jnp.where(number == 0, x, -1))
    gathered = [gathered_ref[k : k + 1, :] + v for k, v in enumerate(gathered)]

    group = max(capacity, LANES)
    together = group // capacity
    vertex_rows = -(-together * PARTS // 16) * 16
    chunk = lax.broadcasted_iota(jnp.int32, (1, group), 1) // capacity
    for s in range(0, slots // group):
        lanes = slice(s * group, (s + 1) * group)
        shape = [shape_ref[k : k + 1, lanes] for k in range(21)]
        terms = tet_terms(gathered[3][:, lanes], [gathered[k][:, lanes] for k in range(3)], shape)
        left, right = [], []
        for c in range(4):
            row = vertex_ref[c : c + 1, lanes] // LANES + chunk * PARTS
            match = lax.broadcasted_iota(jnp.int32, (vertex_rows, group), 0) == row
            blocks = []
            for k in range(3):
                blocks += split(jnp.where(match, terms[c][k], 0.0))
            left.append(jnp.concatenate(blocks, axis=0))
            right.append(vertex_hot_ref[c, :, lanes])
        product = lax.dot_general(
            jnp.concatenate(left, axis=1), jnp.concatenate(right, axis=1),
            (((1,), (1,)), ((), ())), preferred_element_type=F32,
        )
        for k in range(3):
            big = product[2 * k * vertex_rows : (2 * k + 1) * vertex_rows]
            small = product[(2 * k + 1) * vertex_rows : (2 * k + 2) * vertex_rows]
            total = big + small
            for q in range(together):
                owner = s * together + q
                sums[owner % 2, owner // 2, k * PARTS : (k + 1) * PARTS, :] = total[q * PARTS : (q + 1) * PARTS]
    core = lax.rem(lax.axis_index("blk"), 2)
    keep_ref[...] = sums[core]
    send_ref[...] = sums[1 - core]
    for store in stores:
        store.wait()


def fourth_kernel(keep_ref, got_ref, mine_ref, *refs):
    count = keep_ref.shape[0]
    me = lax.rem(lax.axis_index("blk") // 2, count)
    mine_ref[...] = keep_ref[me] + got_ref[me]
    for k, ref in enumerate(refs):
        partner = lax.bitwise_xor(me, k + 1)
        ref[...] = keep_ref[partner] + got_ref[partner]


def last_kernel(*refs):
    total = refs[0][...]
    for ref in refs[1:-1]:
        total = total + ref[...]
    for k in range(3):
        for part in range(PARTS):
            at = k * PARTS + part
            refs[-1][k : k + 1, part * LANES : (part + 1) * LANES] = total[at : at + 1, :]


def swap(value, axis, pairs):
    return lax.ppermute(value, axis, pairs + [(b, a) for a, b in pairs])


def neighbours(value_a, value_b, axis):
    count = lax.axis_size(axis)
    first = [(i, i + 1) for i in range(0, count - 1, 2)]
    second = [(i, i + 1) for i in range(1, count - 1, 2)]
    return swap(value_a, axis, first), swap(value_b, axis, second)


def local(
    adjoint_init, adjoint_rhs, flow_state, face_weights, pseudo_time,
    tet_coords, tet_weights, tet_cell, tet_vertex, tet_count,
):
    edge, span = pseudo_time.shape
    owners = tet_count.shape[1]
    blocks = lax.axis_size("blk")
    padded = (5, edge + 2 * ROWS, span + 2 * LANES)
    struct = jax.ShapeDtypeStruct
    packed = (16 * edge // LANES, edge, LANES)
    slots = tet_cell.shape[0]
    cell = tet_cell.reshape(1, slots)
    message = struct((16, span), F32)
    fields = (adjoint_init, adjoint_rhs, flow_state, face_weights, pseudo_time)
    xa, xb = call(
        plane_kernel,
        [message] * 2,
        [HBM] * 5,
        [VMEM] * 2,
        [pltpu.VMEM((5, 2 * ROWS, span), F32)] * 3
        + [pltpu.VMEM((6, edge, span), BF16), pltpu.VMEM((2 * ROWS, span), F32), pltpu.VMEM((2, 16, span), F32),
           pltpu.SemaphoreType.DMA((9,))],
        "plane_messages",
    )(*fields)
    ra, rb = neighbours(xa, xb, "grp")
    part, ylo, yhi, column, vertex_hot, shapes = call(
        first_kernel,
        [struct((5, edge, span), F32), struct(packed, F32), struct(packed, F32), struct((2 * LANES, slots), BF16),
         struct((4, LANES, slots), BF16), struct((24, slots), F32)],
        [VMEM] * 9 + [SMEM],
        [VMEM] * 6,
        [pltpu.VMEM(padded, F32), pltpu.VMEM((6, edge, span), F32)],
        "partial_sweep",
        flops=12_000_000,
    )(*fields, jnp.transpose(tet_coords, (1, 0, 2)), tet_weights, cell, tet_vertex, tet_count)
    res, ya, yb = call(
        second_kernel,
        [struct((2, 16, span), F32), struct(packed, F32), struct(packed, F32)],
        [VMEM] * 6,
        [VMEM] * 3,
        [pltpu.VMEM((2,) + packed, F32)],
        "streamwise_halo",
    )(xa, xb, ra, rb, ylo, yhi)
    sa, sb = neighbours(ya, yb, "blk")
    table = (4 * edge * (span // (2 * LANES) - 1), 2 * LANES)
    adjoint, gathered = call(
        middle_kernel,
        [struct((5, edge, span), F32), struct((4, slots), F32)],
        [VMEM] * 8,
        [HBM, VMEM],
        [pltpu.VMEM(padded, F32), pltpu.VMEM((5, edge, span - 2 * LANES), F32), pltpu.VMEM(table, BF16),
         pltpu.VMEM(table, BF16), pltpu.SemaphoreType.DMA],
        "middle_sweep",
        flops=12_000_000,
    )(part, *fields[1:], res, column, cell)
    half = owners // 2
    sums_shape = (half, 3 * PARTS, LANES)
    table = (4 * edge, 2 * LANES)
    adjoint, keep, send = call(
        third_kernel,
        [struct((5, edge, span), F32), struct(sums_shape, F32), struct(sums_shape, F32)],
        [HBM] + [VMEM] * 18,
        [HBM, VMEM, VMEM],
        [pltpu.VMEM((2, 5, edge + 2 * ROWS, 3 * LANES), F32), pltpu.VMEM((2, 5, edge, LANES), F32),
         pltpu.VMEM(table, BF16), pltpu.VMEM(table, BF16), pltpu.VMEM((2,) + sums_shape, F32),
         pltpu.SemaphoreType.DMA((2,))],
        "edge_sweep_and_sums",
        flops=12_000_000,
        aliases={0: 0},
    )(
        adjoint, part, *fields[1:], res, ra, rb, ya, yb, sa, sb,
        gathered, column, cell, tet_vertex, vertex_hot, shapes,
    )
    got = swap(send, "blk", [(i, i + 1) for i in range(0, blocks, 2)])
    place = lax.axis_index("blk") // 2
    while half > 4:
        half //= 2
        both = (keep + got).reshape(2, half, 3 * PARTS, LANES)
        bit = lax.rem(place // half, 2)
        keep = lax.dynamic_index_in_dim(both, bit, 0, keepdims=False)
        send = lax.dynamic_index_in_dim(both, 1 - bit, 0, keepdims=False)
        got = lax.ppermute(send, "blk", [(i, i ^ (2 * half)) for i in range(blocks)])
    one = struct((3 * PARTS, LANES), F32)
    mine, *others = call(
        fourth_kernel, [one] * half, [VMEM] * 2, [VMEM] * half, [], "core_pair_sums"
    )(keep, got)
    others = [
        lax.ppermute(v, "blk", [(i, i ^ (2 * (k + 1))) for i in range(blocks)]) for k, v in enumerate(others)
    ]
    sensitivity = call(
        last_kernel, struct((3, VERT_DEV), F32), [VMEM] * half, VMEM, [], "own_sums"
    )(mine, *others)
    return adjoint, sensitivity


def solution(mesh):
    return jax.shard_map(
        local,
        mesh=mesh,
        in_specs=(
            P(None, "grp", "blk"),
            P(None, "grp", "blk"),
            P(None, "grp", "blk"),
            P(None, "grp", "blk"),
            P("grp", "blk"),
            P(None, None, ("grp", "blk")),
            P(None, ("grp", "blk")),
            P(("grp", "blk")),
            P(None, ("grp", "blk")),
            P(("grp", "blk"), None),
        ),
        out_specs=(P(None, "grp", "blk"), P(None, ("grp", "blk"))),
        check_vma=False,
    )
```

time: 41.1 us -> 35.8 us (0.87)
  the two profiles are of different devices: /device:TPU:4 before, /device:TPU:2 now
where the time goes in v2:
time: 35.8 us; the launch traced here: 35.5 us
  starting transfers between devices  13.1 us (37%)
  Pallas kernels  10.5 us (29%)
  waiting for transfers between devices  5.79 us (16%)
  local copies, waits for them, and re-layouts  5.19 us (14%)
  between operations  0.85 us (2%)
    ppermute x5, starting transfers between devices, swap(): return lax.ppermute(value, axis, pairs + [(b, a) for a, b in pairs])  8.68 us
    unnamed x26, local copies, waits for them, and re-layouts  5.19 us
    ppermute x3, waiting for transfers between devices, local(): lax.ppermute(v, 'blk', [(i, i ^ 2 * (k + 1)) for i in range(blocks)])  4.86 us
    ppermute x3, starting transfers between devices, local(): lax.ppermute(v, 'blk', [(i, i ^ 2 * (k + 1)) for i in range(blocks)])  4.45 us
    pallas_call x1, Pallas kernels, local(): call(first_kernel, [struct((5, edge, span), F32), struct(packed, F32), st...  4.04 us
    pallas_call x1, Pallas kernels, local(): call(middle_kernel, [struct((5, edge, span), F32), struct((4, slots), F32...  2.74 us
    pallas_call x1, Pallas kernels, local(): call(third_kernel, [struct((5, edge, span), F32), struct(sums_shape, F32)...  1.87 us
    pallas_call x1, Pallas kernels, local(): call(plane_kernel, [message] * 2, [HBM] * 5, [VMEM] * 2, [pltpu.VMEM((5,...  1.04 us
  transfers between devices with their start and end apart: 8, of which 3 were waited for; matrix products, arithmetic and copies ran while one was open for 0% of the time, Pallas kernels for 19%

profile of v2, /device:TPU:2, one launch (start us, length us, event | category | flops | bytes accessed | tf_op | source)
XLA Modules:
  0.0 35.5 jit_solution(16278389533371904418)
XLA Ops:
  0.6 0.0 copy-start
  0.6 1.1 %copy-done = f32[5,32,1024]{2,1,0:T(8,128)S(1)} copy-done((f32[5,32,1024]{2,1,0:T(8,128)S(1)}, f32[5,32,1024]{2,1,0:T(8,128)}, u32[]{:S(2)}) %copy-start) | copy-done | bytes 655384
  1.7 1.1 %copy-done.2 = f32[5,32,1024]{2,1,0:T(8,128)S(1)} copy-done((f32[5,32,1024]{2,1,0:T(8,128)S(1)}, f32[5,32,1024]{2,1,0:T(8,128)}, u32[]{:S(2)}) %copy-start.2) | copy-done | bytes 655384
  2.8 1.0 %copy-done.4 = bf16[6,32,1024]{2,1,0:T(8,128)(2,1)S(1)} copy-done((bf16[6,32,1024]{2,1,0:T(8,128)(2,1)S(1)}, bf16[6,32,1024]{2,1,0:T(8,128)(2,1)}, u32[]{:S(2)}) %copy-start.4) | copy-done | bytes 393240
  3.8 1.1 %copy-done.6 = f32[5,32,1024]{2,1,0:T(8,128)S(1)} copy-done((f32[5,32,1024]{2,1,0:T(8,128)S(1)}, f32[5,32,1024]{2,1,0:T(8,128)}, u32[]{:S(2)}) %copy-start.6) | copy-done | bytes 655384
  4.9 0.9 %copy-done.7 = f32[32,1024]{1,0:T(8,128)S(1)} copy-done((f32[32,1024]{1,0:T(8,128)S(1)}, f32[32,1024]{1,0:T(8,128)}, u32[]{:S(2)}) %copy-start.7) | copy-done | bytes 131096
  5.8 0.0 copy-start.12
  5.8 1.0 %plane_messages.1 = (f32[16,1024]{1,0:T(8,128)S(1)}, f32[16,1024]{1,0:T(8,128)S(1)}) custom-call(f32[5,32,1024]{2,1,0:T(8,128)S(1)} %copy-done.6, f32[5,32,1024]{2,1,0:T(8,128)S(1)} %copy-done, f32[5,32,1024]{2,1,0:T(8,128)S(1)} %copy-done.2, bf16[6,32,1024]{2,1,0:T(8,128)(2,1)S(1)} %copy-done.4, f32[32,1024]{1,0:T(8,128)S(1)} %copy-done.7), custom_call_target="tpu_custom_call" | custom-call | flops 1000 | bytes 250 | tf_op jit(solution)/shard_map/plane_messages/pallas_call | solution.py:659
  6.9 0.0 copy-start.1
  6.9 0.0 copy-start.3
  6.9 0.0 copy-start.5
  6.9 0.1 collective-permute-start
  7.0 4.9 %collective-permute-start.1 = (f32[16,1024]{1,0:T(8,128)S(1)}, f32[16,1024]{1,0:T(8,128)S(1)}, u32[]{:S(2)}, u32[]{:S(2)}) collective-permute-start(f32[16,1024]{1,0:T(8,128)S(1)} %get-tuple-element.24.xb_ref), channel_id=1, source_target_pairs={{8,16},{16,8},{9,17},{17,9},{10,18},{18,10},{11,19},{19,11},{12,20... | collective-permute-start | bytes 196616 | tf_op jit(solution)/shard_map/ppermute | solution.py:635
  11.9 4.0 %partial_sweep.1 = (f32[5,32,1024]{2,1,0:T(8,128)S(1)}, f32[4,32,128]{2,1,0:T(8,128)S(1)}, f32[4,32,128]{2,1,0:T(8,128)S(1)}, bf16[256,2048]{1,0:T(8,128)(2,1)S(...) custom-call(f32[5,32,1024]{2,1,0:T(8,128)S(1)} %copy-done.6, f32[5,32,1024]{2,1,0:T(8,128)S(1)} %copy-done, ...), custom_call_target="tpu_custom_call" | custom-call | flops 12000000 | bytes 3000000 | tf_op jit(solution)/shard_map/partial_sweep/pallas_call | solution.py:670
  16.0 0.0 collective-permute-done.ra_ref
  16.0 0.0 collective-permute-done.1.rb_ref
  16.0 0.2 streamwise_halo.1
  16.2 0.1 collective-permute-start.2
  16.2 0.7 %collective-permute-start.3 = (f32[4,32,128]{2,1,0:T(8,128)S(1)}, f32[4,32,128]{2,1,0:T(8,128)S(1)}, u32[]{:S(2)}, u32[]{:S(2)}) collective-permute-start(f32[4,32,128]{2,1,0:T(8,128)S(1)} %get-tuple-element.31.yb_ref), channel_id=1, source_target_pairs={{1,2},{3,4},{5,6},{2,1},{4,3},{6,5},{9,10},{11,12},{13,14},{10,9},... | collective-permute-start | bytes 196616 | tf_op jit(solution)/shard_map/ppermute | solution.py:635
  16.9 2.7 %middle_sweep.1 = (f32[5,32,1024]{2,1,0:T(8,128)}, f32[4,2048]{1,0:T(4,128)S(1)}) custom-call(f32[5,32,1024]{2,1,0:T(8,128)S(1)} %get-tuple-element.22.part_ref, f32[5,32,1024]{2,1,0:T(8,128)S(1)} %copy-done.1, f32[5,32,1024]{2,1,0:T(8,128)S(1)} %copy-done.3, bf16[6,32,1024]{2,1,0:T(8,128)(2,1)S(1)} %copy-done.5, f32[32,1024]{1,0:T(8,128)S(1)} %copy-done.7, ...), custom_call_target="tpu_custom_call" | custom-call | flops 12000000 | bytes 3000000 | tf_op jit(solution)/shard_map/middle_sweep/pallas_call | solution.py:690
  19.7 0.0 collective-permute-done.2.sa_ref
  19.7 0.0 collective-permute-done.3.sb_ref
  19.7 1.9 %edge_sweep_and_sums.1 = (f32[5,32,1024]{2,1,0:T(8,128)}, f32[4,36,128]{2,1,0:T(8,128)S(1)}, f32[4,36,128]{2,1,0:T(8,128)S(1)}) custom-call(f32[5,32,1024]{2,1,0:T(8,128)} %get-tuple-element.29.adjoint_ref, f32[5,32,1024]{2,1,0:T(8,128)S(1)} %get-tuple-element.22.part_ref, f32[5,32,1024]{2,1,0:T(8,128)S(1)} %copy-done.1, ...), custom_call_target="tpu_custom_call", output_to_operand_aliasing={{0}: (0, {})} | custom-call | flops 12000000 | bytes 3000000 | tf_op jit(solution)/shard_map/edge_sweep_and_sums/pallas_call | solution.py:703
  21.6 3.0 %collective-permute-start.4 = (f32[4,36,128]{2,1,0:T(8,128)S(1)}, f32[4,36,128]{2,1,0:T(8,128)S(1)}, u32[]{:S(2)}, u32[]{:S(2)}) collective-permute-start(f32[4,36,128]{2,1,0:T(8,128)S(1)} %get-tuple-element.37), channel_id=1, source_target_pairs={{0,1},{2,3},{4,5},{6,7},{1,0},{3,2},{5,4},{7,6},{8,9},{10,11},{12,... | collective-permute-start | bytes 221192 | tf_op jit(solution)/shard_map/ppermute | solution.py:635
  24.6 0.9 %collective-permute-done.4.got_ref = f32[4,36,128]{2,1,0:T(8,128)S(1)} collective-permute-done((f32[4,36,128]{2,1,0:T(8,128)S(1)}, f32[4,36,128]{2,1,0:T(8,128)S(1)}, u32[]{:S(2)}, u32[]{:S(2)}) %collective-permute-start.4) | collective-permute-done | bytes 73760 | tf_op jit(solution)/shard_map/ppermute | solution.py:635
  25.5 1.6 %collective-permute-start.5 = (f32[36,128]{1,0:T(8,128)S(1)}, f32[36,128]{1,0:T(8,128)S(1)}, u32[]{:S(2)}, u32[]{:S(2)}) collective-permute-start(f32[36,128]{1,0:T(8,128)S(1)} %get-tuple-element.39), channel_id=1, source_target_pairs={{0,2},{1,3},{2,0},{3,1},{4,6},{5,7},{6,4},{7,5},{8,10},{9,11},{10,... | collective-permute-start | bytes 55304 | tf_op jit(solution)/shard_map/ppermute | solution.py:732
  27.2 2.1 %collective-permute-start.6 = (f32[36,128]{1,0:T(8,128)S(1)}, f32[36,128]{1,0:T(8,128)S(1)}, u32[]{:S(2)}, u32[]{:S(2)}) collective-permute-start(f32[36,128]{1,0:T(8,128)S(1)} %get-tuple-element.40), channel_id=1, source_target_pairs={{0,4},{1,5},{2,6},{3,7},{4,0},{5,1},{6,2},{7,3},{8,12},{9,13},{10,... | collective-permute-start | bytes 55304 | tf_op jit(solution)/shard_map/ppermute | solution.py:732
  29.3 0.7 %collective-permute-start.7 = (f32[36,128]{1,0:T(8,128)S(1)}, f32[36,128]{1,0:T(8,128)S(1)}, u32[]{:S(2)}, u32[]{:S(2)}) collective-permute-start(f32[36,128]{1,0:T(8,128)S(1)} %get-tuple-element.41), channel_id=1, source_target_pairs={{0,6},{1,7},{2,4},{3,5},{4,2},{5,3},{6,0},{7,1},{8,14},{9,15},{10,... | collective-permute-start | bytes 55304 | tf_op jit(solution)/shard_map/ppermute | solution.py:732
  30.0 0.0 collective-permute-done.5.refs_1_
  30.0 2.0 %collective-permute-done.6.refs_2_ = f32[36,128]{1,0:T(8,128)S(1)} collective-permute-done((f32[36,128]{1,0:T(8,128)S(1)}, f32[36,128]{1,0:T(8,128)S(1)}, u32[]{:S(2)}, u32[]{:S(2)}) %collective-permute-start.6) | collective-permute-done | bytes 18464 | tf_op jit(solution)/shard_map/ppermute | solution.py:732
  32.0 2.9 %collective-permute-done.7.refs_3_ = f32[36,128]{1,0:T(8,128)S(1)} collective-permute-done((f32[36,128]{1,0:T(8,128)S(1)}, f32[36,128]{1,0:T(8,128)S(1)}, u32[]{:S(2)}, u32[]{:S(2)}) %collective-permute-start.7) | collective-permute-done | bytes 18464 | tf_op jit(solution)/shard_map/ppermute | solution.py:732
  34.8 0.6 %own_sums.1 = f32[3,1536]{1,0:T(4,128)} custom-call(f32[36,128]{1,0:T(8,128)S(1)} %get-tuple-element.38.refs_0_, f32[36,128]{1,0:T(8,128)S(1)} %collective-permute-done.5.refs_1_, f32[36,128]{1,0:T(8,128)S(1)} %collective-permute-done.6.refs_2_, f32[36,128]{1,0:T(8,128)S(1)} %collective-permute-done.7.refs_3_), custom_call_target="tpu_custom_call" | custom-call | flops 1000 | bytes 250 | tf_op jit(solution)/shard_map/own_sums/pallas_call | solution.py:734
  (17 shorter events, 0.0 us)
Async XLA Ops:
  0.6 1.1 %copy-start = (f32[5,32,1024]{2,1,0:T(8,128)S(1)}, f32[5,32,1024]{2,1,0:T(8,128)}, u32[]{:S(2)}) copy-start(f32[5,32,1024]{2,1,0:T(8,128)} %rhs_ref.5) | copy-start | bytes 1966084
  1.7 1.1 %copy-start.2 = (f32[5,32,1024]{2,1,0:T(8,128)S(1)}, f32[5,32,1024]{2,1,0:T(8,128)}, u32[]{:S(2)}) copy-start(f32[5,32,1024]{2,1,0:T(8,128)} %state_ref.5) | copy-start | bytes 1966084
  2.8 1.0 %copy-start.4 = (bf16[6,32,1024]{2,1,0:T(8,128)(2,1)S(1)}, bf16[6,32,1024]{2,1,0:T(8,128)(2,1)}, u32[]{:S(2)}) copy-start(bf16[6,32,1024]{2,1,0:T(8,128)(2,1)} %face_ref.5) | copy-start | bytes 1179652
  3.8 1.1 %copy-start.6 = (f32[5,32,1024]{2,1,0:T(8,128)S(1)}, f32[5,32,1024]{2,1,0:T(8,128)}, u32[]{:S(2)}) copy-start(f32[5,32,1024]{2,1,0:T(8,128)} %adjoint_hbm.1) | copy-start | bytes 1966084
  4.9 0.9 %copy-start.7 = (f32[32,1024]{1,0:T(8,128)S(1)}, f32[32,1024]{1,0:T(8,128)}, u32[]{:S(2)}) copy-start(f32[32,1024]{1,0:T(8,128)} %pseudo_ref.5) | copy-start | bytes 393220
  5.8 6.1 %copy-start.8 = (s32[4,2048]{1,0:T(4,128)S(1)}, s32[4,2048]{1,0:T(4,128)}, u32[]{:S(2)}) copy-start(s32[4,2048]{1,0:T(4,128)} %vertex_ref.3) | copy-start | bytes 98308
  5.8 6.1 %copy-start.9 = (f32[4,3,2048]{2,0,1:T(4,128)S(1)}, f32[4,3,2048]{2,0,1:T(4,128)}, u32[]{:S(2)}) copy-start(f32[4,3,2048]{2,0,1:T(4,128)} %param.15) | copy-start | bytes 294916
  5.8 6.1 %copy-start.10 = (s32[2048]{0:T(1024)S(1)}, s32[2048]{0:T(1024)}, u32[]{:S(2)}) copy-start(s32[2048]{0:T(1024)} %param.17) | copy-start | bytes 24580
  5.8 6.1 %copy-start.11 = (f32[4,2048]{1,0:T(4,128)S(1)}, f32[4,2048]{1,0:T(4,128)}, u32[]{:S(2)}) copy-start(f32[4,2048]{1,0:T(4,128)} %weight_ref.1) | copy-start | bytes 98308
  5.8 6.1 %copy-start.12 = (s32[1,8]{1,0:T(1,128)S(1)}, s32[1,8]{1,0:T(1,128)}, u32[]{:S(2)}) copy-start(s32[1,8]{1,0:T(1,128)} %count_ref.1) | copy-start | bytes 100
  6.9 10.0 %copy-start.1 = (f32[5,32,1024]{2,1,0:T(8,128)S(1)}, f32[5,32,1024]{2,1,0:T(8,128)}, u32[]{:S(2)}) copy-start(f32[5,32,1024]{2,1,0:T(8,128)} %rhs_ref.5) | copy-start | bytes 1966084
  6.9 10.0 %copy-start.3 = (f32[5,32,1024]{2,1,0:T(8,128)S(1)}, f32[5,32,1024]{2,1,0:T(8,128)}, u32[]{:S(2)}) copy-start(f32[5,32,1024]{2,1,0:T(8,128)} %state_ref.5) | copy-start | bytes 1966084
  6.9 10.0 %copy-start.5 = (bf16[6,32,1024]{2,1,0:T(8,128)(2,1)S(1)}, bf16[6,32,1024]{2,1,0:T(8,128)(2,1)}, u32[]{:S(2)}) copy-start(bf16[6,32,1024]{2,1,0:T(8,128)(2,1)} %face_ref.5) | copy-start | bytes 1179652
  6.9 9.1 %collective-permute-start = (f32[16,1024]{1,0:T(8,128)S(1)}, f32[16,1024]{1,0:T(8,128)S(1)}, u32[]{:S(2)}, u32[]{:S(2)}) collective-permute-start(f32[16,1024]{1,0:T(8,128)S(1)} %get-tuple-element.23.xa_ref), channel_id=1, source_target_pairs={{0,8},{16,24},{8,0},{24,16},{1,9},{17,25},{9,1},{25,17},{2,10},{18... | collective-permute-start | bytes 196616 | tf_op jit(solution)/shard_map/ppermute | solution.py:635
  7.0 9.0 %collective-permute-start.1 = (f32[16,1024]{1,0:T(8,128)S(1)}, f32[16,1024]{1,0:T(8,128)S(1)}, u32[]{:S(2)}, u32[]{:S(2)}) collective-permute-start(f32[16,1024]{1,0:T(8,128)S(1)} %get-tuple-element.24.xb_ref), channel_id=1, source_target_pairs={{8,16},{16,8},{9,17},{17,9},{10,18},{18,10},{11,19},{19,11},{12,20... | collective-permute-start | bytes 196616 | tf_op jit(solution)/shard_map/ppermute | solution.py:635
  16.2 3.5 %collective-permute-start.2 = (f32[4,32,128]{2,1,0:T(8,128)S(1)}, f32[4,32,128]{2,1,0:T(8,128)S(1)}, u32[]{:S(2)}, u32[]{:S(2)}) collective-permute-start(f32[4,32,128]{2,1,0:T(8,128)S(1)} %get-tuple-element.30.ya_ref), channel_id=1, source_target_pairs={{0,1},{2,3},{4,5},{6,7},{1,0},{3,2},{5,4},{7,6},{8,9},{10,11},{12,... | collective-permute-start | bytes 196616 | tf_op jit(solution)/shard_map/ppermute | solution.py:635
  16.2 3.5 %collective-permute-start.3 = (f32[4,32,128]{2,1,0:T(8,128)S(1)}, f32[4,32,128]{2,1,0:T(8,128)S(1)}, u32[]{:S(2)}, u32[]{:S(2)}) collective-permute-start(f32[4,32,128]{2,1,0:T(8,128)S(1)} %get-tuple-element.31.yb_ref), channel_id=1, source_target_pairs={{1,2},{3,4},{5,6},{2,1},{4,3},{6,5},{9,10},{11,12},{13,14},{10,9},... | collective-permute-start | bytes 196616 | tf_op jit(solution)/shard_map/ppermute | solution.py:635
  21.6 3.9 %collective-permute-start.4 = (f32[4,36,128]{2,1,0:T(8,128)S(1)}, f32[4,36,128]{2,1,0:T(8,128)S(1)}, u32[]{:S(2)}, u32[]{:S(2)}) collective-permute-start(f32[4,36,128]{2,1,0:T(8,128)S(1)} %get-tuple-element.37), channel_id=1, source_target_pairs={{0,1},{2,3},{4,5},{6,7},{1,0},{3,2},{5,4},{7,6},{8,9},{10,11},{12,... | collective-permute-start | bytes 221192 | tf_op jit(solution)/shard_map/ppermute | solution.py:635
  25.5 4.5 %collective-permute-start.5 = (f32[36,128]{1,0:T(8,128)S(1)}, f32[36,128]{1,0:T(8,128)S(1)}, u32[]{:S(2)}, u32[]{:S(2)}) collective-permute-start(f32[36,128]{1,0:T(8,128)S(1)} %get-tuple-element.39), channel_id=1, source_target_pairs={{0,2},{1,3},{2,0},{3,1},{4,6},{5,7},{6,4},{7,5},{8,10},{9,11},{10,... | collective-permute-start | bytes 55304 | tf_op jit(solution)/shard_map/ppermute | solution.py:732
  27.2 4.8 %collective-permute-start.6 = (f32[36,128]{1,0:T(8,128)S(1)}, f32[36,128]{1,0:T(8,128)S(1)}, u32[]{:S(2)}, u32[]{:S(2)}) collective-permute-start(f32[36,128]{1,0:T(8,128)S(1)} %get-tuple-element.40), channel_id=1, source_target_pairs={{0,4},{1,5},{2,6},{3,7},{4,0},{5,1},{6,2},{7,3},{8,12},{9,13},{10,... | collective-permute-start | bytes 55304 | tf_op jit(solution)/shard_map/ppermute | solution.py:732
  29.3 5.6 %collective-permute-start.7 = (f32[36,128]{1,0:T(8,128)S(1)}, f32[36,128]{1,0:T(8,128)S(1)}, u32[]{:S(2)}, u32[]{:S(2)}) collective-permute-start(f32[36,128]{1,0:T(8,128)S(1)} %get-tuple-element.41), channel_id=1, source_target_pairs={{0,6},{1,7},{2,4},{3,5},{4,2},{5,3},{6,0},{7,1},{8,14},{9,15},{10,... | collective-permute-start | bytes 55304 | tf_op jit(solution)/shard_map/ppermute | solution.py:732

commit v3 on v2

--- a/solution.py
+++ b/solution.py
@@ -78,16 +78,29 @@
 
 def combine(rhs, reach, vel, speed_sq, enthalpy, faces, pairs):
     spread = None
-    total = None
+    scaled = None
     for axis_id, (upper, lower) in enumerate(pairs):
         upper = [faces[2 * axis_id] * v for v in upper]
         lower = [faces[2 * axis_id + 1] * v for v in lower]
         both = [u + v for u, v in zip(upper, lower)]
-        difference = [u - v for u, v in zip(upper, lower)]
+        field = [u - v for u, v in zip(upper, lower)]
         spread = both if spread is None else [u + v for u, v in zip(spread, both)]
-        turned = transposed(vel, enthalpy, 0.5 * (GAMMA - 1.0) * speed_sq, axis_id, difference)
-        total = turned if total is None else [u + v for u, v in zip(total, turned)]
-    return [rhs[k] + total[k] + reach * spread[k] for k in range(5)]
+        normal = vel[axis_id]
+        energy = normal * field[4]
+        common = vel[0] * field[1] + vel[1] * field[2] + vel[2] * field[3] + enthalpy * field[4]
+        along = field[1 + axis_id] + energy
+        parts = [normal * common] + [normal * field[1 + j] for j in range(3)] + [energy]
+        parts[1 + axis_id] = parts[1 + axis_id] + (field[0] + common)
+        if scaled is None:
+            scaled, total = along, parts
+        else:
+            scaled = scaled + along
+            total = [u + v for u, v in zip(total, parts)]
+    scaled = (GAMMA - 1.0) * scaled
+    turned = [0.5 * speed_sq * scaled - total[0]]
+    turned += [total[1 + j] - vel[j] * scaled for j in range(3)]
+    turned.append(scaled + total[4])
+    return [rhs[k] + turned[k] + reach * spread[k] for k in range(5)]
 
 
 def inside_faces(faces, edge, shape):
@@ -157,31 +170,40 @@
             body(top, pl.multiple_of(j * LANES, LANES))
             return carry
 
-        lax.fori_loop(first, last, step, 0)
+        lax.fori_loop(first, last, step, 0, unroll=True)
 
 
 def plane_kernel(
-    adjoint_hbm, rhs_hbm, state_hbm, face_hbm, pseudo_hbm,
-    xa_ref, xb_ref,
-    adjoint_ref, rhs_ref, state_ref, face_ref, pseudo_ref, xsides, sem,
+    adjoint_hbm, rhs_hbm, state_hbm, face_hbm, pseudo_hbm, coord_hbm, weight_hbm, cell_hbm, vertex_hbm,
+    xa_ref, xb_ref, adjoint_ref, rhs_ref, state_ref, face_ref, pseudo_ref, coord_ref, weight_ref, cell_ref,
+    vertex_ref,
+    xsides, sem,
 ):
     edge, span = pseudo_hbm.shape
-    copies = [pltpu.make_async_copy(face_hbm, face_ref, sem.at[0])]
+    early, late = [], []
+
+    def move(into, source, target):
+        into.append(pltpu.make_async_copy(source, target, sem.at[len(early) + len(late)]))
+        into[-1].start()
+
+    fields = (
+        (state_hbm, state_ref), (adjoint_hbm, adjoint_ref), (rhs_hbm, rhs_ref), (pseudo_hbm, pseudo_ref)
+    )
+
+    def rows_of(ref, first, count):
+        return ref.at[(slice(None),) * (len(ref.shape) - 2) + (pl.ds(first, count),)]
+
+    move(early, face_hbm, face_ref)
+    for source, target in fields:
+        for first in (0, edge - ROWS):
+            move(early, rows_of(source, first, ROWS), rows_of(target, first, ROWS))
+    for source, target in fields:
+        move(late, rows_of(source, ROWS, edge - 2 * ROWS), rows_of(target, ROWS, edge - 2 * ROWS))
     for source, target in (
-        (state_hbm, state_ref), (adjoint_hbm, adjoint_ref), (rhs_hbm, rhs_ref), (pseudo_hbm, pseudo_ref)
+        (coord_hbm, coord_ref), (weight_hbm, weight_ref), (cell_hbm, cell_ref), (vertex_hbm, vertex_ref)
     ):
-        for side in (0, 1):
-            there = pl.ds(side * (edge - ROWS), ROWS)
-            here = pl.ds(side * ROWS, ROWS)
-            whole = (slice(None),) * (len(source.shape) - 2)
-            copies.append(
-                pltpu.make_async_copy(
-                    source.at[whole + (there,)], target.at[whole + (here,)], sem.at[len(copies)]
-                )
-            )
-    for copy in copies:
-        copy.start()
-    for copy in copies:
+        move(late, source, target)
+    for copy in early:
         copy.wait()
     even = is_even("grp")
     shape = (2, LANES)
@@ -194,7 +216,7 @@
     def planes(ref, k, j, inner=0):
         at = (k,) if k is not None else ()
         lanes = slice(j * LANES, (j + 1) * LANES)
-        last = 2 * ROWS - 2 - inner
+        last = edge - 2 - inner
         return jnp.where(upper_row, ref[at + (slice(last, last + 2), lanes)], ref[at + (slice(inner, inner + 2), lanes)])
 
     for j in range(tiles):
@@ -227,6 +249,8 @@
                 xsides[slot, k : k + 1, lanes] = value[side : side + 1]
     xa_ref[...] = xsides[0]
     xb_ref[...] = xsides[1]
+    for copy in late:
+        copy.wait()
 
 
 def first_kernel(
@@ -408,8 +432,8 @@
 
 
 def hot(shape, index):
-    rows = lax.broadcasted_iota(jnp.int32, shape, 0)
-    return jnp.where(rows == index, 1.0, 0.0).astype(BF16)
+    rows = lax.broadcasted_iota(jnp.int16, shape, 0)
+    return jnp.where(rows == index.astype(jnp.int16), jnp.ones((), BF16), jnp.zeros((), BF16))
 
 
 def gather(high, low, column_ref, row):
@@ -588,10 +612,10 @@
         left, right = [], []
         for c in range(4):
             row = vertex_ref[c : c + 1, lanes] // LANES + chunk * PARTS
-            match = lax.broadcasted_iota(jnp.int32, (vertex_rows, group), 0) == row
+            match = lax.broadcasted_iota(jnp.int16, (vertex_rows, group), 0) == row.astype(jnp.int16)
             blocks = []
             for k in range(3):
-                blocks += split(jnp.where(match, terms[c][k], 0.0))
+                blocks += [jnp.where(match, v, jnp.zeros((), BF16)) for v in split(terms[c][k])]
             left.append(jnp.concatenate(blocks, axis=0))
             right.append(vertex_hot_ref[c, :, lanes])
         product = lax.dot_general(
@@ -656,16 +680,16 @@
     cell = tet_cell.reshape(1, slots)
     message = struct((16, span), F32)
     fields = (adjoint_init, adjoint_rhs, flow_state, face_weights, pseudo_time)
-    xa, xb = call(
+    arrays = (*fields, jnp.transpose(tet_coords, (1, 0, 2)), tet_weights, cell, tet_vertex)
+    xa, xb, *arrays = call(
         plane_kernel,
-        [message] * 2,
-        [HBM] * 5,
-        [VMEM] * 2,
-        [pltpu.VMEM((5, 2 * ROWS, span), F32)] * 3
-        + [pltpu.VMEM((6, edge, span), BF16), pltpu.VMEM((2 * ROWS, span), F32), pltpu.VMEM((2, 16, span), F32),
-           pltpu.SemaphoreType.DMA((9,))],
+        [message] * 2 + [struct(v.shape, v.dtype) for v in arrays],
+        [HBM] * 9,
+        [VMEM] * 11,
+        [pltpu.VMEM((2, 16, span), F32), pltpu.SemaphoreType.DMA((17,))],
         "plane_messages",
-    )(*fields)
+    )(*(pltpu.with_memory_space_constraint(v, pltpu.HBM) for v in arrays))
+    fields, (coords, weights, cell, vertex) = arrays[:5], arrays[5:]
     ra, rb = neighbours(xa, xb, "grp")
     part, ylo, yhi, column, vertex_hot, shapes = call(
         first_kernel,
@@ -676,7 +700,7 @@
         [pltpu.VMEM(padded, F32), pltpu.VMEM((6, edge, span), F32)],
         "partial_sweep",
         flops=12_000_000,
-    )(*fields, jnp.transpose(tet_coords, (1, 0, 2)), tet_weights, cell, tet_vertex, tet_count)
+    )(*fields, coords, weights, cell, vertex, tet_count)
     res, ya, yb = call(
         second_kernel,
         [struct((2, 16, span), F32), struct(packed, F32), struct(packed, F32)],
@@ -713,7 +737,7 @@
         aliases={0: 0},
     )(
         adjoint, part, *fields[1:], res, ra, rb, ya, yb, sa, sb,
-        gathered, column, cell, tet_vertex, vertex_hot, shapes,
+        gathered, column, cell, vertex, vertex_hot, shapes,
     )
     got = swap(send, "blk", [(i, i + 1) for i in range(0, blocks, 2)])
     place = lax.axis_index("blk") // 2

time: 35.8 us -> 30.8 us (0.86)
  the two profiles are of different devices: /device:TPU:2 before, /device:TPU:4 now
where the time goes in v3:
time: 30.8 us; the launch traced here: 30.6 us
  starting transfers between devices  12 us (39%)
  Pallas kernels  9.01 us (29%)
  waiting for transfers between devices  8.88 us (29%)
  between operations  0.74 us (2%)
    ppermute x5, starting transfers between devices, swap(): return lax.ppermute(value, axis, pairs + [(b, a) for a, b in pairs])  7.55 us
    ppermute x3, waiting for transfers between devices, local(): lax.ppermute(v, 'blk', [(i, i ^ 2 * (k + 1)) for i in range(blocks)])  5.23 us
    ppermute x3, starting transfers between devices, local(): lax.ppermute(v, 'blk', [(i, i ^ 2 * (k + 1)) for i in range(blocks)])  4.45 us
    ppermute x5, waiting for transfers between devices, swap(): return lax.ppermute(value, axis, pairs + [(b, a) for a, b in pairs])  3.65 us
    pallas_call x1, Pallas kernels, local(): call(first_kernel, [struct((5, edge, span), F32), struct(packed, F32), st...  2.38 us
    pallas_call x1, Pallas kernels, local(): call(middle_kernel, [struct((5, edge, span), F32), struct((4, slots), F32...  2.07 us
    pallas_call x1, Pallas kernels, local(): call(plane_kernel, [message] * 2 + [struct(v.shape, v.dtype) for v in arr...  1.91 us
    pallas_call x1, Pallas kernels, local(): call(third_kernel, [struct((5, edge, span), F32), struct(sums_shape, F32)...  1.84 us
  transfers between devices with their start and end apart: 8, of which 4 were waited for; matrix products, arithmetic and copies ran while one was open for 0% of the time, Pallas kernels for 15%

profile of v3, /device:TPU:4, one launch (start us, length us, event | category | flops | bytes accessed | tf_op | source)
XLA Modules:
  0.0 30.6 jit_solution(8906941411772456005)
XLA Ops:
  0.6 0.0 copy-start
  0.6 1.9 %plane_messages.1 = (f32[16,1024]{1,0:T(8,128)S(1)}, f32[16,1024]{1,0:T(8,128)S(1)}, f32[5,32,1024]{2,1,0:T(8,128)S(1)}, f32[5,32,1024]{2,1,0:T(8,128)S(1)}, f32...) custom-call(f32[5,32,1024]{2,1,0:T(8,128)} %adjoint_hbm.1, ...), custom_call_target="tpu_custom_call" | custom-call | flops 1000 | bytes 250 | tf_op jit(solution)/shard_map/plane_messages/pallas_call | solution.py:684
  2.6 1.6 %collective-permute-start = (f32[16,1024]{1,0:T(8,128)S(1)}, f32[16,1024]{1,0:T(8,128)S(1)}, u32[]{:S(2)}, u32[]{:S(2)}) collective-permute-start(f32[16,1024]{1,0:T(8,128)S(1)} %get-tuple-element.41.xa_ref), channel_id=1, source_target_pairs={{0,8},{16,24},{8,0},{24,16},{1,9},{17,25},{9,1},{25,17},{2,10},{18... | collective-permute-start | bytes 196616 | tf_op jit(solution)/shard_map/ppermute | solution.py:659
  4.1 1.9 %collective-permute-start.1 = (f32[16,1024]{1,0:T(8,128)S(1)}, f32[16,1024]{1,0:T(8,128)S(1)}, u32[]{:S(2)}, u32[]{:S(2)}) collective-permute-start(f32[16,1024]{1,0:T(8,128)S(1)} %get-tuple-element.42.xb_ref), channel_id=1, source_target_pairs={{8,16},{16,8},{9,17},{17,9},{10,18},{18,10},{11,19},{19,11},{12,20... | collective-permute-start | bytes 196616 | tf_op jit(solution)/shard_map/ppermute | solution.py:659
  6.0 0.0 copy-done
  6.0 2.4 %partial_sweep.1 = (f32[5,32,1024]{2,1,0:T(8,128)S(1)}, f32[4,32,128]{2,1,0:T(8,128)S(1)}, f32[4,32,128]{2,1,0:T(8,128)S(1)}, bf16[256,2048]{1,0:T(8,128)(2,1)S(...) custom-call(f32[5,32,1024]{2,1,0:T(8,128)S(1)} %get-tuple-element.31.adjoint_ref, ...), custom_call_target="tpu_custom_call" | custom-call | flops 12000000 | bytes 3000000 | tf_op jit(solution)/shard_map/partial_sweep/pallas_call | solution.py:694
  8.4 0.0 collective-permute-done.ra_ref
  8.4 2.7 %collective-permute-done.1.rb_ref = f32[16,1024]{1,0:T(8,128)S(1)} collective-permute-done((f32[16,1024]{1,0:T(8,128)S(1)}, f32[16,1024]{1,0:T(8,128)S(1)}, u32[]{:S(2)}, u32[]{:S(2)}) %collective-permute-start.1) | collective-permute-done | bytes 65568 | tf_op jit(solution)/shard_map/ppermute | solution.py:659
  11.2 0.2 streamwise_halo.1
  11.3 0.1 collective-permute-start.2
  11.4 0.7 %collective-permute-start.3 = (f32[4,32,128]{2,1,0:T(8,128)S(1)}, f32[4,32,128]{2,1,0:T(8,128)S(1)}, u32[]{:S(2)}, u32[]{:S(2)}) collective-permute-start(f32[4,32,128]{2,1,0:T(8,128)S(1)} %get-tuple-element.49.yb_ref), channel_id=1, source_target_pairs={{1,2},{3,4},{5,6},{2,1},{4,3},{6,5},{9,10},{11,12},{13,14},{10,9},... | collective-permute-start | bytes 196616 | tf_op jit(solution)/shard_map/ppermute | solution.py:659
  12.1 2.1 %middle_sweep.1 = (f32[5,32,1024]{2,1,0:T(8,128)}, f32[4,2048]{1,0:T(4,128)S(1)}) custom-call(f32[5,32,1024]{2,1,0:T(8,128)S(1)} %get-tuple-element.40.part_ref, f32[5,32,1024]{2,1,0:T(8,128)S(1)} %get-tuple-element.32.rhs_ref, f32[5,32,1024]{2,1,0:T(8,128)S(1)} %get-tuple-element.33.state_ref, bf16[6,32,1024]{2,1,0:T(8,128)(2,1)S(1)} %get-tuple-element.34.face_ref, ...), custom_call_target="tpu_custom_call" | custom-call | flops 12000000 | bytes 3000000 | tf_op jit(solution)/shard_map/middle_sweep/pallas_call | solution.py:714
  14.2 0.0 collective-permute-done.2.sa_ref
  14.2 0.0 collective-permute-done.3.sb_ref
  14.2 1.8 %edge_sweep_and_sums.1 = (f32[5,32,1024]{2,1,0:T(8,128)}, f32[4,36,128]{2,1,0:T(8,128)S(1)}, f32[4,36,128]{2,1,0:T(8,128)S(1)}) custom-call(f32[5,32,1024]{2,1,0:T(8,128)} %get-tuple-element.47.adjoint_ref, f32[5,32,1024]{2,1,0:T(8,128)S(1)} %get-tuple-element.40.part_ref, ...), custom_call_target="tpu_custom_call", output_to_operand_aliasing={{0}: (0, {})} | custom-call | flops 12000000 | bytes 3000000 | tf_op jit(solution)/shard_map/edge_sweep_and_sums/pallas_call | solution.py:727
  16.0 3.4 %collective-permute-start.4 = (f32[4,36,128]{2,1,0:T(8,128)S(1)}, f32[4,36,128]{2,1,0:T(8,128)S(1)}, u32[]{:S(2)}, u32[]{:S(2)}) collective-permute-start(f32[4,36,128]{2,1,0:T(8,128)S(1)} %get-tuple-element.55), channel_id=1, source_target_pairs={{0,1},{2,3},{4,5},{6,7},{1,0},{3,2},{5,4},{7,6},{8,9},{10,11},{12,... | collective-permute-start | bytes 221192 | tf_op jit(solution)/shard_map/ppermute | solution.py:659
  19.4 0.9 %collective-permute-done.4.got_ref = f32[4,36,128]{2,1,0:T(8,128)S(1)} collective-permute-done((f32[4,36,128]{2,1,0:T(8,128)S(1)}, f32[4,36,128]{2,1,0:T(8,128)S(1)}, u32[]{:S(2)}, u32[]{:S(2)}) %collective-permute-start.4) | collective-permute-done | bytes 73760 | tf_op jit(solution)/shard_map/ppermute | solution.py:659
  20.3 1.6 %collective-permute-start.5 = (f32[36,128]{1,0:T(8,128)S(1)}, f32[36,128]{1,0:T(8,128)S(1)}, u32[]{:S(2)}, u32[]{:S(2)}) collective-permute-start(f32[36,128]{1,0:T(8,128)S(1)} %get-tuple-element.57), channel_id=1, source_target_pairs={{0,2},{1,3},{2,0},{3,1},{4,6},{5,7},{6,4},{7,5},{8,10},{9,11},{10,... | collective-permute-start | bytes 55304 | tf_op jit(solution)/shard_map/ppermute | solution.py:756
  22.0 2.5 %collective-permute-start.6 = (f32[36,128]{1,0:T(8,128)S(1)}, f32[36,128]{1,0:T(8,128)S(1)}, u32[]{:S(2)}, u32[]{:S(2)}) collective-permute-start(f32[36,128]{1,0:T(8,128)S(1)} %get-tuple-element.58), channel_id=1, source_target_pairs={{0,4},{1,5},{2,6},{3,7},{4,0},{5,1},{6,2},{7,3},{8,12},{9,13},{10,... | collective-permute-start | bytes 55304 | tf_op jit(solution)/shard_map/ppermute | solution.py:756
  24.4 0.4 %collective-permute-start.7 = (f32[36,128]{1,0:T(8,128)S(1)}, f32[36,128]{1,0:T(8,128)S(1)}, u32[]{:S(2)}, u32[]{:S(2)}) collective-permute-start(f32[36,128]{1,0:T(8,128)S(1)} %get-tuple-element.59), channel_id=1, source_target_pairs={{0,6},{1,7},{2,4},{3,5},{4,2},{5,3},{6,0},{7,1},{8,14},{9,15},{10,... | collective-permute-start | bytes 55304 | tf_op jit(solution)/shard_map/ppermute | solution.py:756
  24.8 0.0 collective-permute-done.5.refs_1_
  24.8 2.0 %collective-permute-done.6.refs_2_ = f32[36,128]{1,0:T(8,128)S(1)} collective-permute-done((f32[36,128]{1,0:T(8,128)S(1)}, f32[36,128]{1,0:T(8,128)S(1)}, u32[]{:S(2)}, u32[]{:S(2)}) %collective-permute-start.6) | collective-permute-done | bytes 18464 | tf_op jit(solution)/shard_map/ppermute | solution.py:756
  26.8 3.3 %collective-permute-done.7.refs_3_ = f32[36,128]{1,0:T(8,128)S(1)} collective-permute-done((f32[36,128]{1,0:T(8,128)S(1)}, f32[36,128]{1,0:T(8,128)S(1)}, u32[]{:S(2)}, u32[]{:S(2)}) %collective-permute-start.7) | collective-permute-done | bytes 18464 | tf_op jit(solution)/shard_map/ppermute | solution.py:756
  30.0 0.6 %own_sums.1 = f32[3,1536]{1,0:T(4,128)} custom-call(f32[36,128]{1,0:T(8,128)S(1)} %get-tuple-element.56.refs_0_, f32[36,128]{1,0:T(8,128)S(1)} %collective-permute-done.5.refs_1_, f32[36,128]{1,0:T(8,128)S(1)} %collective-permute-done.6.refs_2_, f32[36,128]{1,0:T(8,128)S(1)} %collective-permute-done.7.refs_3_), custom_call_target="tpu_custom_call" | custom-call | flops 1000 | bytes 250 | tf_op jit(solution)/shard_map/own_sums/pallas_call | solution.py:758
  (1 shorter events, 0.0 us)
Async XLA Ops:
  0.6 5.4 %copy-start = (s32[1,8]{1,0:T(1,128)S(1)}, s32[1,8]{1,0:T(1,128)}, u32[]{:S(2)}) copy-start(s32[1,8]{1,0:T(1,128)} %count_ref.1) | copy-start | bytes 100
  2.6 5.9 %collective-permute-start = (f32[16,1024]{1,0:T(8,128)S(1)}, f32[16,1024]{1,0:T(8,128)S(1)}, u32[]{:S(2)}, u32[]{:S(2)}) collective-permute-start(f32[16,1024]{1,0:T(8,128)S(1)} %get-tuple-element.41.xa_ref), channel_id=1, source_target_pairs={{0,8},{16,24},{8,0},{24,16},{1,9},{17,25},{9,1},{25,17},{2,10},{18... | collective-permute-start | bytes 196616 | tf_op jit(solution)/shard_map/ppermute | solution.py:659
  4.1 7.0 %collective-permute-start.1 = (f32[16,1024]{1,0:T(8,128)S(1)}, f32[16,1024]{1,0:T(8,128)S(1)}, u32[]{:S(2)}, u32[]{:S(2)}) collective-permute-start(f32[16,1024]{1,0:T(8,128)S(1)} %get-tuple-element.42.xb_ref), channel_id=1, source_target_pairs={{8,16},{16,8},{9,17},{17,9},{10,18},{18,10},{11,19},{19,11},{12,20... | collective-permute-start | bytes 196616 | tf_op jit(solution)/shard_map/ppermute | solution.py:659
  11.3 2.8 %collective-permute-start.2 = (f32[4,32,128]{2,1,0:T(8,128)S(1)}, f32[4,32,128]{2,1,0:T(8,128)S(1)}, u32[]{:S(2)}, u32[]{:S(2)}) collective-permute-start(f32[4,32,128]{2,1,0:T(8,128)S(1)} %get-tuple-element.48.ya_ref), channel_id=1, source_target_pairs={{0,1},{2,3},{4,5},{6,7},{1,0},{3,2},{5,4},{7,6},{8,9},{10,11},{12,... | collective-permute-start | bytes 196616 | tf_op jit(solution)/shard_map/ppermute | solution.py:659
  11.4 2.8 %collective-permute-start.3 = (f32[4,32,128]{2,1,0:T(8,128)S(1)}, f32[4,32,128]{2,1,0:T(8,128)S(1)}, u32[]{:S(2)}, u32[]{:S(2)}) collective-permute-start(f32[4,32,128]{2,1,0:T(8,128)S(1)} %get-tuple-element.49.yb_ref), channel_id=1, source_target_pairs={{1,2},{3,4},{5,6},{2,1},{4,3},{6,5},{9,10},{11,12},{13,14},{10,9},... | collective-permute-start | bytes 196616 | tf_op jit(solution)/shard_map/ppermute | solution.py:659
  16.0 4.3 %collective-permute-start.4 = (f32[4,36,128]{2,1,0:T(8,128)S(1)}, f32[4,36,128]{2,1,0:T(8,128)S(1)}, u32[]{:S(2)}, u32[]{:S(2)}) collective-permute-start(f32[4,36,128]{2,1,0:T(8,128)S(1)} %get-tuple-element.55), channel_id=1, source_target_pairs={{0,1},{2,3},{4,5},{6,7},{1,0},{3,2},{5,4},{7,6},{8,9},{10,11},{12,... | collective-permute-start | bytes 221192 | tf_op jit(solution)/shard_map/ppermute | solution.py:659
  20.3 4.5 %collective-permute-start.5 = (f32[36,128]{1,0:T(8,128)S(1)}, f32[36,128]{1,0:T(8,128)S(1)}, u32[]{:S(2)}, u32[]{:S(2)}) collective-permute-start(f32[36,128]{1,0:T(8,128)S(1)} %get-tuple-element.57), channel_id=1, source_target_pairs={{0,2},{1,3},{2,0},{3,1},{4,6},{5,7},{6,4},{7,5},{8,10},{9,11},{10,... | collective-permute-start | bytes 55304 | tf_op jit(solution)/shard_map/ppermute | solution.py:756
  22.0 4.8 %collective-permute-start.6 = (f32[36,128]{1,0:T(8,128)S(1)}, f32[36,128]{1,0:T(8,128)S(1)}, u32[]{:S(2)}, u32[]{:S(2)}) collective-permute-start(f32[36,128]{1,0:T(8,128)S(1)} %get-tuple-element.58), channel_id=1, source_target_pairs={{0,4},{1,5},{2,6},{3,7},{4,0},{5,1},{6,2},{7,3},{8,12},{9,13},{10,... | collective-permute-start | bytes 55304 | tf_op jit(solution)/shard_map/ppermute | solution.py:756
  24.4 5.6 %collective-permute-start.7 = (f32[36,128]{1,0:T(8,128)S(1)}, f32[36,128]{1,0:T(8,128)S(1)}, u32[]{:S(2)}, u32[]{:S(2)}) collective-permute-start(f32[36,128]{1,0:T(8,128)S(1)} %get-tuple-element.59), channel_id=1, source_target_pairs={{0,6},{1,7},{2,4},{3,5},{4,2},{5,3},{6,0},{7,1},{8,14},{9,15},{10,... | collective-permute-start | bytes 55304 | tf_op jit(solution)/shard_map/ppermute | solution.py:756

commit v4 on v3

--- a/solution.py
+++ b/solution.py
@@ -630,18 +630,17 @@
                 owner = s * together + q
                 sums[owner % 2, owner // 2, k * PARTS : (k + 1) * PARTS, :] = total[q * PARTS : (q + 1) * PARTS]
     core = lax.rem(lax.axis_index("blk"), 2)
-    keep_ref[...] = sums[core]
-    send_ref[...] = sums[1 - core]
+    keep_ref[...] = sums[1 - core]
+    send_ref[...] = sums[core]
     for store in stores:
         store.wait()
 
 
-def fourth_kernel(keep_ref, got_ref, mine_ref, *refs):
+def fourth_kernel(keep_ref, got_ref, *refs):
     count = keep_ref.shape[0]
     me = lax.rem(lax.axis_index("blk") // 2, count)
-    mine_ref[...] = keep_ref[me] + got_ref[me]
     for k, ref in enumerate(refs):
-        partner = lax.bitwise_xor(me, k + 1)
+        partner = lax.bitwise_xor(me, k)
         ref[...] = keep_ref[partner] + got_ref[partner]
 
 
@@ -749,15 +748,11 @@
         send = lax.dynamic_index_in_dim(both, 1 - bit, 0, keepdims=False)
         got = lax.ppermute(send, "blk", [(i, i ^ (2 * half)) for i in range(blocks)])
     one = struct((3 * PARTS, LANES), F32)
-    mine, *others = call(
+    parts = call(
         fourth_kernel, [one] * half, [VMEM] * 2, [VMEM] * half, [], "core_pair_sums"
     )(keep, got)
-    others = [
-        lax.ppermute(v, "blk", [(i, i ^ (2 * (k + 1))) for i in range(blocks)]) for k, v in enumerate(others)
-    ]
-    sensitivity = call(
-        last_kernel, struct((3, VERT_DEV), F32), [VMEM] * half, VMEM, [], "own_sums"
-    )(mine, *others)
+    parts = [lax.ppermute(v, "blk", [(i, i ^ (2 * k + 1)) for i in range(blocks)]) for k, v in enumerate(parts)]
+    sensitivity = call(last_kernel, struct((3, VERT_DEV), F32), [VMEM] * half, VMEM, [], "own_sums")(*parts)
     return adjoint, sensitivity
 
 

time: 30.8 us -> 30.6 us (level)
  the two profiles are of different devices: /device:TPU:4 before, /device:TPU:5 now
where the time goes in v4:
time: 30.6 us; the launch traced here: 30.5 us
  starting transfers between devices  12.8 us (42%)
  Pallas kernels  8.99 us (29%)
  waiting for transfers between devices  7.91 us (26%)
  between operations  0.73 us (2%)
    ppermute x5, starting transfers between devices, swap(): return lax.ppermute(value, axis, pairs + [(b, a) for a, b in pairs])  8.52 us
    ppermute x4, waiting for transfers between devices, local(): lax.ppermute(v, 'blk', [(i, i ^ 2 * k + 1) for i in range(blocks)])  4.7 us
    ppermute x4, starting transfers between devices, local(): lax.ppermute(v, 'blk', [(i, i ^ 2 * k + 1) for i in range(blocks)])  4.29 us
    ppermute x5, waiting for transfers between devices, swap(): return lax.ppermute(value, axis, pairs + [(b, a) for a, b in pairs])  3.21 us
    pallas_call x1, Pallas kernels, local(): call(first_kernel, [struct((5, edge, span), F32), struct(packed, F32), st...  2.38 us
    pallas_call x1, Pallas kernels, local(): call(middle_kernel, [struct((5, edge, span), F32), struct((4, slots), F32...  2.07 us
    pallas_call x1, Pallas kernels, local(): call(plane_kernel, [message] * 2 + [struct(v.shape, v.dtype) for v in arr...  1.91 us
    pallas_call x1, Pallas kernels, local(): call(third_kernel, [struct((5, edge, span), F32), struct(sums_shape, F32)...  1.82 us
  transfers between devices with their start and end apart: 9, of which 5 were waited for; matrix products, arithmetic and copies ran while one was open for 0% of the time, Pallas kernels for 15%

profile of v4, /device:TPU:5, one launch (start us, length us, event | category | flops | bytes accessed | tf_op | source)
XLA Modules:
  0.0 30.5 jit_solution(4059586987105342075)
XLA Ops:
  0.6 0.0 copy-start
  0.6 1.9 %plane_messages.1 = (f32[16,1024]{1,0:T(8,128)S(1)}, f32[16,1024]{1,0:T(8,128)S(1)}, f32[5,32,1024]{2,1,0:T(8,128)S(1)}, f32[5,32,1024]{2,1,0:T(8,128)S(1)}, f32...) custom-call(f32[5,32,1024]{2,1,0:T(8,128)} %adjoint_hbm.1, ...), custom_call_target="tpu_custom_call" | custom-call | flops 1000 | bytes 250 | tf_op jit(solution)/shard_map/plane_messages/pallas_call | solution.py:683
  2.6 1.3 %collective-permute-start = (f32[16,1024]{1,0:T(8,128)S(1)}, f32[16,1024]{1,0:T(8,128)S(1)}, u32[]{:S(2)}, u32[]{:S(2)}) collective-permute-start(f32[16,1024]{1,0:T(8,128)S(1)} %get-tuple-element.41.xa_ref), channel_id=1, source_target_pairs={{0,8},{16,24},{8,0},{24,16},{1,9},{17,25},{9,1},{25,17},{2,10},{18... | collective-permute-start | bytes 196616 | tf_op jit(solution)/shard_map/ppermute | solution.py:658
  3.8 1.9 %collective-permute-start.1 = (f32[16,1024]{1,0:T(8,128)S(1)}, f32[16,1024]{1,0:T(8,128)S(1)}, u32[]{:S(2)}, u32[]{:S(2)}) collective-permute-start(f32[16,1024]{1,0:T(8,128)S(1)} %get-tuple-element.42.xb_ref), channel_id=1, source_target_pairs={{8,16},{16,8},{9,17},{17,9},{10,18},{18,10},{11,19},{19,11},{12,20... | collective-permute-start | bytes 196616 | tf_op jit(solution)/shard_map/ppermute | solution.py:658
  5.7 0.0 copy-done
  5.8 2.4 %partial_sweep.1 = (f32[5,32,1024]{2,1,0:T(8,128)S(1)}, f32[4,32,128]{2,1,0:T(8,128)S(1)}, f32[4,32,128]{2,1,0:T(8,128)S(1)}, bf16[256,2048]{1,0:T(8,128)(2,1)S(...) custom-call(f32[5,32,1024]{2,1,0:T(8,128)S(1)} %get-tuple-element.31.adjoint_ref, ...), custom_call_target="tpu_custom_call" | custom-call | flops 12000000 | bytes 3000000 | tf_op jit(solution)/shard_map/partial_sweep/pallas_call | solution.py:693
  8.1 0.0 collective-permute-done.ra_ref
  8.2 1.6 %collective-permute-done.1.rb_ref = f32[16,1024]{1,0:T(8,128)S(1)} collective-permute-done((f32[16,1024]{1,0:T(8,128)S(1)}, f32[16,1024]{1,0:T(8,128)S(1)}, u32[]{:S(2)}, u32[]{:S(2)}) %collective-permute-start.1) | collective-permute-done | bytes 65568 | tf_op jit(solution)/shard_map/ppermute | solution.py:658
  9.7 0.2 streamwise_halo.1
  9.9 2.2 %collective-permute-start.2 = (f32[4,32,128]{2,1,0:T(8,128)S(1)}, f32[4,32,128]{2,1,0:T(8,128)S(1)}, u32[]{:S(2)}, u32[]{:S(2)}) collective-permute-start(f32[4,32,128]{2,1,0:T(8,128)S(1)} %get-tuple-element.48.ya_ref), channel_id=1, source_target_pairs={{0,1},{2,3},{4,5},{6,7},{1,0},{3,2},{5,4},{7,6},{8,9},{10,11},{12,... | collective-permute-start | bytes 196616 | tf_op jit(solution)/shard_map/ppermute | solution.py:658
  12.1 3.1 %collective-permute-start.3 = (f32[4,32,128]{2,1,0:T(8,128)S(1)}, f32[4,32,128]{2,1,0:T(8,128)S(1)}, u32[]{:S(2)}, u32[]{:S(2)}) collective-permute-start(f32[4,32,128]{2,1,0:T(8,128)S(1)} %get-tuple-element.49.yb_ref), channel_id=1, source_target_pairs={{1,2},{3,4},{5,6},{2,1},{4,3},{6,5},{9,10},{11,12},{13,14},{10,9},... | collective-permute-start | bytes 196616 | tf_op jit(solution)/shard_map/ppermute | solution.py:658
  15.2 2.1 %middle_sweep.1 = (f32[5,32,1024]{2,1,0:T(8,128)}, f32[4,2048]{1,0:T(4,128)S(1)}) custom-call(f32[5,32,1024]{2,1,0:T(8,128)S(1)} %get-tuple-element.40.part_ref, f32[5,32,1024]{2,1,0:T(8,128)S(1)} %get-tuple-element.32.rhs_ref, f32[5,32,1024]{2,1,0:T(8,128)S(1)} %get-tuple-element.33.state_ref, bf16[6,32,1024]{2,1,0:T(8,128)(2,1)S(1)} %get-tuple-element.34.face_ref, ...), custom_call_target="tpu_custom_call" | custom-call | flops 12000000 | bytes 3000000 | tf_op jit(solution)/shard_map/middle_sweep/pallas_call | solution.py:713
  17.3 0.0 collective-permute-done.2.sa_ref
  17.3 0.4 %collective-permute-done.3.sb_ref = f32[4,32,128]{2,1,0:T(8,128)S(1)} collective-permute-done((f32[4,32,128]{2,1,0:T(8,128)S(1)}, f32[4,32,128]{2,1,0:T(8,128)S(1)}, u32[]{:S(2)}, u32[]{:S(2)}) %collective-permute-start.3) | collective-permute-done | bytes 65568 | tf_op jit(solution)/shard_map/ppermute | solution.py:658
  17.7 1.8 %edge_sweep_and_sums.1 = (f32[5,32,1024]{2,1,0:T(8,128)}, f32[4,36,128]{2,1,0:T(8,128)S(1)}, f32[4,36,128]{2,1,0:T(8,128)S(1)}) custom-call(f32[5,32,1024]{2,1,0:T(8,128)} %get-tuple-element.47.adjoint_ref, f32[5,32,1024]{2,1,0:T(8,128)S(1)} %get-tuple-element.40.part_ref, ...), custom_call_target="tpu_custom_call", output_to_operand_aliasing={{0}: (0, {})} | custom-call | flops 12000000 | bytes 3000000 | tf_op jit(solution)/shard_map/edge_sweep_and_sums/pallas_call | solution.py:726
  19.5 0.1 collective-permute-start.4
  19.6 1.3 %collective-permute-done.4.got_ref = f32[4,36,128]{2,1,0:T(8,128)S(1)} collective-permute-done((f32[4,36,128]{2,1,0:T(8,128)S(1)}, f32[4,36,128]{2,1,0:T(8,128)S(1)}, u32[]{:S(2)}, u32[]{:S(2)}) %collective-permute-start.4) | collective-permute-done | bytes 73760 | tf_op jit(solution)/shard_map/ppermute | solution.py:658
  20.8 0.2 collective-permute-start.5
  21.1 1.5 %collective-permute-start.6 = (f32[36,128]{1,0:T(8,128)S(1)}, f32[36,128]{1,0:T(8,128)S(1)}, u32[]{:S(2)}, u32[]{:S(2)}) collective-permute-start(f32[36,128]{1,0:T(8,128)S(1)} %get-tuple-element.57), channel_id=1, source_target_pairs={{0,3},{1,2},{2,1},{3,0},{4,7},{5,6},{6,5},{7,4},{8,11},{9,10},{10,... | collective-permute-start | bytes 55304 | tf_op jit(solution)/shard_map/ppermute | solution.py:754
  22.6 2.2 %collective-permute-start.7 = (f32[36,128]{1,0:T(8,128)S(1)}, f32[36,128]{1,0:T(8,128)S(1)}, u32[]{:S(2)}, u32[]{:S(2)}) collective-permute-start(f32[36,128]{1,0:T(8,128)S(1)} %get-tuple-element.58), channel_id=1, source_target_pairs={{0,5},{1,4},{2,7},{3,6},{4,1},{5,0},{6,3},{7,2},{8,13},{9,12},{10,... | collective-permute-start | bytes 55304 | tf_op jit(solution)/shard_map/ppermute | solution.py:754
  24.8 0.3 %collective-permute-start.8 = (f32[36,128]{1,0:T(8,128)S(1)}, f32[36,128]{1,0:T(8,128)S(1)}, u32[]{:S(2)}, u32[]{:S(2)}) collective-permute-start(f32[36,128]{1,0:T(8,128)S(1)} %get-tuple-element.59), channel_id=1, source_target_pairs={{0,7},{1,6},{2,5},{3,4},{4,3},{5,2},{6,1},{7,0},{8,15},{9,14},{10,... | collective-permute-start | bytes 55304 | tf_op jit(solution)/shard_map/ppermute | solution.py:754
  25.1 0.0 collective-permute-done.5.refs_0_
  25.1 0.0 collective-permute-done.6.refs_1_
  25.1 1.7 %collective-permute-done.7.refs_2_ = f32[36,128]{1,0:T(8,128)S(1)} collective-permute-done((f32[36,128]{1,0:T(8,128)S(1)}, f32[36,128]{1,0:T(8,128)S(1)}, u32[]{:S(2)}, u32[]{:S(2)}) %collective-permute-start.7) | collective-permute-done | bytes 18464 | tf_op jit(solution)/shard_map/ppermute | solution.py:754
  26.8 3.0 %collective-permute-done.8.refs_3_ = f32[36,128]{1,0:T(8,128)S(1)} collective-permute-done((f32[36,128]{1,0:T(8,128)S(1)}, f32[36,128]{1,0:T(8,128)S(1)}, u32[]{:S(2)}, u32[]{:S(2)}) %collective-permute-start.8) | collective-permute-done | bytes 18464 | tf_op jit(solution)/shard_map/ppermute | solution.py:754
  29.8 0.6 %own_sums.1 = f32[3,1536]{1,0:T(4,128)} custom-call(f32[36,128]{1,0:T(8,128)S(1)} %collective-permute-done.5.refs_0_, f32[36,128]{1,0:T(8,128)S(1)} %collective-permute-done.6.refs_1_, f32[36,128]{1,0:T(8,128)S(1)} %collective-permute-done.7.refs_2_, f32[36,128]{1,0:T(8,128)S(1)} %collective-permute-done.8.refs_3_), custom_call_target="tpu_custom_call" | custom-call | flops 1000 | bytes 250 | tf_op jit(solution)/shard_map/own_sums/pallas_call | solution.py:755
  (1 shorter events, 0.0 us)
Async XLA Ops:
  0.6 5.1 %copy-start = (s32[1,8]{1,0:T(1,128)S(1)}, s32[1,8]{1,0:T(1,128)}, u32[]{:S(2)}) copy-start(s32[1,8]{1,0:T(1,128)} %count_ref.1) | copy-start | bytes 100
  2.6 5.6 %collective-permute-start = (f32[16,1024]{1,0:T(8,128)S(1)}, f32[16,1024]{1,0:T(8,128)S(1)}, u32[]{:S(2)}, u32[]{:S(2)}) collective-permute-start(f32[16,1024]{1,0:T(8,128)S(1)} %get-tuple-element.41.xa_ref), channel_id=1, source_target_pairs={{0,8},{16,24},{8,0},{24,16},{1,9},{17,25},{9,1},{25,17},{2,10},{18... | collective-permute-start | bytes 196616 | tf_op jit(solution)/shard_map/ppermute | solution.py:658
  3.8 5.9 %collective-permute-start.1 = (f32[16,1024]{1,0:T(8,128)S(1)}, f32[16,1024]{1,0:T(8,128)S(1)}, u32[]{:S(2)}, u32[]{:S(2)}) collective-permute-start(f32[16,1024]{1,0:T(8,128)S(1)} %get-tuple-element.42.xb_ref), channel_id=1, source_target_pairs={{8,16},{16,8},{9,17},{17,9},{10,18},{18,10},{11,19},{19,11},{12,20... | collective-permute-start | bytes 196616 | tf_op jit(solution)/shard_map/ppermute | solution.py:658
  9.9 7.4 %collective-permute-start.2 = (f32[4,32,128]{2,1,0:T(8,128)S(1)}, f32[4,32,128]{2,1,0:T(8,128)S(1)}, u32[]{:S(2)}, u32[]{:S(2)}) collective-permute-start(f32[4,32,128]{2,1,0:T(8,128)S(1)} %get-tuple-element.48.ya_ref), channel_id=1, source_target_pairs={{0,1},{2,3},{4,5},{6,7},{1,0},{3,2},{5,4},{7,6},{8,9},{10,11},{12,... | collective-permute-start | bytes 196616 | tf_op jit(solution)/shard_map/ppermute | solution.py:658
  12.1 5.6 %collective-permute-start.3 = (f32[4,32,128]{2,1,0:T(8,128)S(1)}, f32[4,32,128]{2,1,0:T(8,128)S(1)}, u32[]{:S(2)}, u32[]{:S(2)}) collective-permute-start(f32[4,32,128]{2,1,0:T(8,128)S(1)} %get-tuple-element.49.yb_ref), channel_id=1, source_target_pairs={{1,2},{3,4},{5,6},{2,1},{4,3},{6,5},{9,10},{11,12},{13,14},{10,9},... | collective-permute-start | bytes 196616 | tf_op jit(solution)/shard_map/ppermute | solution.py:658
  19.5 1.3 %collective-permute-start.4 = (f32[4,36,128]{2,1,0:T(8,128)S(1)}, f32[4,36,128]{2,1,0:T(8,128)S(1)}, u32[]{:S(2)}, u32[]{:S(2)}) collective-permute-start(f32[4,36,128]{2,1,0:T(8,128)S(1)} %get-tuple-element.55), channel_id=1, source_target_pairs={{0,1},{2,3},{4,5},{6,7},{1,0},{3,2},{5,4},{7,6},{8,9},{10,11},{12,... | collective-permute-start | bytes 221192 | tf_op jit(solution)/shard_map/ppermute | solution.py:658
  20.8 4.3 %collective-permute-start.5 = (f32[36,128]{1,0:T(8,128)S(1)}, f32[36,128]{1,0:T(8,128)S(1)}, u32[]{:S(2)}, u32[]{:S(2)}) collective-permute-start(f32[36,128]{1,0:T(8,128)S(1)} %get-tuple-element.56), channel_id=1, source_target_pairs={{0,1},{1,0},{2,3},{3,2},{4,5},{5,4},{6,7},{7,6},{8,9},{9,8},{10,11... | collective-permute-start | bytes 55304 | tf_op jit(solution)/shard_map/ppermute | solution.py:754
  21.1 4.1 %collective-permute-start.6 = (f32[36,128]{1,0:T(8,128)S(1)}, f32[36,128]{1,0:T(8,128)S(1)}, u32[]{:S(2)}, u32[]{:S(2)}) collective-permute-start(f32[36,128]{1,0:T(8,128)S(1)} %get-tuple-element.57), channel_id=1, source_target_pairs={{0,3},{1,2},{2,1},{3,0},{4,7},{5,6},{6,5},{7,4},{8,11},{9,10},{10,... | collective-permute-start | bytes 55304 | tf_op jit(solution)/shard_map/ppermute | solution.py:754
  22.6 4.2 %collective-permute-start.7 = (f32[36,128]{1,0:T(8,128)S(1)}, f32[36,128]{1,0:T(8,128)S(1)}, u32[]{:S(2)}, u32[]{:S(2)}) collective-permute-start(f32[36,128]{1,0:T(8,128)S(1)} %get-tuple-element.58), channel_id=1, source_target_pairs={{0,5},{1,4},{2,7},{3,6},{4,1},{5,0},{6,3},{7,2},{8,13},{9,12},{10,... | collective-permute-start | bytes 55304 | tf_op jit(solution)/shard_map/ppermute | solution.py:754
  24.8 5.0 %collective-permute-start.8 = (f32[36,128]{1,0:T(8,128)S(1)}, f32[36,128]{1,0:T(8,128)S(1)}, u32[]{:S(2)}, u32[]{:S(2)}) collective-permute-start(f32[36,128]{1,0:T(8,128)S(1)} %get-tuple-element.59), channel_id=1, source_target_pairs={{0,7},{1,6},{2,5},{3,4},{4,3},{5,2},{6,1},{7,0},{8,15},{9,14},{10,... | collective-permute-start | bytes 55304 | tf_op jit(solution)/shard_map/ppermute | solution.py:754

commit v5 on v4

--- a/solution.py
+++ b/solution.py
@@ -507,15 +507,61 @@
     store.wait()
 
 
+def add_up(value_ref, shape_ref, vertex_ref, vertex_hot_ref, out_ref, parity, capacity):
+    slots = value_ref.shape[1]
+    group = max(capacity, LANES)
+    together = group // capacity
+    vertex_rows = -(-together * PARTS // 16) * 16
+    chunk = lax.broadcasted_iota(jnp.int32, (1, group), 1) // capacity
+    if together == 1:
+        groups = [pl.multiple_of((s + parity) * group, group) for s in range(0, slots // group, 2)]
+    else:
+        groups = [s * group for s in range(slots // group)]
+    for s, start in enumerate(groups):
+        lanes = pl.ds(start, group)
+        shape = [shape_ref[k : k + 1, lanes] for k in range(21)]
+        values = [value_ref[k : k + 1, lanes] for k in range(4)]
+        terms = tet_terms(values[3], values[:3], shape)
+        left, right = [], []
+        for c in range(4):
+            row = vertex_ref[c : c + 1, lanes] // LANES + chunk * PARTS
+            match = lax.broadcasted_iota(jnp.int16, (vertex_rows, group), 0) == row.astype(jnp.int16)
+            blocks = []
+            for k in range(3):
+                blocks += [jnp.where(match, v, jnp.zeros((), BF16)) for v in split(terms[c][k])]
+            left.append(jnp.concatenate(blocks, axis=0))
+            right.append(vertex_hot_ref[c, :, lanes])
+        product = lax.dot_general(
+            jnp.concatenate(left, axis=1), jnp.concatenate(right, axis=1),
+            (((1,), (1,)), ((), ())), preferred_element_type=F32,
+        )
+        for k in range(3):
+            big = product[2 * k * vertex_rows : (2 * k + 1) * vertex_rows]
+            small = product[(2 * k + 1) * vertex_rows : (2 * k + 2) * vertex_rows]
+            total = big + small
+            rows = slice(k * PARTS, (k + 1) * PARTS)
+            if together == 1:
+                out_ref[s, rows, :] = total[:PARTS]
+            for q in range(0, together - 1, 2):
+                pair = [total[(q + i) * PARTS : (q + i + 1) * PARTS] for i in range(2)]
+                out_ref[(s * together + q) // 2, rows, :] = jnp.where(parity == 0, *pair)
+
+
+def keep_kernel(value_ref, shape_ref, vertex_ref, vertex_hot_ref, keep_ref):
+    capacity = value_ref.shape[1] // (2 * keep_ref.shape[0])
+    parity = 1 - lax.rem(lax.axis_index("blk"), 2)
+    add_up(value_ref, shape_ref, vertex_ref, vertex_hot_ref, keep_ref, parity, capacity)
+
+
 def third_kernel(
-    adjoint_ref, part_ref, rhs_ref, state_ref, face_ref, pseudo_ref, res_ref, ra_ref, rb_ref,
+    part_ref, rhs_ref, state_ref, face_ref, pseudo_ref, res_ref, ra_ref, rb_ref,
     ya_ref, yb_ref, sa_ref, sb_ref, gathered_ref, column_ref, cell_ref, vertex_ref, vertex_hot_ref, shape_ref,
-    out_ref, keep_ref, send_ref,
-    grids, field, high, low, sums, sem,
+    field, value_ref, send_ref,
+    grids, high, low,
 ):
     edge, span = pseudo_ref.shape
     per = LANES // edge
-    owners = 2 * keep_ref.shape[0]
+    owners = 2 * send_ref.shape[0]
     slots = cell_ref.shape[1]
     capacity = slots // owners
     even = is_even("grp")
@@ -523,7 +569,6 @@
     lane = lax.broadcasted_iota(jnp.int32, (edge, LANES), 1)
     lane_row = lax.broadcasted_iota(jnp.int32, (1, LANES), 1)
     rows = slice(ROWS, ROWS + edge)
-    stores = []
 
     def pick(a_ref, b_ref, flag, k):
         g, q = divmod(k, per)
@@ -593,47 +638,26 @@
                 at = slice(k * edge + top, k * edge + top + 2 * ROWS)
                 high[at, wide] = big
                 low[at, wide] = small
-        store = pltpu.make_async_copy(field.at[side], out_ref.at[:, :, lanes], sem.at[side])
-        store.start()
-        stores.append(store)
 
     x, number = chunk_of(cell_ref[...], span)
     gathered = gather(high, low, column_ref, jnp.where(number == 0, x, -1))
     gathered = [gathered_ref[k : k + 1, :] + v for k, v in enumerate(gathered)]
 
-    group = max(capacity, LANES)
-    together = group // capacity
-    vertex_rows = -(-together * PARTS // 16) * 16
-    chunk = lax.broadcasted_iota(jnp.int32, (1, group), 1) // capacity
-    for s in range(0, slots // group):
-        lanes = slice(s * group, (s + 1) * group)
-        shape = [shape_ref[k : k + 1, lanes] for k in range(21)]
-        terms = tet_terms(gathered[3][:, lanes], [gathered[k][:, lanes] for k in range(3)], shape)
-        left, right = [], []
-        for c in range(4):
-            row = vertex_ref[c : c + 1, lanes] // LANES + chunk * PARTS
-            match = lax.broadcasted_iota(jnp.int16, (vertex_rows, group), 0) == row.astype(jnp.int16)
-            blocks = []
-            for k in range(3):
-                blocks += [jnp.where(match, v, jnp.zeros((), BF16)) for v in split(terms[c][k])]
-            left.append(jnp.concatenate(blocks, axis=0))
-            right.append(vertex_hot_ref[c, :, lanes])
-        product = lax.dot_general(
-            jnp.concatenate(left, axis=1), jnp.concatenate(right, axis=1),
-            (((1,), (1,)), ((), ())), preferred_element_type=F32,
-        )
-        for k in range(3):
-            big = product[2 * k * vertex_rows : (2 * k + 1) * vertex_rows]
-            small = product[(2 * k + 1) * vertex_rows : (2 * k + 2) * vertex_rows]
-            total = big + small
-            for q in range(together):
-                owner = s * together + q
-                sums[owner % 2, owner // 2, k * PARTS : (k + 1) * PARTS, :] = total[q * PARTS : (q + 1) * PARTS]
-    core = lax.rem(lax.axis_index("blk"), 2)
-    keep_ref[...] = sums[1 - core]
-    send_ref[...] = sums[core]
-    for store in stores:
-        store.wait()
+    for k in range(4):
+        value_ref[k : k + 1, :] = gathered[k]
+    add_up(value_ref, shape_ref, vertex_ref, vertex_hot_ref, send_ref, lax.rem(lax.axis_index("blk"), 2), capacity)
+
+
+def store_kernel(adjoint_ref, field_ref, after_ref, out_ref, sem):
+    span = out_ref.shape[2]
+    copies = [
+        pltpu.make_async_copy(field_ref.at[side], out_ref.at[:, :, pl.ds(start, LANES)], sem.at[side])
+        for side, start in ((0, 0), (1, span - LANES))
+    ]
+    for copy in copies:
+        copy.start()
+    for copy in copies:
+        copy.wait()
 
 
 def fourth_kernel(keep_ref, got_ref, *refs):
@@ -723,22 +747,22 @@
     half = owners // 2
     sums_shape = (half, 3 * PARTS, LANES)
     table = (4 * edge, 2 * LANES)
-    adjoint, keep, send = call(
+    ends, values, send = call(
         third_kernel,
-        [struct((5, edge, span), F32), struct(sums_shape, F32), struct(sums_shape, F32)],
-        [HBM] + [VMEM] * 18,
-        [HBM, VMEM, VMEM],
-        [pltpu.VMEM((2, 5, edge + 2 * ROWS, 3 * LANES), F32), pltpu.VMEM((2, 5, edge, LANES), F32),
-         pltpu.VMEM(table, BF16), pltpu.VMEM(table, BF16), pltpu.VMEM((2,) + sums_shape, F32),
-         pltpu.SemaphoreType.DMA((2,))],
+        [struct((2, 5, edge, LANES), F32), struct((4, slots), F32), struct(sums_shape, F32)],
+        [VMEM] * 18,
+        [VMEM] * 3,
+        [pltpu.VMEM((2, 5, edge + 2 * ROWS, 3 * LANES), F32), pltpu.VMEM(table, BF16), pltpu.VMEM(table, BF16)],
         "edge_sweep_and_sums",
         flops=12_000_000,
-        aliases={0: 0},
     )(
-        adjoint, part, *fields[1:], res, ra, rb, ya, yb, sa, sb,
+        part, *fields[1:], res, ra, rb, ya, yb, sa, sb,
         gathered, column, cell, vertex, vertex_hot, shapes,
     )
     got = swap(send, "blk", [(i, i + 1) for i in range(0, blocks, 2)])
+    keep = call(
+        keep_kernel, struct(sums_shape, F32), [VMEM] * 4, VMEM, [], "kept_sums", flops=3_000_000
+    )(values, shapes, vertex, vertex_hot)
     place = lax.axis_index("blk") // 2
     while half > 4:
         half //= 2
@@ -751,6 +775,10 @@
     parts = call(
         fourth_kernel, [one] * half, [VMEM] * 2, [VMEM] * half, [], "core_pair_sums"
     )(keep, got)
+    adjoint = call(
+        store_kernel, struct((5, edge, span), F32), [HBM, VMEM, VMEM], HBM, [pltpu.SemaphoreType.DMA((2,))],
+        "store_field", flops=3_000_000, aliases={0: 0},
+    )(adjoint, ends, parts[0])
     parts = [lax.ppermute(v, "blk", [(i, i ^ (2 * k + 1)) for i in range(blocks)]) for k, v in enumerate(parts)]
     sensitivity = call(last_kernel, struct((3, VERT_DEV), F32), [VMEM] * half, VMEM, [], "own_sums")(*parts)
     return adjoint, sensitivity

time: 30.6 us -> 30.3 us (level)
  waiting for transfers between devices: 7.91 us -> 6.73 us
  Pallas kernels: 8.99 us -> 9.84 us
    pallas_call x1 -> x3, Pallas kernels: 1.82 us -> 2.62 us  [the longest x1 1.52 us: local(): call(third_kernel, [struct((2, 5, edge, LANES), F32), struct((4, slots),...]
    ppermute x4, waiting for transfers between devices: 4.7 us -> 3.99 us  [local(): lax.ppermute(v, 'blk', [(i, i ^ 2 * k + 1) for i in range(blocks)])]
    ppermute x5, waiting for transfers between devices: 3.21 us -> 2.74 us  [swap(): return lax.ppermute(value, axis, pairs + [(b, a) for a, b in pairs])]
  transfers between devices with their start and end apart: 9 -> 9, of which waited for: 5 -> 5; matrix products, arithmetic and copies ran while one was open for 0% -> 0% of each run, Pallas kernels for 15% -> 19%
where the time goes in v5:
time: 30.3 us; the launch traced here: 30.1 us
  starting transfers between devices  12.8 us (42%)
  Pallas kernels  9.84 us (32%)
  waiting for transfers between devices  6.73 us (22%)
  between operations  0.75 us (2%)
    ppermute x5, starting transfers between devices, swap(): return lax.ppermute(value, axis, pairs + [(b, a) for a, b in pairs])  8.52 us
    ppermute x4, starting transfers between devices, local(): lax.ppermute(v, 'blk', [(i, i ^ 2 * k + 1) for i in range(blocks)])  4.29 us
    ppermute x4, waiting for transfers between devices, local(): lax.ppermute(v, 'blk', [(i, i ^ 2 * k + 1) for i in range(blocks)])  3.99 us
    ppermute x5, waiting for transfers between devices, swap(): return lax.ppermute(value, axis, pairs + [(b, a) for a, b in pairs])  2.74 us
    pallas_call x1, Pallas kernels, local(): call(first_kernel, [struct((5, edge, span), F32), struct(packed, F32), st...  2.42 us
    pallas_call x1, Pallas kernels, local(): call(middle_kernel, [struct((5, edge, span), F32), struct((4, slots), F32...  2.08 us
    pallas_call x1, Pallas kernels, local(): call(plane_kernel, [message] * 2 + [struct(v.shape, v.dtype) for v in arr...  1.91 us
    pallas_call x1, Pallas kernels, local(): call(third_kernel, [struct((2, 5, edge, LANES), F32), struct((4, slots),...  1.52 us
  transfers between devices with their start and end apart: 9, of which 5 were waited for; matrix products, arithmetic and copies ran while one was open for 0% of the time, Pallas kernels for 19%

profile of v5, /device:TPU:5, one launch (start us, length us, event | category | flops | bytes accessed | tf_op | source)
XLA Modules:
  0.0 30.1 jit_solution(12211751194214072992)
XLA Ops:
  0.6 0.0 copy-start
  0.6 1.9 %plane_messages.1 = (f32[16,1024]{1,0:T(8,128)S(1)}, f32[16,1024]{1,0:T(8,128)S(1)}, f32[5,32,1024]{2,1,0:T(8,128)S(1)}, f32[5,32,1024]{2,1,0:T(8,128)S(1)}, f32...) custom-call(f32[5,32,1024]{2,1,0:T(8,128)} %adjoint_hbm.1, ...), custom_call_target="tpu_custom_call" | custom-call | flops 1000 | bytes 250 | tf_op jit(solution)/shard_map/plane_messages/pallas_call | solution.py:707
  2.6 1.3 %collective-permute-start = (f32[16,1024]{1,0:T(8,128)S(1)}, f32[16,1024]{1,0:T(8,128)S(1)}, u32[]{:S(2)}, u32[]{:S(2)}) collective-permute-start(f32[16,1024]{1,0:T(8,128)S(1)} %get-tuple-element.41.xa_ref), channel_id=1, source_target_pairs={{0,8},{16,24},{8,0},{24,16},{1,9},{17,25},{9,1},{25,17},{2,10},{18... | collective-permute-start | bytes 196616 | tf_op jit(solution)/shard_map/ppermute | solution.py:682
  3.8 1.9 %collective-permute-start.1 = (f32[16,1024]{1,0:T(8,128)S(1)}, f32[16,1024]{1,0:T(8,128)S(1)}, u32[]{:S(2)}, u32[]{:S(2)}) collective-permute-start(f32[16,1024]{1,0:T(8,128)S(1)} %get-tuple-element.42.xb_ref), channel_id=1, source_target_pairs={{8,16},{16,8},{9,17},{17,9},{10,18},{18,10},{11,19},{19,11},{12,20... | collective-permute-start | bytes 196616 | tf_op jit(solution)/shard_map/ppermute | solution.py:682
  5.7 0.0 copy-done
  5.8 2.4 %partial_sweep.1 = (f32[5,32,1024]{2,1,0:T(8,128)S(1)}, f32[4,32,128]{2,1,0:T(8,128)S(1)}, f32[4,32,128]{2,1,0:T(8,128)S(1)}, bf16[256,2048]{1,0:T(8,128)(2,1)S(...) custom-call(f32[5,32,1024]{2,1,0:T(8,128)S(1)} %get-tuple-element.31.adjoint_ref, ...), custom_call_target="tpu_custom_call" | custom-call | flops 12000000 | bytes 3000000 | tf_op jit(solution)/shard_map/partial_sweep/pallas_call | solution.py:717
  8.2 0.0 collective-permute-done.ra_ref
  8.2 1.5 %collective-permute-done.1.rb_ref = f32[16,1024]{1,0:T(8,128)S(1)} collective-permute-done((f32[16,1024]{1,0:T(8,128)S(1)}, f32[16,1024]{1,0:T(8,128)S(1)}, u32[]{:S(2)}, u32[]{:S(2)}) %collective-permute-start.1) | collective-permute-done | bytes 65568 | tf_op jit(solution)/shard_map/ppermute | solution.py:682
  9.7 0.2 streamwise_halo.1
  9.9 2.2 %collective-permute-start.2 = (f32[4,32,128]{2,1,0:T(8,128)S(1)}, f32[4,32,128]{2,1,0:T(8,128)S(1)}, u32[]{:S(2)}, u32[]{:S(2)}) collective-permute-start(f32[4,32,128]{2,1,0:T(8,128)S(1)} %get-tuple-element.48.ya_ref), channel_id=1, source_target_pairs={{0,1},{2,3},{4,5},{6,7},{1,0},{3,2},{5,4},{7,6},{8,9},{10,11},{12,... | collective-permute-start | bytes 196616 | tf_op jit(solution)/shard_map/ppermute | solution.py:682
  12.1 3.1 %collective-permute-start.3 = (f32[4,32,128]{2,1,0:T(8,128)S(1)}, f32[4,32,128]{2,1,0:T(8,128)S(1)}, u32[]{:S(2)}, u32[]{:S(2)}) collective-permute-start(f32[4,32,128]{2,1,0:T(8,128)S(1)} %get-tuple-element.49.yb_ref), channel_id=1, source_target_pairs={{1,2},{3,4},{5,6},{2,1},{4,3},{6,5},{9,10},{11,12},{13,14},{10,9},... | collective-permute-start | bytes 196616 | tf_op jit(solution)/shard_map/ppermute | solution.py:682
  15.2 2.1 %middle_sweep.1 = (f32[5,32,1024]{2,1,0:T(8,128)}, f32[4,2048]{1,0:T(4,128)S(1)}) custom-call(f32[5,32,1024]{2,1,0:T(8,128)S(1)} %get-tuple-element.40.part_ref, f32[5,32,1024]{2,1,0:T(8,128)S(1)} %get-tuple-element.32.rhs_ref, f32[5,32,1024]{2,1,0:T(8,128)S(1)} %get-tuple-element.33.state_ref, bf16[6,32,1024]{2,1,0:T(8,128)(2,1)S(1)} %get-tuple-element.34.face_ref, ...), custom_call_target="tpu_custom_call" | custom-call | flops 12000000 | bytes 3000000 | tf_op jit(solution)/shard_map/middle_sweep/pallas_call | solution.py:737
  17.3 0.0 collective-permute-done.2.sa_ref
  17.3 0.4 %collective-permute-done.3.sb_ref = f32[4,32,128]{2,1,0:T(8,128)S(1)} collective-permute-done((f32[4,32,128]{2,1,0:T(8,128)S(1)}, f32[4,32,128]{2,1,0:T(8,128)S(1)}, u32[]{:S(2)}, u32[]{:S(2)}) %collective-permute-start.3) | collective-permute-done | bytes 65568 | tf_op jit(solution)/shard_map/ppermute | solution.py:682
  17.7 1.5 %edge_sweep_and_sums.1 = (f32[2,5,32,128]{3,2,1,0:T(8,128)S(1)}, f32[4,2048]{1,0:T(4,128)S(1)}, f32[4,36,128]{2,1,0:T(8,128)S(1)}) custom-call(f32[5,32,1024]{2,1,0:T(8,128)S(1)} %get-tuple-element.40.part_ref, f32[5,32,1024]{2,1,0:T(8,128)S(1)} %get-tuple-element.32.rhs_ref, f32[5,32,1024]{2,1,0:T(8,128)S(1)} %get-tuple-element.33.state_ref, ...), custom_call_target="tpu_custom_call" | custom-call | flops 12000000 | bytes 3000000 | tf_op jit(solution)/shard_map/edge_sweep_and_sums/pallas_call | solution.py:750
  19.2 0.1 collective-permute-start.4
  19.3 0.4 %kept_sums.1.keep_ref = f32[4,36,128]{2,1,0:T(8,128)S(1)} custom-call(f32[4,2048]{1,0:T(4,128)S(1)} %get-tuple-element.54.value_ref, f32[24,2048]{1,0:T(8,128)S(1)} %get-tuple-element.52.shape_ref, s32[4,2048]{1,0:T(4,128)S(1)} %get-tuple-element.39.vertex_ref, bf16[4,128,2048]{2,1,0:T(8,128)(2,1)S(1)} %get-tuple-element.51.vertex_hot_ref), custom_call_target="tpu_custom_call" | custom-call | flops 3000000 | bytes 750000 | tf_op jit(solution)/shard_map/kept_sums/pallas_call | solution.py:763
  19.7 0.8 %collective-permute-done.4.got_ref = f32[4,36,128]{2,1,0:T(8,128)S(1)} collective-permute-done((f32[4,36,128]{2,1,0:T(8,128)S(1)}, f32[4,36,128]{2,1,0:T(8,128)S(1)}, u32[]{:S(2)}, u32[]{:S(2)}) %collective-permute-start.4) | collective-permute-done | bytes 73760 | tf_op jit(solution)/shard_map/ppermute | solution.py:682
  20.5 0.2 collective-permute-start.5
  20.8 1.5 %collective-permute-start.6 = (f32[36,128]{1,0:T(8,128)S(1)}, f32[36,128]{1,0:T(8,128)S(1)}, u32[]{:S(2)}, u32[]{:S(2)}) collective-permute-start(f32[36,128]{1,0:T(8,128)S(1)} %get-tuple-element.57), channel_id=1, source_target_pairs={{0,3},{1,2},{2,1},{3,0},{4,7},{5,6},{6,5},{7,4},{8,11},{9,10},{10,... | collective-permute-start | bytes 55304 | tf_op jit(solution)/shard_map/ppermute | solution.py:782
  22.3 2.2 %collective-permute-start.7 = (f32[36,128]{1,0:T(8,128)S(1)}, f32[36,128]{1,0:T(8,128)S(1)}, u32[]{:S(2)}, u32[]{:S(2)}) collective-permute-start(f32[36,128]{1,0:T(8,128)S(1)} %get-tuple-element.58), channel_id=1, source_target_pairs={{0,5},{1,4},{2,7},{3,6},{4,1},{5,0},{6,3},{7,2},{8,13},{9,12},{10,... | collective-permute-start | bytes 55304 | tf_op jit(solution)/shard_map/ppermute | solution.py:782
  24.5 0.3 %collective-permute-start.8 = (f32[36,128]{1,0:T(8,128)S(1)}, f32[36,128]{1,0:T(8,128)S(1)}, u32[]{:S(2)}, u32[]{:S(2)}) collective-permute-start(f32[36,128]{1,0:T(8,128)S(1)} %get-tuple-element.59), channel_id=1, source_target_pairs={{0,7},{1,6},{2,5},{3,4},{4,3},{5,2},{6,1},{7,0},{8,15},{9,14},{10,... | collective-permute-start | bytes 55304 | tf_op jit(solution)/shard_map/ppermute | solution.py:782
  24.8 0.7 %store_field.1 = f32[5,32,1024]{2,1,0:T(8,128)} custom-call(f32[5,32,1024]{2,1,0:T(8,128)} %get-tuple-element.47.adjoint_ref, f32[2,5,32,128]{3,2,1,0:T(8,128)S(1)} %get-tuple-element.53.field_ref, f32[36,128]{1,0:T(8,128)S(1)} %get-tuple-element.56.after_ref), custom_call_target="tpu_custom_call", output_to_operand_aliasing={{}: (0, {})} | custom-call | flops 3000000 | bytes 750000 | tf_op jit(solution)/shard_map/store_field/pallas_call | solution.py:778
  25.5 0.0 collective-permute-done.5.refs_0_
  25.5 0.0 collective-permute-done.6.refs_1_
  25.5 1.0 %collective-permute-done.7.refs_2_ = f32[36,128]{1,0:T(8,128)S(1)} collective-permute-done((f32[36,128]{1,0:T(8,128)S(1)}, f32[36,128]{1,0:T(8,128)S(1)}, u32[]{:S(2)}, u32[]{:S(2)}) %collective-permute-start.7) | collective-permute-done | bytes 18464 | tf_op jit(solution)/shard_map/ppermute | solution.py:782
  26.5 3.0 %collective-permute-done.8.refs_3_ = f32[36,128]{1,0:T(8,128)S(1)} collective-permute-done((f32[36,128]{1,0:T(8,128)S(1)}, f32[36,128]{1,0:T(8,128)S(1)}, u32[]{:S(2)}, u32[]{:S(2)}) %collective-permute-start.8) | collective-permute-done | bytes 18464 | tf_op jit(solution)/shard_map/ppermute | solution.py:782
  29.5 0.6 %own_sums.1 = f32[3,1536]{1,0:T(4,128)} custom-call(f32[36,128]{1,0:T(8,128)S(1)} %collective-permute-done.5.refs_0_, f32[36,128]{1,0:T(8,128)S(1)} %collective-permute-done.6.refs_1_, f32[36,128]{1,0:T(8,128)S(1)} %collective-permute-done.7.refs_2_, f32[36,128]{1,0:T(8,128)S(1)} %collective-permute-done.8.refs_3_), custom_call_target="tpu_custom_call" | custom-call | flops 1000 | bytes 250 | tf_op jit(solution)/shard_map/own_sums/pallas_call | solution.py:783
  (1 shorter events, 0.0 us)
Async XLA Ops:
  0.6 5.1 %copy-start = (s32[1,8]{1,0:T(1,128)S(1)}, s32[1,8]{1,0:T(1,128)}, u32[]{:S(2)}) copy-start(s32[1,8]{1,0:T(1,128)} %count_ref.1) | copy-start | bytes 100
  2.6 5.6 %collective-permute-start = (f32[16,1024]{1,0:T(8,128)S(1)}, f32[16,1024]{1,0:T(8,128)S(1)}, u32[]{:S(2)}, u32[]{:S(2)}) collective-permute-start(f32[16,1024]{1,0:T(8,128)S(1)} %get-tuple-element.41.xa_ref), channel_id=1, source_target_pairs={{0,8},{16,24},{8,0},{24,16},{1,9},{17,25},{9,1},{25,17},{2,10},{18... | collective-permute-start | bytes 196616 | tf_op jit(solution)/shard_map/ppermute | solution.py:682
  3.8 5.9 %collective-permute-start.1 = (f32[16,1024]{1,0:T(8,128)S(1)}, f32[16,1024]{1,0:T(8,128)S(1)}, u32[]{:S(2)}, u32[]{:S(2)}) collective-permute-start(f32[16,1024]{1,0:T(8,128)S(1)} %get-tuple-element.42.xb_ref), channel_id=1, source_target_pairs={{8,16},{16,8},{9,17},{17,9},{10,18},{18,10},{11,19},{19,11},{12,20... | collective-permute-start | bytes 196616 | tf_op jit(solution)/shard_map/ppermute | solution.py:682
  9.9 7.4 %collective-permute-start.2 = (f32[4,32,128]{2,1,0:T(8,128)S(1)}, f32[4,32,128]{2,1,0:T(8,128)S(1)}, u32[]{:S(2)}, u32[]{:S(2)}) collective-permute-start(f32[4,32,128]{2,1,0:T(8,128)S(1)} %get-tuple-element.48.ya_ref), channel_id=1, source_target_pairs={{0,1},{2,3},{4,5},{6,7},{1,0},{3,2},{5,4},{7,6},{8,9},{10,11},{12,... | collective-permute-start | bytes 196616 | tf_op jit(solution)/shard_map/ppermute | solution.py:682
  12.1 5.6 %collective-permute-start.3 = (f32[4,32,128]{2,1,0:T(8,128)S(1)}, f32[4,32,128]{2,1,0:T(8,128)S(1)}, u32[]{:S(2)}, u32[]{:S(2)}) collective-permute-start(f32[4,32,128]{2,1,0:T(8,128)S(1)} %get-tuple-element.49.yb_ref), channel_id=1, source_target_pairs={{1,2},{3,4},{5,6},{2,1},{4,3},{6,5},{9,10},{11,12},{13,14},{10,9},... | collective-permute-start | bytes 196616 | tf_op jit(solution)/shard_map/ppermute | solution.py:682
  19.2 1.3 %collective-permute-start.4 = (f32[4,36,128]{2,1,0:T(8,128)S(1)}, f32[4,36,128]{2,1,0:T(8,128)S(1)}, u32[]{:S(2)}, u32[]{:S(2)}) collective-permute-start(f32[4,36,128]{2,1,0:T(8,128)S(1)} %get-tuple-element.55), channel_id=1, source_target_pairs={{0,1},{2,3},{4,5},{6,7},{1,0},{3,2},{5,4},{7,6},{8,9},{10,11},{12,... | collective-permute-start | bytes 221192 | tf_op jit(solution)/shard_map/ppermute | solution.py:682
  20.5 5.0 %collective-permute-start.5 = (f32[36,128]{1,0:T(8,128)S(1)}, f32[36,128]{1,0:T(8,128)S(1)}, u32[]{:S(2)}, u32[]{:S(2)}) collective-permute-start(f32[36,128]{1,0:T(8,128)S(1)} %get-tuple-element.56.after_ref), channel_id=1, source_target_pairs={{0,1},{1,0},{2,3},{3,2},{4,5},{5,4},{6,7},{7,6},{8,9},{9,8},{10,11... | collective-permute-start | bytes 55304 | tf_op jit(solution)/shard_map/ppermute | solution.py:782
  20.8 4.8 %collective-permute-start.6 = (f32[36,128]{1,0:T(8,128)S(1)}, f32[36,128]{1,0:T(8,128)S(1)}, u32[]{:S(2)}, u32[]{:S(2)}) collective-permute-start(f32[36,128]{1,0:T(8,128)S(1)} %get-tuple-element.57), channel_id=1, source_target_pairs={{0,3},{1,2},{2,1},{3,0},{4,7},{5,6},{6,5},{7,4},{8,11},{9,10},{10,... | collective-permute-start | bytes 55304 | tf_op jit(solution)/shard_map/ppermute | solution.py:782
  22.3 4.2 %collective-permute-start.7 = (f32[36,128]{1,0:T(8,128)S(1)}, f32[36,128]{1,0:T(8,128)S(1)}, u32[]{:S(2)}, u32[]{:S(2)}) collective-permute-start(f32[36,128]{1,0:T(8,128)S(1)} %get-tuple-element.58), channel_id=1, source_target_pairs={{0,5},{1,4},{2,7},{3,6},{4,1},{5,0},{6,3},{7,2},{8,13},{9,12},{10,... | collective-permute-start | bytes 55304 | tf_op jit(solution)/shard_map/ppermute | solution.py:782
  24.5 5.0 %collective-permute-start.8 = (f32[36,128]{1,0:T(8,128)S(1)}, f32[36,128]{1,0:T(8,128)S(1)}, u32[]{:S(2)}, u32[]{:S(2)}) collective-permute-start(f32[36,128]{1,0:T(8,128)S(1)} %get-tuple-element.59), channel_id=1, source_target_pairs={{0,7},{1,6},{2,5},{3,4},{4,3},{5,2},{6,1},{7,0},{8,15},{9,14},{10,... | collective-permute-start | bytes 55304 | tf_op jit(solution)/shard_map/ppermute | solution.py:782

commit v6 on v5

--- a/solution.py
+++ b/solution.py
@@ -14,7 +14,6 @@
 F32 = jnp.float32
 BF16 = jnp.bfloat16
 VMEM = pl.BlockSpec(memory_space=pltpu.VMEM)
-SMEM = pl.BlockSpec(memory_space=pltpu.SMEM)
 HBM = pl.BlockSpec(memory_space=pltpu.HBM)
 LIMIT = 40 * 1024 * 1024
 
@@ -175,8 +174,9 @@
 
 def plane_kernel(
     adjoint_hbm, rhs_hbm, state_hbm, face_hbm, pseudo_hbm, coord_hbm, weight_hbm, cell_hbm, vertex_hbm,
+    count_hbm,
     xa_ref, xb_ref, adjoint_ref, rhs_ref, state_ref, face_ref, pseudo_ref, coord_ref, weight_ref, cell_ref,
-    vertex_ref,
+    vertex_ref, count_ref,
     xsides, sem,
 ):
     edge, span = pseudo_hbm.shape
@@ -200,7 +200,8 @@
     for source, target in fields:
         move(late, rows_of(source, ROWS, edge - 2 * ROWS), rows_of(target, ROWS, edge - 2 * ROWS))
     for source, target in (
-        (coord_hbm, coord_ref), (weight_hbm, weight_ref), (cell_hbm, cell_ref), (vertex_hbm, vertex_ref)
+        (coord_hbm, coord_ref), (weight_hbm, weight_ref), (cell_hbm, cell_ref), (vertex_hbm, vertex_ref),
+        (count_hbm, count_ref),
     ):
         move(late, source, target)
     for copy in early:
@@ -323,9 +324,10 @@
     within = lax.rem(lane_group, capacity)
     for s in range(0, slots // group):
         lanes = slice(s * group, (s + 1) * group)
-        count = count_ref[0, s * together]
+        first = s * together
+        count = jnp.broadcast_to(count_ref[:, first : first + 1], (1, group))
         for q in range(1, together):
-            count = jnp.where(chunk == q, count_ref[0, s * together + q], count)
+            count = jnp.where(chunk == q, count_ref[:, first + q : first + q + 1], count)
         live = jnp.where(within < count, 1.0, 0.0)
         weights = [weight_ref[c : c + 1, lanes] * live for c in range(4)]
         corner = [[coord_ref[k, c : c + 1, lanes] for k in range(3)] for c in range(4)]
@@ -703,27 +705,27 @@
     cell = tet_cell.reshape(1, slots)
     message = struct((16, span), F32)
     fields = (adjoint_init, adjoint_rhs, flow_state, face_weights, pseudo_time)
-    arrays = (*fields, jnp.transpose(tet_coords, (1, 0, 2)), tet_weights, cell, tet_vertex)
+    arrays = (*fields, jnp.transpose(tet_coords, (1, 0, 2)), tet_weights, cell, tet_vertex, tet_count)
     xa, xb, *arrays = call(
         plane_kernel,
         [message] * 2 + [struct(v.shape, v.dtype) for v in arrays],
-        [HBM] * 9,
-        [VMEM] * 11,
-        [pltpu.VMEM((2, 16, span), F32), pltpu.SemaphoreType.DMA((17,))],
+        [HBM] * 10,
+        [VMEM] * 12,
+        [pltpu.VMEM((2, 16, span), F32), pltpu.SemaphoreType.DMA((18,))],
         "plane_messages",
     )(*(pltpu.with_memory_space_constraint(v, pltpu.HBM) for v in arrays))
-    fields, (coords, weights, cell, vertex) = arrays[:5], arrays[5:]
+    fields, (coords, weights, cell, vertex, counts) = arrays[:5], arrays[5:]
     ra, rb = neighbours(xa, xb, "grp")
     part, ylo, yhi, column, vertex_hot, shapes = call(
         first_kernel,
         [struct((5, edge, span), F32), struct(packed, F32), struct(packed, F32), struct((2 * LANES, slots), BF16),
          struct((4, LANES, slots), BF16), struct((24, slots), F32)],
-        [VMEM] * 9 + [SMEM],
+        [VMEM] * 10,
         [VMEM] * 6,
         [pltpu.VMEM(padded, F32), pltpu.VMEM((6, edge, span), F32)],
         "partial_sweep",
         flops=12_000_000,
-    )(*fields, coords, weights, cell, vertex, tet_count)
+    )(*fields, coords, weights, cell, vertex, counts)
     res, ya, yb = call(
         second_kernel,
         [struct((2, 16, span), F32), struct(packed, F32), struct(packed, F32)],

time: 30.3 us -> 30.3 us (level)
  waiting for transfers between devices: 6.73 us -> 7.33 us
  Pallas kernels: 9.84 us -> 9.26 us
    ppermute x5, waiting for transfers between devices: 2.74 us -> 3.34 us  [swap(): return lax.ppermute(value, axis, pairs + [(b, a) for a, b in pairs])]
    pallas_call x1, Pallas kernels: 2.42 us -> 1.83 us  [local(): call(first_kernel, [struct((5, edge, span), F32), struct(packed, F32), st...]
  transfers between devices with their start and end apart: 9 -> 9, of which waited for: 5 -> 5; matrix products, arithmetic and copies ran while one was open for 0% -> 0% of each run, Pallas kernels for 19% -> 17%
where the time goes in v6:
time: 30.3 us; the launch traced here: 30.1 us
  starting transfers between devices  12.8 us (42%)
  Pallas kernels  9.26 us (31%)
  waiting for transfers between devices  7.33 us (24%)
  between operations  0.74 us (2%)
    ppermute x5, starting transfers between devices, swap(): return lax.ppermute(value, axis, pairs + [(b, a) for a, b in pairs])  8.52 us
    ppermute x4, starting transfers between devices, local(): lax.ppermute(v, 'blk', [(i, i ^ 2 * k + 1) for i in range(blocks)])  4.29 us
    ppermute x4, waiting for transfers between devices, local(): lax.ppermute(v, 'blk', [(i, i ^ 2 * k + 1) for i in range(blocks)])  3.99 us
    ppermute x5, waiting for transfers between devices, swap(): return lax.ppermute(value, axis, pairs + [(b, a) for a, b in pairs])  3.34 us
    pallas_call x1, Pallas kernels, local(): call(middle_kernel, [struct((5, edge, span), F32), struct((4, slots), F32...  2.08 us
    pallas_call x1, Pallas kernels, local(): call(plane_kernel, [message] * 2 + [struct(v.shape, v.dtype) for v in arr...  1.92 us
    pallas_call x1, Pallas kernels, local(): call(first_kernel, [struct((5, edge, span), F32), struct(packed, F32), st...  1.83 us
    pallas_call x1, Pallas kernels, local(): call(third_kernel, [struct((2, 5, edge, LANES), F32), struct((4, slots),...  1.52 us
  transfers between devices with their start and end apart: 9, of which 5 were waited for; matrix products, arithmetic and copies ran while one was open for 0% of the time, Pallas kernels for 17%

profile of v6, /device:TPU:5, one launch (start us, length us, event | category | flops | bytes accessed | tf_op | source)
XLA Modules:
  0.0 30.1 jit_solution(9302558237047759678)
XLA Ops:
  0.6 1.9 %plane_messages.1 = (f32[16,1024]{1,0:T(8,128)S(1)}, f32[16,1024]{1,0:T(8,128)S(1)}, f32[5,32,1024]{2,1,0:T(8,128)S(1)}, f32[5,32,1024]{2,1,0:T(8,128)S(1)}, f32...) custom-call(f32[5,32,1024]{2,1,0:T(8,128)} %adjoint_hbm.1, ...), custom_call_target="tpu_custom_call" | custom-call | flops 1000 | bytes 250 | tf_op jit(solution)/shard_map/plane_messages/pallas_call | solution.py:709
  2.6 1.3 %collective-permute-start = (f32[16,1024]{1,0:T(8,128)S(1)}, f32[16,1024]{1,0:T(8,128)S(1)}, u32[]{:S(2)}, u32[]{:S(2)}) collective-permute-start(f32[16,1024]{1,0:T(8,128)S(1)} %get-tuple-element.43.xa_ref), channel_id=1, source_target_pairs={{0,8},{16,24},{8,0},{24,16},{1,9},{17,25},{9,1},{25,17},{2,10},{18... | collective-permute-start | bytes 196616 | tf_op jit(solution)/shard_map/ppermute | solution.py:684
  3.8 1.9 %collective-permute-start.1 = (f32[16,1024]{1,0:T(8,128)S(1)}, f32[16,1024]{1,0:T(8,128)S(1)}, u32[]{:S(2)}, u32[]{:S(2)}) collective-permute-start(f32[16,1024]{1,0:T(8,128)S(1)} %get-tuple-element.44.xb_ref), channel_id=1, source_target_pairs={{8,16},{16,8},{9,17},{17,9},{10,18},{18,10},{11,19},{19,11},{12,20... | collective-permute-start | bytes 196616 | tf_op jit(solution)/shard_map/ppermute | solution.py:684
  5.7 1.8 %partial_sweep.1 = (f32[5,32,1024]{2,1,0:T(8,128)S(1)}, f32[4,32,128]{2,1,0:T(8,128)S(1)}, f32[4,32,128]{2,1,0:T(8,128)S(1)}, bf16[256,2048]{1,0:T(8,128)(2,1)S(...) custom-call(f32[5,32,1024]{2,1,0:T(8,128)S(1)} %get-tuple-element.32.adjoint_ref, ...), custom_call_target="tpu_custom_call" | custom-call | flops 12000000 | bytes 3000000 | tf_op jit(solution)/shard_map/partial_sweep/pallas_call | solution.py:719
  7.6 0.0 collective-permute-done.ra_ref
  7.6 2.1 %collective-permute-done.1.rb_ref = f32[16,1024]{1,0:T(8,128)S(1)} collective-permute-done((f32[16,1024]{1,0:T(8,128)S(1)}, f32[16,1024]{1,0:T(8,128)S(1)}, u32[]{:S(2)}, u32[]{:S(2)}) %collective-permute-start.1) | collective-permute-done | bytes 65568 | tf_op jit(solution)/shard_map/ppermute | solution.py:684
  9.7 0.2 streamwise_halo.1
  9.9 2.2 %collective-permute-start.2 = (f32[4,32,128]{2,1,0:T(8,128)S(1)}, f32[4,32,128]{2,1,0:T(8,128)S(1)}, u32[]{:S(2)}, u32[]{:S(2)}) collective-permute-start(f32[4,32,128]{2,1,0:T(8,128)S(1)} %get-tuple-element.50.ya_ref), channel_id=1, source_target_pairs={{0,1},{2,3},{4,5},{6,7},{1,0},{3,2},{5,4},{7,6},{8,9},{10,11},{12,... | collective-permute-start | bytes 196616 | tf_op jit(solution)/shard_map/ppermute | solution.py:684
  12.1 3.1 %collective-permute-start.3 = (f32[4,32,128]{2,1,0:T(8,128)S(1)}, f32[4,32,128]{2,1,0:T(8,128)S(1)}, u32[]{:S(2)}, u32[]{:S(2)}) collective-permute-start(f32[4,32,128]{2,1,0:T(8,128)S(1)} %get-tuple-element.51.yb_ref), channel_id=1, source_target_pairs={{1,2},{3,4},{5,6},{2,1},{4,3},{6,5},{9,10},{11,12},{13,14},{10,9},... | collective-permute-start | bytes 196616 | tf_op jit(solution)/shard_map/ppermute | solution.py:684
  15.2 2.1 %middle_sweep.1 = (f32[5,32,1024]{2,1,0:T(8,128)}, f32[4,2048]{1,0:T(4,128)S(1)}) custom-call(f32[5,32,1024]{2,1,0:T(8,128)S(1)} %get-tuple-element.42.part_ref, f32[5,32,1024]{2,1,0:T(8,128)S(1)} %get-tuple-element.33.rhs_ref, f32[5,32,1024]{2,1,0:T(8,128)S(1)} %get-tuple-element.34.state_ref, bf16[6,32,1024]{2,1,0:T(8,128)(2,1)S(1)} %get-tuple-element.35.face_ref, ...), custom_call_target="tpu_custom_call" | custom-call | flops 12000000 | bytes 3000000 | tf_op jit(solution)/shard_map/middle_sweep/pallas_call | solution.py:739
  17.3 0.0 collective-permute-done.2.sa_ref
  17.3 0.4 %collective-permute-done.3.sb_ref = f32[4,32,128]{2,1,0:T(8,128)S(1)} collective-permute-done((f32[4,32,128]{2,1,0:T(8,128)S(1)}, f32[4,32,128]{2,1,0:T(8,128)S(1)}, u32[]{:S(2)}, u32[]{:S(2)}) %collective-permute-start.3) | collective-permute-done | bytes 65568 | tf_op jit(solution)/shard_map/ppermute | solution.py:684
  17.7 1.5 %edge_sweep_and_sums.1 = (f32[2,5,32,128]{3,2,1,0:T(8,128)S(1)}, f32[4,2048]{1,0:T(4,128)S(1)}, f32[4,36,128]{2,1,0:T(8,128)S(1)}) custom-call(f32[5,32,1024]{2,1,0:T(8,128)S(1)} %get-tuple-element.42.part_ref, f32[5,32,1024]{2,1,0:T(8,128)S(1)} %get-tuple-element.33.rhs_ref, f32[5,32,1024]{2,1,0:T(8,128)S(1)} %get-tuple-element.34.state_ref, ...), custom_call_target="tpu_custom_call" | custom-call | flops 12000000 | bytes 3000000 | tf_op jit(solution)/shard_map/edge_sweep_and_sums/pallas_call | solution.py:752
  19.2 0.1 collective-permute-start.4
  19.3 0.4 %kept_sums.1.keep_ref = f32[4,36,128]{2,1,0:T(8,128)S(1)} custom-call(f32[4,2048]{1,0:T(4,128)S(1)} %get-tuple-element.56.value_ref, f32[24,2048]{1,0:T(8,128)S(1)} %get-tuple-element.54.shape_ref, s32[4,2048]{1,0:T(4,128)S(1)} %get-tuple-element.40.vertex_ref, bf16[4,128,2048]{2,1,0:T(8,128)(2,1)S(1)} %get-tuple-element.53.vertex_hot_ref), custom_call_target="tpu_custom_call" | custom-call | flops 3000000 | bytes 750000 | tf_op jit(solution)/shard_map/kept_sums/pallas_call | solution.py:765
  19.7 0.8 %collective-permute-done.4.got_ref = f32[4,36,128]{2,1,0:T(8,128)S(1)} collective-permute-done((f32[4,36,128]{2,1,0:T(8,128)S(1)}, f32[4,36,128]{2,1,0:T(8,128)S(1)}, u32[]{:S(2)}, u32[]{:S(2)}) %collective-permute-start.4) | collective-permute-done | bytes 73760 | tf_op jit(solution)/shard_map/ppermute | solution.py:684
  20.5 0.2 collective-permute-start.5
  20.8 1.5 %collective-permute-start.6 = (f32[36,128]{1,0:T(8,128)S(1)}, f32[36,128]{1,0:T(8,128)S(1)}, u32[]{:S(2)}, u32[]{:S(2)}) collective-permute-start(f32[36,128]{1,0:T(8,128)S(1)} %get-tuple-element.59), channel_id=1, source_target_pairs={{0,3},{1,2},{2,1},{3,0},{4,7},{5,6},{6,5},{7,4},{8,11},{9,10},{10,... | collective-permute-start | bytes 55304 | tf_op jit(solution)/shard_map/ppermute | solution.py:784
  22.3 2.2 %collective-permute-start.7 = (f32[36,128]{1,0:T(8,128)S(1)}, f32[36,128]{1,0:T(8,128)S(1)}, u32[]{:S(2)}, u32[]{:S(2)}) collective-permute-start(f32[36,128]{1,0:T(8,128)S(1)} %get-tuple-element.60), channel_id=1, source_target_pairs={{0,5},{1,4},{2,7},{3,6},{4,1},{5,0},{6,3},{7,2},{8,13},{9,12},{10,... | collective-permute-start | bytes 55304 | tf_op jit(solution)/shard_map/ppermute | solution.py:784
  24.5 0.3 %collective-permute-start.8 = (f32[36,128]{1,0:T(8,128)S(1)}, f32[36,128]{1,0:T(8,128)S(1)}, u32[]{:S(2)}, u32[]{:S(2)}) collective-permute-start(f32[36,128]{1,0:T(8,128)S(1)} %get-tuple-element.61), channel_id=1, source_target_pairs={{0,7},{1,6},{2,5},{3,4},{4,3},{5,2},{6,1},{7,0},{8,15},{9,14},{10,... | collective-permute-start | bytes 55304 | tf_op jit(solution)/shard_map/ppermute | solution.py:784
  24.8 0.7 %store_field.1 = f32[5,32,1024]{2,1,0:T(8,128)} custom-call(f32[5,32,1024]{2,1,0:T(8,128)} %get-tuple-element.49.adjoint_ref, f32[2,5,32,128]{3,2,1,0:T(8,128)S(1)} %get-tuple-element.55.field_ref, f32[36,128]{1,0:T(8,128)S(1)} %get-tuple-element.58.after_ref), custom_call_target="tpu_custom_call", output_to_operand_aliasing={{}: (0, {})} | custom-call | flops 3000000 | bytes 750000 | tf_op jit(solution)/shard_map/store_field/pallas_call | solution.py:780
  25.5 0.0 collective-permute-done.5.refs_0_
  25.5 0.0 collective-permute-done.6.refs_1_
  25.5 1.0 %collective-permute-done.7.refs_2_ = f32[36,128]{1,0:T(8,128)S(1)} collective-permute-done((f32[36,128]{1,0:T(8,128)S(1)}, f32[36,128]{1,0:T(8,128)S(1)}, u32[]{:S(2)}, u32[]{:S(2)}) %collective-permute-start.7) | collective-permute-done | bytes 18464 | tf_op jit(solution)/shard_map/ppermute | solution.py:784
  26.5 3.0 %collective-permute-done.8.refs_3_ = f32[36,128]{1,0:T(8,128)S(1)} collective-permute-done((f32[36,128]{1,0:T(8,128)S(1)}, f32[36,128]{1,0:T(8,128)S(1)}, u32[]{:S(2)}, u32[]{:S(2)}) %collective-permute-start.8) | collective-permute-done | bytes 18464 | tf_op jit(solution)/shard_map/ppermute | solution.py:784
  29.5 0.6 %own_sums.1 = f32[3,1536]{1,0:T(4,128)} custom-call(f32[36,128]{1,0:T(8,128)S(1)} %collective-permute-done.5.refs_0_, f32[36,128]{1,0:T(8,128)S(1)} %collective-permute-done.6.refs_1_, f32[36,128]{1,0:T(8,128)S(1)} %collective-permute-done.7.refs_2_, f32[36,128]{1,0:T(8,128)S(1)} %collective-permute-done.8.refs_3_), custom_call_target="tpu_custom_call" | custom-call | flops 1000 | bytes 250 | tf_op jit(solution)/shard_map/own_sums/pallas_call | solution.py:785
  (1 shorter events, 0.0 us)
Async XLA Ops:
  2.6 5.0 %collective-permute-start = (f32[16,1024]{1,0:T(8,128)S(1)}, f32[16,1024]{1,0:T(8,128)S(1)}, u32[]{:S(2)}, u32[]{:S(2)}) collective-permute-start(f32[16,1024]{1,0:T(8,128)S(1)} %get-tuple-element.43.xa_ref), channel_id=1, source_target_pairs={{0,8},{16,24},{8,0},{24,16},{1,9},{17,25},{9,1},{25,17},{2,10},{18... | collective-permute-start | bytes 196616 | tf_op jit(solution)/shard_map/ppermute | solution.py:684
  3.8 5.9 %collective-permute-start.1 = (f32[16,1024]{1,0:T(8,128)S(1)}, f32[16,1024]{1,0:T(8,128)S(1)}, u32[]{:S(2)}, u32[]{:S(2)}) collective-permute-start(f32[16,1024]{1,0:T(8,128)S(1)} %get-tuple-element.44.xb_ref), channel_id=1, source_target_pairs={{8,16},{16,8},{9,17},{17,9},{10,18},{18,10},{11,19},{19,11},{12,20... | collective-permute-start | bytes 196616 | tf_op jit(solution)/shard_map/ppermute | solution.py:684
  9.9 7.4 %collective-permute-start.2 = (f32[4,32,128]{2,1,0:T(8,128)S(1)}, f32[4,32,128]{2,1,0:T(8,128)S(1)}, u32[]{:S(2)}, u32[]{:S(2)}) collective-permute-start(f32[4,32,128]{2,1,0:T(8,128)S(1)} %get-tuple-element.50.ya_ref), channel_id=1, source_target_pairs={{0,1},{2,3},{4,5},{6,7},{1,0},{3,2},{5,4},{7,6},{8,9},{10,11},{12,... | collective-permute-start | bytes 196616 | tf_op jit(solution)/shard_map/ppermute | solution.py:684
  12.1 5.6 %collective-permute-start.3 = (f32[4,32,128]{2,1,0:T(8,128)S(1)}, f32[4,32,128]{2,1,0:T(8,128)S(1)}, u32[]{:S(2)}, u32[]{:S(2)}) collective-permute-start(f32[4,32,128]{2,1,0:T(8,128)S(1)} %get-tuple-element.51.yb_ref), channel_id=1, source_target_pairs={{1,2},{3,4},{5,6},{2,1},{4,3},{6,5},{9,10},{11,12},{13,14},{10,9},... | collective-permute-start | bytes 196616 | tf_op jit(solution)/shard_map/ppermute | solution.py:684
  19.2 1.3 %collective-permute-start.4 = (f32[4,36,128]{2,1,0:T(8,128)S(1)}, f32[4,36,128]{2,1,0:T(8,128)S(1)}, u32[]{:S(2)}, u32[]{:S(2)}) collective-permute-start(f32[4,36,128]{2,1,0:T(8,128)S(1)} %get-tuple-element.57), channel_id=1, source_target_pairs={{0,1},{2,3},{4,5},{6,7},{1,0},{3,2},{5,4},{7,6},{8,9},{10,11},{12,... | collective-permute-start | bytes 221192 | tf_op jit(solution)/shard_map/ppermute | solution.py:684
  20.5 5.0 %collective-permute-start.5 = (f32[36,128]{1,0:T(8,128)S(1)}, f32[36,128]{1,0:T(8,128)S(1)}, u32[]{:S(2)}, u32[]{:S(2)}) collective-permute-start(f32[36,128]{1,0:T(8,128)S(1)} %get-tuple-element.58.after_ref), channel_id=1, source_target_pairs={{0,1},{1,0},{2,3},{3,2},{4,5},{5,4},{6,7},{7,6},{8,9},{9,8},{10,11... | collective-permute-start | bytes 55304 | tf_op jit(solution)/shard_map/ppermute | solution.py:784
  20.8 4.8 %collective-permute-start.6 = (f32[36,128]{1,0:T(8,128)S(1)}, f32[36,128]{1,0:T(8,128)S(1)}, u32[]{:S(2)}, u32[]{:S(2)}) collective-permute-start(f32[36,128]{1,0:T(8,128)S(1)} %get-tuple-element.59), channel_id=1, source_target_pairs={{0,3},{1,2},{2,1},{3,0},{4,7},{5,6},{6,5},{7,4},{8,11},{9,10},{10,... | collective-permute-start | bytes 55304 | tf_op jit(solution)/shard_map/ppermute | solution.py:784
  22.3 4.2 %collective-permute-start.7 = (f32[36,128]{1,0:T(8,128)S(1)}, f32[36,128]{1,0:T(8,128)S(1)}, u32[]{:S(2)}, u32[]{:S(2)}) collective-permute-start(f32[36,128]{1,0:T(8,128)S(1)} %get-tuple-element.60), channel_id=1, source_target_pairs={{0,5},{1,4},{2,7},{3,6},{4,1},{5,0},{6,3},{7,2},{8,13},{9,12},{10,... | collective-permute-start | bytes 55304 | tf_op jit(solution)/shard_map/ppermute | solution.py:784
  24.5 5.0 %collective-permute-start.8 = (f32[36,128]{1,0:T(8,128)S(1)}, f32[36,128]{1,0:T(8,128)S(1)}, u32[]{:S(2)}, u32[]{:S(2)}) collective-permute-start(f32[36,128]{1,0:T(8,128)S(1)} %get-tuple-element.61), channel_id=1, source_target_pairs={{0,7},{1,6},{2,5},{3,4},{4,3},{5,2},{6,1},{7,0},{8,15},{9,14},{10,... | collective-permute-start | bytes 55304 | tf_op jit(solution)/shard_map/ppermute | solution.py:784
